TPU v7x, 32 devices: a whole 2x2x4 slice. The times are simulated.
32 devices in a mesh: row: 4 (over z), col: 8 (over y, x, core).
Axes of the slice: x: 2, y: 2, z: 4, core: 2. Of those that a mesh axis runs over, the one named last changes fastest.
Arguments:
- tokens: bfloat16 [256, 8192], P('row', 'col'), may hold values from -6 to 6
- weights: bfloat16 [2, 8192, 28672], P(None, 'col', 'row'), may hold values from -2 to 2
- adapter_in: bfloat16 [2, 64, 8192], P(None, None, 'col'), may hold values from -0.75 to 0.75
- adapter_out: bfloat16 [2, 64, 28672], P(None, None, 'row'), may hold values from -0.3 to 0.3
- magnitude: float32 [2, 28672], P(None, 'row'), may hold values from 0.5 to 2
- hidden_cot: bfloat16 [256, 28672], P('col', 'row'), may hold values from -0.29882812 to 0.29882812
Outputs:
- hidden: bfloat16 [256, 28672], P('col', 'row')
- grad_in: float32 [2, 64, 8192], P(None, None, 'col')
- grad_out: float32 [2, 64, 28672], P(None, None, 'row')
- grad_mag: float32 [2, 28672], P(None, 'row')
All inputs are finite; a program needn't handle non-finite values.
Results may differ from a plain program's by a relative error of at most 0.028.
Values may be sent and summed in bfloat16 or wider, within the bound.
No kernel may reach another device: no remote copies, remote signals or barrier semaphores. Data moves between devices by JAX's collectives and lax.ppermute only.
A program may use at most 256 MiB of HBM per device.

v0:
```python
import jax
import jax.numpy as jnp
from jax import lax
from jax.sharding import PartitionSpec as P

EPSILON = 1e-06


def cotangents(gate, up_proj, cot_rows):
    sigmoid_g = jax.nn.sigmoid(gate)
    cot_float = cot_rows.astype(jnp.float32)
    d_gate = (cot_float * up_proj * sigmoid_g * (1.0 + gate * (1.0 - sigmoid_g))).astype(
        jnp.bfloat16
    )
    d_up = (cot_float * gate * sigmoid_g).astype(jnp.bfloat16)
    return (d_gate, d_up)


def on_device(tokens, weights, adapter_in, adapter_out, magnitude, hidden_cot):
    in_float = adapter_in.astype(jnp.float32)
    out_float = adapter_out.astype(jnp.float32)
    low_rank = jnp.einsum(
        "prd,prf->pdf", adapter_in, adapter_out, preferred_element_type=jnp.float32
    )
    direction = weights.astype(jnp.float32) + low_rank
    square_sum = lax.psum(jnp.sum(direction * direction, axis=1), "col")
    column_norm = jnp.sqrt(square_sum + EPSILON)
    merged = (direction * (magnitude / column_norm)[:, None, :]).astype(jnp.bfloat16)
    token_all = lax.all_gather(tokens, "row", axis=0, tiled=True)
    share_rows = token_all.shape[0] // lax.axis_size("col")
    partial_value = jnp.einsum("td,pdf->ptf", token_all, merged, preferred_element_type=jnp.float32)
    summed = lax.psum(partial_value.astype(jnp.bfloat16), "col").astype(jnp.float32)
    gate, up_proj = (summed[0], summed[1])
    hidden_all = (gate * jax.nn.sigmoid(gate) * up_proj).astype(jnp.bfloat16)
    hidden = lax.dynamic_slice_in_dim(hidden_all, lax.axis_index("col") * share_rows, share_rows, 0)
    cot_all = lax.all_gather(hidden_cot, "col", axis=0, tiled=True)
    d_gate, d_up = cotangents(gate, up_proj, cot_all)
    d_stack = jnp.stack((d_gate, d_up), axis=0)
    grad_weight = jnp.einsum("td,ptf->pdf", token_all, d_stack, preferred_element_type=jnp.float32)
    coef_grad = magnitude / column_norm
    statistic = lax.psum(jnp.sum(grad_weight * direction, axis=1), "col")
    coef_dir = magnitude * statistic / column_norm**3
    d_direction = coef_grad[:, None, :] * grad_weight - coef_dir[:, None, :] * direction
    right_part = jnp.einsum("prd,pdf->prf", in_float, d_direction, precision=lax.Precision.HIGHEST)
    grad_out = lax.psum(right_part.astype(jnp.bfloat16), "col").astype(jnp.float32)
    left_part = jnp.einsum("prf,pdf->prd", out_float, d_direction, precision=lax.Precision.HIGHEST)
    grad_in = lax.psum(left_part.astype(jnp.bfloat16), "row").astype(jnp.float32)
    grad_mag = statistic / column_norm
    return (hidden, grad_in, grad_out, grad_mag)


def solution(mesh):
    in_specs = (
        P("row", "col"),
        P(None, "col", "row"),
        P(None, None, "col"),
        P(None, None, "row"),
        P(None, "row"),
        P("col", "row"),
    )
    out_specs = (P("col", "row"), P(None, None, "col"), P(None, None, "row"), P(None, "row"))
    return jax.shard_map(
        on_device, mesh=mesh, in_specs=in_specs, out_specs=out_specs, check_vma=False
    )
```

profile of v0, /device:TPU:0, one launch (start us, length us, event | category | flops | bytes accessed | tf_op | source)
XLA Modules:
  0.0 500.9 jit_solution(8905132916887551212)
XLA Ops:
  7.2 0.0 copy-start
  7.2 0.0 all-reduce.4.cloned.1.call-start
  7.2 17.7 %all_gather.6 = bf16[256,1024]{1,0:T(8,128)(2,1)S(1)} all-gather(bf16[64,1024]{1,0:T(8,128)(2,1)} %param.6), channel_id=1, replica_groups=mesh['row'=4,'col'=8] {'row'}, dimensions={0}, use_global_device_ids=true | all-gather | bytes 655360 | tf_op jit(solution)/shard_map/all_gather | solution.py:29
  24.9 0.0 copy-done
  24.9 29.6 %multiply_reduce_fusion = (f32[2,7168]{1,0:T(2,128)S(1)}, f32[2,1024,7168]{2,1,0:T(8,128)}) fusion(bf16[2,64,1024]{2,1,0:T(8,128)(2,1)} %param.8, bf16[2,64,7168]{2,1,0:T(8,128)(2,1)S(1)} %copy-done, bf16[2,1024,7168]{2,1,0:T(8,128)(2,1)} %param.7), kind=kOutput, calls=%fused_computation.5 | convolution fusion | flops 1937754112 | bytes 90234880 | tf_op jit(solution)/shard_map/prd,prf->pdf/dot_general | solution.py:22
  54.5 23.1 %psum.35 = f32[2,7168]{1,0:T(2,128)S(1)} all-reduce(f32[2,7168]{1,0:T(2,128)S(1)} %get-tuple-element.19), channel_id=1, replica_groups=mesh['row'=4,'col'=8] {'col'}, use_global_device_ids=true, to_apply=%region_1.0 | all-reduce | flops 14336 | bytes 114688 | tf_op jit(solution)/shard_map/psum | solution.py:26
  77.6 0.0 copy-done.3
  77.6 0.1 fusion.38
  77.7 24.0 %fusion.9 = bf16[2,256,7168]{1,2,0:T(8,128)(2,1)} fusion(f32[2,1024,7168]{2,1,0:T(8,128)} %get-tuple-element.20, f32[2,7168]{1,0:T(2,128)S(1)} %fusion.38, bf16[256,1024]{1,0:T(8,128)(2,1)S(1)} %all_gather.6), kind=kOutput, calls=%fused_computation.12 | convolution fusion | flops 7549222912 | bytes 66641920 | tf_op jit(solution)/shard_map/td,pdf->ptf/dot_general | solution.py:31
  101.8 0.0 all-reduce.4.cloned.1.call-update
  101.8 0.0 all-gather.2.cloned.1.call-start
  101.9 0.7 all-gather.2.cloned.1.call-update
  102.6 0.2 all-reduce.6.cloned.1.call-start
  102.8 115.4 %all-reduce.4.cloned.1.call-done = bf16[2,256,7168]{1,2,0:T(8,128)(2,1)} async-done(((bf16[2,256,7168]{1,2,0:T(8,128)(2,1)}), bf16[2,256,7168]{1,2,0:T(8,128)(2,1)}) %all-reduce.4.cloned.1.call-update) | async-done | bytes 7340048 | tf_op jit(solution)/shard_map/psum | solution.py:32
  218.2 9.4 %convert_element_type.51 = f32[2,256,7168]{1,2,0:T(8,128)} convert(bf16[2,256,7168]{1,2,0:T(8,128)(2,1)} %all-reduce.4.cloned.1.call-done) | non-fusion elementwise | flops 3670016 | bytes 22020096 | tf_op jit(solution)/shard_map/convert_element_type | solution.py:32
  227.6 27.3 %all-gather.2.cloned.1.call-done = bf16[256,7168]{1,0:T(8,128)(2,1)} async-done(((bf16[32,7168]{1,0:T(8,128)(2,1)}), bf16[256,7168]{1,0:T(8,128)(2,1)}) %all-gather.2.cloned.1.call-update) | async-done | bytes 3670032 | tf_op jit(solution)/shard_map/all_gather | solution.py:36
  254.9 5.9 %copy.15 = bf16[256,7168]{0,1:T(8,128)(2,1)} copy(bf16[256,7168]{1,0:T(8,128)(2,1)} %all-gather.2.cloned.1.call-done) | data formatting | bytes 7340032 | tf_op jit(solution)/shard_map/all_gather | solution.py:36
  260.8 12.1 %fusion.26 = (bf16[1,256,7168]{1,2,0:T(8,128)(2,1)}, bf16[1,256,7168]{1,2,0:T(8,128)(2,1)}, f32[256,7168]{0,1:T(8,128)}) fusion(bf16[256,7168]{0,1:T(8,128)(2,1)} %copy.15, f32[2,256,7168]{1,2,0:T(8,128)} %convert_element_type.51), kind=kLoop, calls=%fused_computation.30 | loop fusion | flops 25690112 | bytes 33030144 | tf_op jit(solution)/shard_map/stack | solution.py:38
  272.9 45.1 %fusion.1 = (f32[2,7168]{1,0:T(2,128)S(1)}, f32[2,7168,1024]{1,2,0:T(8,128)}) fusion(f32[2,1024,7168]{2,1,0:T(8,128)} %get-tuple-element.20, bf16[256,1024]{1,0:T(8,128)(2,1)S(1)} %all_gather.6, bf16[1,256,7168]{1,2,0:T(8,128)(2,1)} %get-tuple-element.13, bf16[1,256,7168]{1,2,0:T(8,128)(2,1)} %get-tuple-element.12), kind=kOutput, calls=%fused_computation.3 | convolution fusion | flops 7549208576 | bytes 125362176 | tf_op jit(solution)/shard_map/td,ptf->pdf/dot_general | solution.py:39
  318.0 24.0 %psum.37 = f32[2,7168]{1,0:T(2,128)S(1)} all-reduce(f32[2,7168]{1,0:T(2,128)S(1)} %get-tuple-element.21), channel_id=1, replica_groups=mesh['row'=4,'col'=8] {'col'}, use_global_device_ids=true, to_apply=%region_4.0 | all-reduce | flops 14336 | bytes 114688 | tf_op jit(solution)/shard_map/psum | solution.py:41
  342.0 0.7 fusion.37
  342.7 45.2 %fusion.31 = bf16[2,64,1024]{2,1,0:T(8,128)(2,1)} fusion(bf16[2,64,7168]{2,1,0:T(8,128)(2,1)S(1)} %copy-done, f32[2,7168,1024]{1,2,0:T(8,128)} %get-tuple-element.22, f32[2,1024,7168]{2,1,0:T(8,128)} %get-tuple-element.20, f32[2,7168]{1,0:T(2,128)S(1)} %get-tuple-element.18, f32[2,7168]{1,0:T(2,128)S(1)} %fusion.38), kind=kOutput, calls=%fused_computation.35 | convolution fusion | flops 11318460416 | bytes 119652352 | tf_op jit(solution)/shard_map/prf,pdf->prd/dot_general | solution.py:46
  387.9 0.0 all-reduce.6.cloned.1.call-update
  387.9 0.3 all-reduce.8.cloned.1.call-start
  388.2 42.2 %fusion.13 = bf16[2,64,7168]{2,1,0:T(8,128)(2,1)} fusion(bf16[2,64,1024]{2,1,0:T(8,128)(2,1)S(1)} %copy-done.2, f32[2,7168,1024]{1,2,0:T(8,128)} %get-tuple-element.22, f32[2,1024,7168]{2,1,0:T(8,128)} %get-tuple-element.20, f32[2,7168]{1,0:T(2,128)S(1)} %get-tuple-element.18, f32[2,7168]{1,0:T(2,128)S(1)} %fusion.38), kind=kOutput, calls=%fused_computation.16 | convolution fusion | flops 11319246848 | bytes 119652352 | tf_op jit(solution)/shard_map/prd,pdf->prf/dot_general | solution.py:44
  430.4 0.0 all-reduce.8.cloned.1.call-update
  430.4 11.4 %slice_bitcast_fusion.1 = (f32[256,7168]{0,1:T(8,128)}, f32[256,7168]{0,1:T(8,128)}) fusion(f32[2,256,7168]{1,2,0:T(8,128)} %convert_element_type.51), kind=kLoop, calls=%fused_computation.23 | loop fusion | bytes 29360128 | tf_op jit(solution)/shard_map/squeeze | solution.py:33
  441.9 8.6 %fusion.27 = bf16[32,7168]{0,1:T(8,128)(2,1)} fusion(f32[256,7168]{0,1:T(8,128)} %get-tuple-element.16, s32[]{:T(128)S(6)} %select_n.3, f32[256,7168]{0,1:T(8,128)} %get-tuple-element.14, f32[256,7168]{0,1:T(8,128)} %get-tuple-element.15), kind=kLoop, calls=%fused_computation.32 | loop fusion | flops 688128 | bytes 3211268 | tf_op jit(solution)/shard_map/convert_element_type | solution.py:34
  450.4 2.4 copy.17
  452.9 1.8 convert_element_type.58
  454.7 36.0 %all-reduce.8.cloned.1.call-done = bf16[2,64,7168]{2,1,0:T(8,128)(2,1)} async-done(((bf16[2,64,7168]{2,1,0:T(8,128)(2,1)}), bf16[2,64,7168]{2,1,0:T(8,128)(2,1)}) %all-reduce.8.cloned.1.call-update) | async-done | bytes 1835024 | tf_op jit(solution)/shard_map/psum | solution.py:45
  490.7 3.7 convert_element_type.61
  (6 shorter events, 0.0 us)
Async XLA Ops:
  7.2 17.8 %copy-start = (bf16[2,64,7168]{2,1,0:T(8,128)(2,1)S(1)}, bf16[2,64,7168]{2,1,0:T(8,128)(2,1)}, u32[]{:S(2)}) copy-start(bf16[2,64,7168]{2,1,0:T(8,128)(2,1)} %param.9) | copy-start | bytes 5505028
  7.2 211.0 %all-reduce.4.cloned.1.call-start = ((), (), s32[]{:S(2)}) async-start(), calls=%async_computation | async-start | bytes 14680064 | tf_op jit(solution)/shard_map/psum | solution.py:32
  24.9 52.7 %copy-start.3 = (f32[2,7168]{1,0:T(2,128)S(1)}, f32[2,7168]{1,0:T(2,128)}, u32[]{:S(2)}) copy-start(f32[2,7168]{1,0:T(2,128)} %param.10) | copy-start | bytes 172036
  101.8 153.1 %all-gather.2.cloned.1.call-start = ((), (), s32[]{:S(2)}) async-start(), calls=%async_computation.1 | async-start | bytes 4128768 | tf_op jit(solution)/shard_map/all_gather | solution.py:36
  102.6 350.3 %all-reduce.6.cloned.1.call-start = ((), (), s32[]{:S(2)}) async-start(), calls=%async_computation.2 | async-start | bytes 524288 | tf_op jit(solution)/shard_map/psum | solution.py:47
  342.7 45.5 %copy-start.2 = (bf16[2,64,1024]{2,1,0:T(8,128)(2,1)S(1)}, bf16[2,64,1024]{2,1,0:T(8,128)(2,1)}, u32[]{:S(2)}) copy-start(bf16[2,64,1024]{2,1,0:T(8,128)(2,1)} %param.8) | copy-start | bytes 786436
  387.9 102.8 %all-reduce.8.cloned.1.call-start = ((), (), s32[]{:S(2)}) async-start(), calls=%async_computation.3 | async-start | bytes 3670016 | tf_op jit(solution)/shard_map/psum | solution.py:45
  441.9 52.5 %copy-start.1 = (bf16[2,64,7168]{2,1,0:T(8,128)(2,1)S(1)}, bf16[2,64,7168]{2,1,0:T(8,128)(2,1)}, u32[]{:S(2)}) copy-start(bf16[2,64,7168]{2,1,0:T(8,128)(2,1)} %param.9) | copy-start | bytes 5505028
Sparse Core Ops, SparseCore 0:
  101.9 116.1 all-reduce.3
  220.2 34.6 all-gather.1
  388.0 35.2 all-reduce.5
  430.5 60.1 all-reduce.7
where the time goes:
time: 502 us; the launch traced here: 501 us
  matrix products  186 us (37%)
  waiting for transfers between devices  179 us (36%)
  blocking collectives  64.8 us (13%)
  other arithmetic  36.5 us (7%)
  local copies, waits for them, and re-layouts  19.8 us (4%)
  between operations  13.8 us (3%)
    psum x1, waiting for transfers between devices, on_device(): lax.psum(partial_value.astype(jnp.bfloat16), 'col').astype(jnp.float32)  115 us
    dot_general x1, matrix products, on_device(): jnp.einsum('prf,pdf->prd', out_float, d_direction, precision=lax.Precisio...  45.2 us
    dot_general x1, matrix products, on_device(): jnp.einsum('td,ptf->pdf', token_all, d_stack, preferred_element_type=jnp....  45.1 us
    dot_general x1, matrix products, on_device(): jnp.einsum('prd,pdf->prf', in_float, d_direction, precision=lax.Precision...  42.2 us
    psum x1, waiting for transfers between devices, on_device(): lax.psum(right_part.astype(jnp.bfloat16), 'col').astype(jnp.float32)  36 us
    dot_general x1, matrix products, on_device(): jnp.einsum('prd,prf->pdf', adapter_in, adapter_out, preferred_element_typ...  29.6 us
    all_gather x1, waiting for transfers between devices, on_device(): cot_all = lax.all_gather(hidden_cot, 'col', axis=0, tiled=True)  27.3 us
    dot_general x1, matrix products, on_device(): jnp.einsum('td,pdf->ptf', token_all, merged, preferred_element_type=jnp.f...  24 us
  transfers between devices with their start and end apart: 4, of which 3 were waited for; matrix products, arithmetic and copies ran while one was open for 15% of the time, Pallas kernels for 0%

commit v1 on v0

v1 whole, which is shorter than its diff:
```python
import functools

import jax
import jax.numpy as jnp
from jax import lax
from jax.experimental import pallas as pl
from jax.experimental.pallas import tpu as pltpu
from jax.sharding import PartitionSpec as P

EPSILON = 1e-06
CHUNKS = 2
VMEM_LIMIT = 48 * 1024 * 1024
BF = jnp.bfloat16
F32 = jnp.float32


def tile_of(width, largest):
    for tile in (1024, 512, 256, 128):
        if tile <= largest and width % tile == 0:
            return tile
    return width


def bit_orders(n):
    bits = [1 << i for i in range(n.bit_length() - 1)]
    return (bits, bits[:1] + bits[1:][::-1])


def block_at(n, order):
    steps = len(order)
    return [sum(order[i] for i in range(steps) if pos >> (steps - 1 - i) & 1) for pos in range(n)]


def swap(x, axis, bit):
    n = lax.axis_size(axis)
    return lax.ppermute(x, axis, [(i, i ^ bit) for i in range(n)])


def dot(a, b, dims=((1,), (0,))):
    return lax.dot_general(a, b, (dims, ((), ())), preferred_element_type=F32)


def split3(x):
    hi = x.astype(BF)
    rest = x - hi.astype(F32)
    mid = rest.astype(BF)
    return hi, mid, (rest - mid.astype(F32)).astype(BF)


def params(**kw):
    return pltpu.CompilerParams(vmem_limit_bytes=VMEM_LIMIT, **kw)


def row_choice(n_blocks, rows, me, order, transpose=False):
    size = n_blocks * rows
    dst = lax.broadcasted_iota(jnp.int32, (size, size), 1 if transpose else 0)
    src = lax.broadcasted_iota(jnp.int32, (size, size), 0 if transpose else 1)
    pos = dst // rows
    block = jnp.zeros_like(pos)
    steps = len(order)
    for i in range(steps):
        block = block + ((pos >> (steps - 1 - i)) & 1) * order[i]
    wanted = (block ^ me) * rows + dst % rows
    return (wanted == src).astype(F32).astype(BF)


def adapter_kernel(n, orders, me_ref, a_ref, w_ref, b_ref, keep_ref, send_ref, sq_ref, aperm, gram):
    rank = a_ref.shape[1]
    half = rank // 2

    @pl.when(pl.program_id(1) == 0)
    def _():
        me = me_ref[0]
        for p in range(2):

            @pl.when(pl.program_id(0) == p)
            def _(p=p):
                choice = row_choice(n, rank // n, me, orders[p])
                aperm[...] = dot(choice, a_ref[0]).astype(BF)

        for i, part in enumerate(split3(dot(aperm[...], a_ref[0], ((1,), (1,))))):
            gram[i] = part

    b = b_ref[0]
    aw = dot(aperm[...], w_ref[0])
    gb = dot(gram[0], b) + dot(gram[1], b) + dot(gram[2], b)
    ad = aw + gb
    keep_ref[0] = ad[:half].astype(BF)
    send_ref[0] = ad[half:].astype(BF)
    both = aw + ad
    squares = jnp.zeros((8, w_ref.shape[2]), F32)
    step = 128
    for i in range(w_ref.shape[1] // step):
        w = w_ref[0, i * step : (i + 1) * step, :].astype(F32)
        squares = squares + jnp.sum((w * w).reshape(step // 8, 8, w.shape[1]), axis=0)
    for p in range(2):

        @pl.when(pl.program_id(0) == p)
        def _(p=p):
            choice = row_choice(n, rank // n, me_ref[0], orders[p])
            cross = both * dot(choice, b)
            sq_ref[0] = jnp.sum(squares, axis=0, keepdims=True) + jnp.sum(cross, axis=0, keepdims=True)


def adapter_call(n, orders, me, a, w, b):
    _, depth, width = w.shape
    rank = a.shape[1]
    tile = tile_of(width, 1024)
    half = jax.ShapeDtypeStruct((2, rank // 2, width), BF)
    return pl.pallas_call(
        functools.partial(adapter_kernel, n, orders),
        grid=(2, width // tile),
        in_specs=[
            pl.BlockSpec(memory_space=pltpu.SMEM),
            pl.BlockSpec((1, rank, depth), lambda p, f: (p, 0, 0)),
            pl.BlockSpec((1, depth, tile), lambda p, f: (p, 0, f)),
            pl.BlockSpec((1, rank, tile), lambda p, f: (p, 0, f)),
        ],
        out_specs=[
            pl.BlockSpec((1, rank // 2, tile), lambda p, f: (p, 0, f)),
            pl.BlockSpec((1, rank // 2, tile), lambda p, f: (p, 0, f)),
            pl.BlockSpec((1, 1, tile), lambda p, f: (p, 0, f)),
        ],
        out_shape=[half, half, jax.ShapeDtypeStruct((2, 1, width), F32)],
        scratch_shapes=[pltpu.VMEM((rank, depth), BF), pltpu.VMEM((3, rank, rank), BF)],
        compiler_params=params(),
        cost_estimate=pl.CostEstimate(
            flops=2 * 4 * rank * depth * width, bytes_accessed=w.size * 2, transcendentals=0
        ),
        name="adapter_pass",
    )(me, a, w, b)


def place_tokens(order, share, me, row, x_refs, x_all):
    steps = len(order)
    per = x_refs[0].shape[0] // share
    for k, x_ref in enumerate(x_refs):
        for h in range(per):
            block = ((row ^ k) * per + h) ^ me
            pos = jnp.int32(0)
            for i in range(steps):
                bit = order[i].bit_length() - 1
                pos = pos + (((block >> bit) & 1) << (steps - 1 - i))
            start = pl.multiple_of(pos * share, share)
            x_all[pl.ds(start, share), :] = x_ref[h * share : (h + 1) * share, :]


def token_kernel(n, share, orders, nx, emit_xa, me_ref, *refs):
    x_refs, (a_ref, w_ref, b_ref) = refs[:nx], refs[nx : nx + 3]
    outs = refs[nx + 3 :]
    keep_ref, send_ref = outs[:2]
    x_all, xa = outs[-2:]
    rank = a_ref.shape[1]
    rows = x_all.shape[0]

    @pl.when(pl.program_id(1) == 0)
    def _():
        me, row = me_ref[0], me_ref[1]
        for p in range(2):

            @pl.when(pl.program_id(0) == p)
            def _(p=p):
                place_tokens(orders[p], share, me, row, x_refs, x_all)

        product = dot(x_all[...], a_ref[0], ((1,), (1,)))
        hi = product.astype(BF)
        xa[0] = hi
        xa[1] = (product - hi.astype(F32)).astype(BF)
        if emit_xa:
            outs[2][0] = product[: rows // 2]
            outs[3][0] = product[rows // 2 :]

    b = b_ref[0]
    y = dot(x_all[...], w_ref[0]) + dot(xa[0], b) + dot(xa[1], b)
    keep_ref[0] = y[: rows // 2].astype(BF)
    send_ref[0] = y[rows // 2 :].astype(BF)


def token_call(n, share, orders, me, xs, a, w, b, first, size, emit_xa):
    _, depth, width = w.shape
    rank = a.shape[1]
    tile = tile_of(size, 512)
    start = first // tile
    rows = n * share
    half = jax.ShapeDtypeStruct((2, rows // 2, size), BF)
    half_spec = pl.BlockSpec((1, rows // 2, tile), lambda p, f: (p, 0, f))
    out_shape, out_specs = [half, half], [half_spec, half_spec]
    if emit_xa:
        out_shape += [jax.ShapeDtypeStruct((2, rows // 2, rank), F32)] * 2
        out_specs += [pl.BlockSpec((1, rows // 2, rank), lambda p, f: (p, 0, 0))] * 2
    return pl.pallas_call(
        functools.partial(token_kernel, n, share, orders, len(xs), emit_xa),
        grid=(2, size // tile),
        in_specs=[pl.BlockSpec(memory_space=pltpu.SMEM)]
        + [pl.BlockSpec(x.shape, lambda p, f: (0, 0)) for x in xs]
        + [
            pl.BlockSpec((1, rank, depth), lambda p, f: (p, 0, 0)),
            pl.BlockSpec((1, depth, tile), lambda p, f: (p, 0, f + start)),
            pl.BlockSpec((1, rank, tile), lambda p, f: (p, 0, f + start)),
        ],
        out_specs=out_specs,
        out_shape=out_shape,
        scratch_shapes=[pltpu.VMEM((rows, depth), BF), pltpu.VMEM((2, rows, rank), BF)],
        compiler_params=params(),
        cost_estimate=pl.CostEstimate(
            flops=4 * rows * depth * size, bytes_accessed=4 * depth * size, transcendentals=0
        ),
        name="token_pass",
    )(me, *xs, a, w, b)


def own_kernel(n, orders, n_parts, has_prior, me_ref, *refs):
    y_refs = refs[: 2 * n_parts]
    xa_ref, sq_ref, mag_ref, b_ref, cot_ref = refs[2 * n_parts : 2 * n_parts + 5]
    outs = refs[2 * n_parts + 5 + has_prior :]
    hid_ref, keep_ref, send_ref, stat_ref, ut_ref, xa = outs
    half = keep_ref.shape[1]
    ys, coefs = [], []
    for p in range(2):
        y = y_refs[p][0].astype(F32)
        for i in range(1, n_parts):
            part = y_refs[2 * i + p]
            y = y + (part[0] if len(part.shape) == 3 else part[...]).astype(F32)
        ys.append(y)
        coefs.append(mag_ref[p] * lax.rsqrt(sq_ref[p] + EPSILON))
    gate, up = ys[0] * coefs[0], ys[1] * coefs[1]
    sig = jax.nn.sigmoid(gate)
    cot = cot_ref[...].astype(F32)
    hid_ref[...] = (gate * sig * up).astype(BF)
    d_pre = (
        (cot * up * sig * (1.0 + gate * (1.0 - sig))).astype(BF),
        (cot * gate * sig).astype(BF),
    )

    @pl.when(pl.program_id(0) == 0)
    def _():
        ut_ref[...] = jnp.zeros_like(ut_ref)
        for p in range(2):
            choice = row_choice(n, xa.shape[2] // n, me_ref[0], orders[p])
            xa[p] = dot(xa_ref[p].astype(BF), choice, ((1,), (1,))).astype(BF)

    for p in range(2):
        d = d_pre[p]
        stat_ref[p] = jnp.sum(d.astype(F32) * ys[p], axis=0, keepdims=True)
        ag = dot(xa[p], d, ((0,), (0,)))
        keep_ref[p] = ag[:half].astype(BF)
        send_ref[p] = ag[half:].astype(BF)
        scaled = (b_ref[p].astype(F32) * coefs[p]).astype(BF)
        ut_ref[p] += dot(d, scaled, ((1,), (1,)))


def own_call(n, orders, me, share, parts, xa, sq, mag, b, cot, prior, first, size):
    width = b.shape[2]
    rank = b.shape[1]
    tile = tile_of(size, 512)
    start = first // tile
    y_args, y_specs = [], []
    for pair in parts:
        for p in range(2):
            part = pair[p]
            y_args.append(part)
            if part.ndim == 3:
                y_specs.append(pl.BlockSpec((1, share, tile), functools.partial(lambda p, f: (p, 0, f), p)))
            else:
                y_specs.append(pl.BlockSpec((share, tile), lambda f: (0, f)))
    half = jax.ShapeDtypeStruct((2, rank // 2, size), BF)
    half_spec = pl.BlockSpec((2, rank // 2, tile), lambda f: (0, 0, f))
    args = [me, *y_args, xa, sq, mag, b, cot]
    specs = [pl.BlockSpec(memory_space=pltpu.SMEM)] + y_specs + [
        pl.BlockSpec(xa.shape, lambda f: (0, 0, 0)),
        pl.BlockSpec((2, 1, tile), lambda f: (0, 0, f + start)),
        pl.BlockSpec((2, 1, tile), lambda f: (0, 0, f + start)),
        pl.BlockSpec((2, rank, tile), lambda f: (0, 0, f + start)),
        pl.BlockSpec((share, tile), lambda f: (0, f + start)),
    ]
    aliases = {}
    if prior is not None:
        aliases = {len(args): 0}
        args.append(prior)
        specs.append(pl.BlockSpec(memory_space=pl.ANY))
    return pl.pallas_call(
        functools.partial(own_kernel, n, orders, len(parts), prior is not None),
        grid=(size // tile,),
        in_specs=specs,
        out_specs=[
            pl.BlockSpec((share, tile), lambda f: (0, f + start)),
            half_spec,
            half_spec,
            pl.BlockSpec((2, 1, tile), lambda f: (0, 0, f)),
            pl.BlockSpec((2, share, rank), lambda f: (0, 0, 0)),
        ],
        out_shape=[
            jax.ShapeDtypeStruct((share, width), BF),
            half,
            half,
            jax.ShapeDtypeStruct((2, 1, size), F32),
            jax.ShapeDtypeStruct((2, share, rank), F32),
        ],
        input_output_aliases=aliases,
        scratch_shapes=[pltpu.VMEM((2, share, rank), BF)],
        compiler_params=params(),
        cost_estimate=pl.CostEstimate(
            flops=4 * rank * share * size * 2, bytes_accessed=share * size * 20, transcendentals=share * size
        ),
        name="own_tokens",
    )(*args)


def second_kernel(w_ref, b_ref, a_ref, cd_ref, out_ref, acc, small):
    last = pl.num_programs(1) - 1

    @pl.when(pl.program_id(1) == 0)
    def _():
        acc[...] = jnp.zeros_like(acc)
        small[...] = jnp.zeros_like(small)

    b = b_ref[0]
    scaled = (b.astype(F32) * cd_ref[0]).astype(BF)
    acc[...] += dot(w_ref[0], scaled, ((1,), (1,)))
    small[...] += dot(b, scaled, ((1,), (1,)))

    @pl.when(pl.program_id(1) == last)
    def _():
        total = acc[...]
        for part in split3(small[...]):
            total = total + dot(a_ref[0], part, ((0,), (0,)))
        out_ref[0] = total


def second_call(w, b, a, cd, first, size):
    _, depth, width = w.shape
    rank = b.shape[1]
    tile = tile_of(size, 512)
    start = first // tile
    return pl.pallas_call(
        second_kernel,
        grid=(2, size // tile),
        in_specs=[
            pl.BlockSpec((1, depth, tile), lambda p, f: (p, 0, f + start)),
            pl.BlockSpec((1, rank, tile), lambda p, f: (p, 0, f + start)),
            pl.BlockSpec((1, rank, depth), lambda p, f: (p, 0, 0)),
            pl.BlockSpec((1, 1, tile), lambda p, f: (p, 0, f)),
        ],
        out_specs=pl.BlockSpec((1, depth, rank), lambda p, f: (p, 0, 0)),
        out_shape=jax.ShapeDtypeStruct((2, depth, rank), F32),
        scratch_shapes=[pltpu.VMEM((depth, rank), F32), pltpu.VMEM((rank, rank), F32)],
        compiler_params=params(),
        cost_estimate=pl.CostEstimate(
            flops=4 * rank * depth * size, bytes_accessed=4 * depth * size, transcendentals=0
        ),
        name="second_pass",
    )(w, b, a, cd)


def join_kernel(share, order, nx, nc, me_ref, *refs):
    x_refs, seconds, ut_refs = refs[:nx], refs[nx : nx + nc], refs[nx + nc : -(nx + 2)]
    outs, (x_all, total) = refs[-(nx + 2) : -2], refs[-2:]
    me, row = me_ref[0], me_ref[1]
    place_tokens(order, share, me, row, x_refs, x_all)
    rank = total.shape[0] // 2
    x = x_all[...]
    for p in range(2):
        ut = jnp.concatenate([ref[p] for ref in ut_refs], axis=0).astype(BF)
        away = seconds[0][p]
        for second in seconds[1:]:
            away = away + second[p]
        total[p * rank : (p + 1) * rank, :] = dot(ut, x, ((0,), (0,))) - away.T
    piece = 2 * rank // nx
    for k in range(nx):
        start = pl.multiple_of((row ^ k) * piece, piece)
        outs[k][...] = total[pl.ds(start, piece), :].astype(outs[k].dtype)


def join_call(share, order, me, xs, seconds, uts):
    depth = xs[0].shape[1]
    rank = seconds[0].shape[2]
    nx = len(xs)
    rows = sum(x.shape[0] for x in xs)
    piece = 2 * rank // nx
    vmem = pl.BlockSpec(memory_space=pltpu.VMEM)
    return pl.pallas_call(
        functools.partial(join_kernel, share, order, nx, len(seconds)),
        in_specs=[pl.BlockSpec(memory_space=pltpu.SMEM)] + [vmem] * (nx + len(seconds) + len(uts)),
        out_specs=[vmem] * nx,
        out_shape=[jax.ShapeDtypeStruct((piece, depth), F32 if k == 0 else BF) for k in range(nx)],
        scratch_shapes=[pltpu.VMEM((rows, depth), BF), pltpu.VMEM((2 * rank, depth), F32)],
        compiler_params=params(),
        name="join_grad_in",
    )(me, *xs, *seconds, *uts)


def lay_kernel(me_ref, *refs):
    out_ref = refs[-1]
    row = me_ref[1]
    for k, ref in enumerate(refs[:-1]):
        piece = ref.shape[0]
        start = pl.multiple_of((row ^ k) * piece, piece)
        out_ref[pl.ds(start, piece), :] = ref[...].astype(F32)


def lay_call(me, pieces):
    rows = sum(x.shape[0] for x in pieces)
    vmem = pl.BlockSpec(memory_space=pltpu.VMEM)
    return pl.pallas_call(
        lay_kernel,
        in_specs=[pl.BlockSpec(memory_space=pltpu.SMEM)] + [vmem] * len(pieces),
        out_specs=vmem,
        out_shape=jax.ShapeDtypeStruct((rows, pieces[0].shape[1]), F32),
        compiler_params=params(),
        name="lay_grad_in",
    )(me, *pieces)


def order_kernel(n, orders, has_prior, me_ref, low_ref, high_ref, *refs):
    out_ref = refs[-1]
    rank = out_ref.shape[1]
    for p in range(2):
        choice = row_choice(n, rank // n, me_ref[0], orders[p], transpose=True)
        both = jnp.concatenate([low_ref[p], high_ref[p]], axis=0)
        out_ref[p] = dot(choice, both)


def order_call(n, orders, me, low, high, prior, first, width):
    _, half, size = low.shape
    tile = tile_of(size, 512)
    start = first // tile
    args = [me, low, high]
    specs = [
        pl.BlockSpec(memory_space=pltpu.SMEM),
        pl.BlockSpec((2, half, tile), lambda f: (0, 0, f)),
        pl.BlockSpec((2, half, tile), lambda f: (0, 0, f)),
    ]
    aliases = {}
    if prior is not None:
        aliases = {3: 0}
        args.append(prior)
        specs.append(pl.BlockSpec(memory_space=pl.ANY))
    return pl.pallas_call(
        functools.partial(order_kernel, n, orders, prior is not None),
        grid=(size // tile,),
        in_specs=specs,
        out_specs=pl.BlockSpec((2, 2 * half, tile), lambda f: (0, 0, f + start)),
        out_shape=jax.ShapeDtypeStruct((2, 2 * half, width), F32),
        input_output_aliases=aliases,
        compiler_params=params(),
        name="order_rows",
    )(*args)


def tied(*xs):
    return lax.optimization_barrier(xs)


def halve(n, orders, keep, send, dtype, extra=()):
    first = swap(send, "col", 1)
    rows = keep.shape[1]
    held = [[keep[p], first[p]] for p in range(2)]
    parts = [(keep, keep), (first, first)]
    for step in range(1, len(orders[0])):
        rows //= 2
        sends = []
        for p in range(2):
            total = sum(part[rows : 2 * rows].astype(F32) for part in held[p])
            sends.append(total.astype(dtype))
        sends = tied(*sends)
        got = tied(*[swap(sends[p], "col", orders[p][step]) for p in range(2)])
        for p in range(2):
            held[p].append(got[p])
        parts.append(tuple(got))
    return parts, rows


def own_rows(parts, rows):
    totals = []
    for p in range(2):
        total = 0.0
        for pair in parts:
            part = pair[p][p] if pair[p].ndim == 3 else pair[p]
            total = total + part[:rows].astype(F32)
        totals.append(total)
    return jnp.stack(totals)


def double_sum(x, bits):
    for bit in bits:
        x = x + swap(x, "col", bit)
    return x


def gather_rows(orders, own):
    held = [own[0], own[1]]
    for step in range(len(orders[0]) - 1, 0, -1):
        sends = tied(*held)
        got = tied(*[swap(sends[p], "col", orders[p][step]) for p in range(2)])
        held = [jnp.concatenate([sends[p], got[p]], axis=0) for p in range(2)]
    low = jnp.stack(held)
    return low, swap(low, "col", 1)


def on_device(tokens, weights, adapter_in, adapter_out, magnitude, hidden_cot):
    n, n_row = lax.axis_size("col"), lax.axis_size("row")
    share = hidden_cot.shape[0]
    width = weights.shape[2]
    orders = bit_orders(n)
    bits = orders[0]
    me = jnp.stack([lax.axis_index("col"), lax.axis_index("row")]).astype(jnp.int32)
    xs = [tokens] + [swap(tokens, "row", k) for k in range(1, n_row)]
    a_keep, a_send, sq_part = adapter_call(n, orders, me, adapter_in, weights, adapter_out)
    squares = double_sum(sq_part, bits)
    a_parts, a_rows = halve(n, orders, a_keep, a_send, BF)
    a_dir = own_rows(a_parts, a_rows)
    mag = magnitude[:, None, :]
    norm = jnp.sqrt(squares + EPSILON)
    coef = mag / norm

    size = width // CHUNKS
    firsts = [c * size for c in range(CHUNKS)]
    y_parts = []
    for c, first in enumerate(firsts):
        outs = token_call(
            n, share, orders, me, xs, adapter_in, weights, adapter_out, first, size, c == 0
        )
        if c == 0:
            xa_parts, _ = halve(n, orders, outs[2], outs[3], F32)
            xa = own_rows(xa_parts, share)
        parts, _ = halve(n, orders, outs[0], outs[1], BF)
        y_parts.append(parts)

    hidden, grad_out, uts, stats, seconds = None, None, [], [], []
    for c, first in enumerate(firsts):
        hidden, g_keep, g_send, stat_part, ut = own_call(
            n, orders, me, share, y_parts[c], xa, squares, mag, adapter_out, hidden_cot, hidden, first, size
        )
        uts.append(ut)
        stat = double_sum(stat_part, bits)
        stats.append(stat)
        span = slice(first, first + size)
        cd = coef[:, :, span] * stat / (norm[:, :, span] ** 2)
        g_parts, g_rows = halve(n, orders, g_keep, g_send, BF)
        own = coef[:, :, span] * own_rows(g_parts, g_rows) - cd * a_dir[:, :, span]
        low, high = gather_rows(orders, own.astype(BF))
        grad_out = order_call(n, orders, me, low, high, grad_out, first, width)
        seconds.append(second_call(weights, adapter_out, adapter_in, cd, first, size))
    grad_mag = (jnp.concatenate(stats, axis=2) / norm)[:, 0, :]

    held = [sum(uts)]
    for bit in bits:
        held = held + [swap(u, "col", bit) for u in held]
    plain = bits[::-1]
    pieces = join_call(share, plain, me, xs, seconds, held)
    total = pieces[0] + sum(swap(pieces[k], "row", k).astype(F32) for k in range(1, n_row))
    total = total.astype(BF)
    laid = lay_call(me, [total] + [swap(total, "row", k) for k in range(1, n_row)])
    grad_in = laid.reshape(2, -1, laid.shape[1])
    return (hidden, grad_in, grad_out, grad_mag)


def solution(mesh):
    in_specs = (
        P("row", "col"),
        P(None, "col", "row"),
        P(None, None, "col"),
        P(None, None, "row"),
        P(None, "row"),
        P("col", "row"),
    )
    out_specs = (P("col", "row"), P(None, None, "col"), P(None, None, "row"), P(None, "row"))
    return jax.shard_map(
        on_device, mesh=mesh, in_specs=in_specs, out_specs=out_specs, check_vma=False
    )
```

time: 502 us -> 218 us (0.43)
  matrix products: 186 us -> 0 us
  waiting for transfers between devices: 179 us -> 48.4 us
  Pallas kernels: 0 us -> 97.7 us
  blocking collectives: 64.8 us -> 0 us
  starting transfers between devices: 0.56 us -> 62.9 us
  other arithmetic: 36.5 us -> 2.75 us
  local copies, waits for them, and re-layouts: 19.8 us -> 3.27 us
  between operations: 13.8 us -> 1.17 us
    dot_general x5 -> x0, matrix products: 186 us -> none  [the longest x1 45.2 us: on_device(): jnp.einsum('prf,pdf->prd', out_float, d_direction, precision=lax.Precisio...]
    psum x3 -> x0, waiting for transfers between devices: 151 us -> none  [the longest x1 115 us: on_device(): lax.psum(partial_value.astype(jnp.bfloat16), 'col').astype(jnp.float32)]
    pallas_call x0 -> x11, Pallas kernels: none -> 97.7 us  [the longest x2 29 us: token_call(): pl.pallas_call(functools.partial(token_kernel, n, share, orders, len(xs),...]
    ppermute x0 -> x65, starting transfers between devices: none -> 62.9 us  [swap(): return lax.ppermute(x, axis, [(i, i ^ bit) for i in range(n)])]
    ppermute x0 -> x65, waiting for transfers between devices: none -> 48.4 us  [swap(): return lax.ppermute(x, axis, [(i, i ^ bit) for i in range(n)])]
    psum x2 -> x0, blocking collectives: 47.1 us -> none  [the longest x1 24 us: on_device(): statistic = lax.psum(jnp.sum(grad_weight * direction, axis=1), 'col')]
    all_gather x1 -> x0, waiting for transfers between devices: 27.3 us -> none  [on_device(): cot_all = lax.all_gather(hidden_cot, 'col', axis=0, tiled=True)]
    convert_element_type x4 -> x12, other arithmetic: 23.6 us -> 1.32 us  [the longest x10 1.17 us: halve(): sends.append(total.astype(dtype))]
  transfers between devices with their start and end apart: 4 -> 65, of which waited for: 3 -> 20; matrix products, arithmetic and copies ran while one was open for 15% -> 2% of each run, Pallas kernels for 0% -> 43%
where the time goes in v1:
time: 218 us; the launch traced here: 216 us
  Pallas kernels  97.7 us (45%)
  starting transfers between devices  62.9 us (29%)
  waiting for transfers between devices  48.4 us (22%)
  local copies, waits for them, and re-layouts  3.27 us (2%)
  other arithmetic  2.75 us (1%)
    ppermute x65, starting transfers between devices, swap(): return lax.ppermute(x, axis, [(i, i ^ bit) for i in range(n)])  62.9 us
    ppermute x65, waiting for transfers between devices, swap(): return lax.ppermute(x, axis, [(i, i ^ bit) for i in range(n)])  48.4 us
    pallas_call x2, Pallas kernels, token_call(): pl.pallas_call(functools.partial(token_kernel, n, share, orders, len(xs),...  29 us
    pallas_call x2, Pallas kernels, second_call(): pl.pallas_call(second_kernel, grid=(2, size // tile), in_specs=[pl.BlockS...  27 us
    pallas_call x1, Pallas kernels, adapter_call(): pl.pallas_call(functools.partial(adapter_kernel, n, orders), grid=(2, wid...  19.4 us
    pallas_call x2, Pallas kernels, own_call(): pl.pallas_call(functools.partial(own_kernel, n, orders, len(parts), prior...  11.8 us
    pallas_call x2, Pallas kernels, order_call(): pl.pallas_call(functools.partial(order_kernel, n, orders, prior is not No...  8.18 us
  transfers between devices with their start and end apart: 65, of which 20 were waited for; matrix products, arithmetic and copies ran while one was open for 2% of the time, Pallas kernels for 43%

profile of v1, /device:TPU:0, one launch (start us, length us, event | category | flops | bytes accessed | tf_op | source)
XLA Modules:
  0.0 216.2 jit_solution(6239923698224508511)
XLA Ops:
  0.6 3.1 %collective-permute-start = (bf16[64,1024]{1,0:T(8,128)(2,1)}, bf16[64,1024]{1,0:T(8,128)(2,1)S(1)}, u32[]{:S(2)}, u32[]{:S(2)}) collective-permute-start(bf16[64,1024]{1,0:T(8,128)(2,1)} %refs_0_.5), channel_id=1, source_target_pairs={{0,8},{8,0},{16,24},{24,16},{1,9},{9,1},{17,25},{25,17},{2,10},{10... | collective-permute-start | bytes 393224 | tf_op jit(solution)/shard_map/ppermute | solution.py:36
  3.7 2.6 %collective-permute-start.1 = (bf16[64,1024]{1,0:T(8,128)(2,1)}, bf16[64,1024]{1,0:T(8,128)(2,1)S(1)}, u32[]{:S(2)}, u32[]{:S(2)}) collective-permute-start(bf16[64,1024]{1,0:T(8,128)(2,1)} %refs_0_.5), channel_id=1, source_target_pairs={{0,16},{8,24},{16,0},{24,8},{1,17},{9,25},{17,1},{25,9},{2,18},{10... | collective-permute-start | bytes 393224 | tf_op jit(solution)/shard_map/ppermute | solution.py:36
  8.8 19.4 %adapter_pass.1 = (bf16[2,32,7168]{2,1,0:T(8,128)(2,1)S(1)}, bf16[2,32,7168]{2,1,0:T(8,128)(2,1)S(1)}, f32[2,1,7168]{2,1,0:T(1,128)S(1)}) custom-call(s32[2]{0:T(128)S(1)} %pad_add_fusion.me_ref, bf16[2,64,1024]{2,1,0:T(8,128)(2,1)S(1)} %copy-done.2, bf16[2,1024,7168]{2,1,0:T(8,128)(2,1)} %w_ref.5, bf16[2,64,7168]{2,1,0:T(8,128)(2,1)S(1)} %copy-done), custom_call_target="tpu_custom_call" | custom-call | flops 3758096384 | bytes 29360128 | tf_op jit(solution)/shard_map/adapter_pass/pallas_call | solution.py:110
  28.3 14.5 %token_pass.3 = (bf16[2,128,3584]{2,1,0:T(8,128)(2,1)S(1)}, bf16[2,128,3584]{2,1,0:T(8,128)(2,1)S(1)}, f32[2,128,64]{2,1,0:T(8,128)S(1)}, f32[2,128,64]{2,1,0:T(8,128)S(1)}) custom-call(s32[2]{0:T(128)S(1)} %pad_add_fusion.me_ref, bf16[64,1024]{1,0:T(8,128)(2,1)S(1)} %copy-done.5, bf16[64,1024]{1,0:T(8,128)(2,1)S(1)} %collective-permute-done.refs_1_, ...), custom_call_target="tpu_custom_call" | custom-call | flops 3758096384 | bytes 14680064 | tf_op jit(solution)/shard_map/token_pass/pallas_call | solution.py:191
  43.5 1.8 collective-permute-start.14
  45.3 2.4 %collective-permute-done.14 = f32[2,1,7168]{2,1,0:T(1,128)S(1)} collective-permute-done((f32[2,1,7168]{2,1,0:T(1,128)S(1)}, f32[2,1,7168]{2,1,0:T(1,128)S(1)}, u32[]{:S(2)}, u32[]{:S(2)}) %collective-permute-start.14) | collective-permute-done | bytes 57376 | tf_op jit(solution)/shard_map/ppermute | solution.py:36
  47.8 1.8 collective-permute-start.15
  49.9 1.7 collective-permute-start.9
  51.6 14.5 %token_pass.2 = (bf16[2,128,3584]{2,1,0:T(8,128)(2,1)S(1)}, bf16[2,128,3584]{2,1,0:T(8,128)(2,1)S(1)}) custom-call(s32[2]{0:T(128)S(1)} %pad_add_fusion.me_ref, bf16[64,1024]{1,0:T(8,128)(2,1)S(1)} %copy-done.5, bf16[64,1024]{1,0:T(8,128)(2,1)S(1)} %collective-permute-done.refs_1_, bf16[64,1024]{1,0:T(8,128)(2,1)S(1)} %collective-permute-done.1.refs_2_, ...), custom_call_target="tpu_custom_call" | custom-call | flops 3758096384 | bytes 14680064 | tf_op jit(solution)/shard_map/token_pass/pallas_call | solution.py:191
  66.2 1.6 collective-permute-start.11
  72.8 1.8 collective-permute-start.17
  76.9 13.2 %collective-permute-done.17.refs_4_ = bf16[64,3584]{1,0:T(8,128)(2,1)S(1)} collective-permute-done((bf16[64,3584]{1,0:T(8,128)(2,1)S(1)}, bf16[64,3584]{1,0:T(8,128)(2,1)S(1)}, u32[]{:S(2)}, u32[]{:S(2)}) %collective-permute-start.17) | collective-permute-done | bytes 458784 | tf_op jit(solution)/shard_map/ppermute | solution.py:36
  92.4 5.6 %collective-permute-done.4.refs_4_ = bf16[64,3584]{1,0:T(8,128)(2,1)S(1)} collective-permute-done((bf16[64,3584]{1,0:T(8,128)(2,1)S(1)}, bf16[64,3584]{1,0:T(8,128)(2,1)S(1)}, u32[]{:S(2)}, u32[]{:S(2)}) %collective-permute-start.4) | collective-permute-done | bytes 458784 | tf_op jit(solution)/shard_map/ppermute | solution.py:36
  98.5 4.5 %collective-permute-done.5.refs_5_ = bf16[64,3584]{1,0:T(8,128)(2,1)S(1)} collective-permute-done((bf16[64,3584]{1,0:T(8,128)(2,1)S(1)}, bf16[64,3584]{1,0:T(8,128)(2,1)S(1)}, u32[]{:S(2)}, u32[]{:S(2)}) %collective-permute-start.5) | collective-permute-done | bytes 458784 | tf_op jit(solution)/shard_map/ppermute | solution.py:36
  104.4 1.7 collective-permute-done.19.refs_6_
  106.1 5.8 %own_tokens.2 = (bf16[32,7168]{1,0:T(8,128)(2,1)}, bf16[2,32,3584]{2,1,0:T(8,128)(2,1)S(1)}, bf16[2,32,3584]{2,1,0:T(8,128)(2,1)S(1)}, f32[2,1,3584]{2,1,0:T(1,128)S(1)}, f32[2,32,64]{2,1,0:T(8,128)S(1)}) custom-call(s32[2]{0:T(128)S(1)} %pad_add_fusion.me_ref, bf16[2,128,3584]{2,1,0:T(8,128)(2,1)S(1)} %get-tuple-element.112.refs_0_.refs_1_, ...), custom_call_target="tpu_custom_call" | custom-call | flops 58720256 | bytes 2293760 | tf_op jit(solution)/shard_map/own_tokens/pallas_call | solution.py:281
  111.9 6.0 %own_tokens.3 = (bf16[32,7168]{1,0:T(8,128)(2,1)}, bf16[2,32,3584]{2,1,0:T(8,128)(2,1)S(1)}, bf16[2,32,3584]{2,1,0:T(8,128)(2,1)S(1)}, f32[2,1,3584]{2,1,0:T(1,128)S(1)}, f32[2,32,64]{2,1,0:T(8,128)S(1)}) custom-call(s32[2]{0:T(128)S(1)} %pad_add_fusion.me_ref, ...), custom_call_target="tpu_custom_call", output_to_operand_aliasing={{0}: (14, {})} | custom-call | flops 58720256 | bytes 2293760 | tf_op jit(solution)/shard_map/own_tokens/pallas_call | solution.py:281
  126.2 1.6 collective-permute-start.23
  128.5 1.6 collective-permute-start.30
  132.9 13.4 %second_pass.3.refs_5_ = f32[2,1024,64]{2,1,0:T(8,128)S(1)} custom-call(bf16[2,1024,7168]{2,1,0:T(8,128)(2,1)} %w_ref.5, bf16[2,64,7168]{2,1,0:T(8,128)(2,1)S(1)} %copy-done.1, bf16[2,64,1024]{2,1,0:T(8,128)(2,1)S(1)} %copy-done.3, f32[2,1,3584]{2,1,0:T(1,128)S(1)} %get-tuple-element.178.cd_ref), custom_call_target="tpu_custom_call" | custom-call | flops 939524096 | bytes 14680064 | tf_op jit(solution)/shard_map/second_pass/pallas_call | solution.py:335
  146.3 13.6 %second_pass.2.refs_4_ = f32[2,1024,64]{2,1,0:T(8,128)S(1)} custom-call(bf16[2,1024,7168]{2,1,0:T(8,128)(2,1)} %w_ref.5, bf16[2,64,7168]{2,1,0:T(8,128)(2,1)S(1)} %copy-done.1, bf16[2,64,1024]{2,1,0:T(8,128)(2,1)S(1)} %copy-done.3, f32[2,1,3584]{2,1,0:T(1,128)S(1)} %get-tuple-element.222.cd_ref), custom_call_target="tpu_custom_call" | custom-call | flops 939524096 | bytes 14680064 | tf_op jit(solution)/shard_map/second_pass/pallas_call | solution.py:335
  161.9 3.5 %collective-permute-start.35 = (bf16[32,1024]{1,0:T(8,128)(2,1)S(1)}, bf16[32,1024]{1,0:T(8,128)(2,1)S(1)}, u32[]{:S(2)}, u32[]{:S(2)}) collective-permute-start(bf16[32,1024]{1,0:T(8,128)(2,1)S(1)} %get-tuple-element.130), channel_id=1, source_target_pairs={{0,16},{8,24},{16,0},{24,8},{1,17},{9,25},{17,1},{25,9},{2,18},{10... | collective-permute-start | bytes 196616 | tf_op jit(solution)/shard_map/ppermute | solution.py:36
  168.4 2.1 collective-permute-done.41
  173.2 2.2 collective-permute-done.56
  178.1 1.6 collective-permute-start.58
  181.3 3.7 %collective-permute-start.38 = (bf16[32,1024]{1,0:T(8,128)(2,1)S(1)}, bf16[32,1024]{1,0:T(8,128)(2,1)S(1)}, u32[]{:S(2)}, u32[]{:S(2)}) collective-permute-start(bf16[32,1024]{1,0:T(8,128)(2,1)S(1)} %add_convert_fusion.10.refs_0_), channel_id=1, source_target_pairs={{0,16},{8,24},{16,0},{24,8},{1,17},{9,25},{17,1},{25,9},{2,18},{10... | collective-permute-start | bytes 196616 | tf_op jit(solution)/shard_map/ppermute | solution.py:36
  187.7 2.0 collective-permute-done.60
  197.0 1.7 collective-permute-done.62
  201.9 1.6 collective-permute-done.52
  203.5 2.1 collective-permute-done.53
  208.0 4.1 %order_rows.2.refs_0_ = f32[2,64,7168]{2,1,0:T(8,128)} custom-call(s32[2]{0:T(128)S(1)} %pad_add_fusion.me_ref, bf16[2,32,3584]{2,1,0:T(8,128)(2,1)S(1)} %pad_maximum_fusion.1.low_ref, bf16[2,32,3584]{2,1,0:T(8,128)(2,1)S(1)} %collective-permute-done.64.high_ref), custom_call_target="tpu_custom_call" | custom-call | tf_op jit(solution)/shard_map/order_rows/pallas_call | solution.py:438
  212.1 4.1 %order_rows.3 = f32[2,64,7168]{2,1,0:T(8,128)} custom-call(s32[2]{0:T(128)S(1)} %pad_add_fusion.me_ref, bf16[2,32,3584]{2,1,0:T(8,128)(2,1)S(1)} %pad_maximum_fusion.low_ref, bf16[2,32,3584]{2,1,0:T(8,128)(2,1)S(1)} %collective-permute-done.54.high_ref, f32[2,64,7168]{2,1,0:T(8,128)} %order_rows.2.refs_0_), custom_call_target="tpu_custom_call", output_to_operand_aliasing={{}: (3, {})} | custom-call | tf_op jit(solution)/shard_map/order_rows/pallas_call | solution.py:438
  (178 shorter events, 54.3 us)
Async XLA Ops:
  0.6 27.7 %collective-permute-start = (bf16[64,1024]{1,0:T(8,128)(2,1)}, bf16[64,1024]{1,0:T(8,128)(2,1)S(1)}, u32[]{:S(2)}, u32[]{:S(2)}) collective-permute-start(bf16[64,1024]{1,0:T(8,128)(2,1)} %refs_0_.5), channel_id=1, source_target_pairs={{0,8},{8,0},{16,24},{24,16},{1,9},{9,1},{17,25},{25,17},{2,10},{10... | collective-permute-start | bytes 393224 | tf_op jit(solution)/shard_map/ppermute | solution.py:36
  3.7 24.6 %collective-permute-start.1 = (bf16[64,1024]{1,0:T(8,128)(2,1)}, bf16[64,1024]{1,0:T(8,128)(2,1)S(1)}, u32[]{:S(2)}, u32[]{:S(2)}) collective-permute-start(bf16[64,1024]{1,0:T(8,128)(2,1)} %refs_0_.5), channel_id=1, source_target_pairs={{0,16},{8,24},{16,0},{24,8},{1,17},{9,25},{17,1},{25,9},{2,18},{10... | collective-permute-start | bytes 393224 | tf_op jit(solution)/shard_map/ppermute | solution.py:36
  6.3 22.0 %collective-permute-start.2 = (bf16[64,1024]{1,0:T(8,128)(2,1)}, bf16[64,1024]{1,0:T(8,128)(2,1)S(1)}, u32[]{:S(2)}, u32[]{:S(2)}) collective-permute-start(bf16[64,1024]{1,0:T(8,128)(2,1)} %refs_0_.5), channel_id=1, source_target_pairs={{0,24},{8,16},{16,8},{24,0},{1,25},{9,17},{17,9},{25,1},{2,26},{10... | collective-permute-start | bytes 393224 | tf_op jit(solution)/shard_map/ppermute | solution.py:36
  28.2 15.2 %collective-permute-start.13 = (f32[2,1,7168]{2,1,0:T(1,128)S(1)}, f32[2,1,7168]{2,1,0:T(1,128)S(1)}, u32[]{:S(2)}, u32[]{:S(2)}) collective-permute-start(f32[2,1,7168]{2,1,0:T(1,128)S(1)} %get-tuple-element.111), channel_id=1, source_target_pairs={{0,1},{1,0},{2,3},{3,2},{4,5},{5,4},{6,7},{7,6},{8,9},{9,8},{10,11... | collective-permute-start | bytes 172040 | tf_op jit(solution)/shard_map/ppermute | solution.py:36
  45.2 26.4 %collective-permute-start.45 = (bf16[2,32,7168]{2,1,0:T(8,128)(2,1)S(1)}, bf16[2,32,7168]{2,1,0:T(8,128)(2,1)S(1)}, u32[]{:S(2)}, u32[]{:S(2)}) collective-permute-start(bf16[2,32,7168]{2,1,0:T(8,128)(2,1)S(1)} %get-tuple-element.143), channel_id=1, source_target_pairs={{0,1},{1,0},{2,3},{3,2},{4,5},{5,4},{6,7},{7,6},{8,9},{9,8},{10,11... | collective-permute-start | bytes 2752520 | tf_op jit(solution)/shard_map/ppermute | solution.py:36
  47.8 20.1 %collective-permute-start.15 = (f32[2,1,7168]{2,1,0:T(1,128)S(1)}, f32[2,1,7168]{2,1,0:T(1,128)S(1)}, u32[]{:S(2)}, u32[]{:S(2)}) collective-permute-start(f32[2,1,7168]{2,1,0:T(1,128)S(1)} %add.328), channel_id=1, source_target_pairs={{0,4},{1,5},{2,6},{3,7},{4,0},{5,1},{6,2},{7,3},{8,12},{9,13},{10,... | collective-permute-start | bytes 172040 | tf_op jit(solution)/shard_map/ppermute | solution.py:36
  49.6 23.0 %collective-permute-start.16 = (bf16[2,128,3584]{2,1,0:T(8,128)(2,1)S(1)}, bf16[2,128,3584]{2,1,0:T(8,128)(2,1)S(1)}, u32[]{:S(2)}, u32[]{:S(2)}) collective-permute-start(bf16[2,128,3584]{2,1,0:T(8,128)(2,1)S(1)} %get-tuple-element.113), channel_id=1, source_target_pairs={{0,1},{1,0},{2,3},{3,2},{4,5},{5,4},{6,7},{7,6},{8,9},{9,8},{10,11... | collective-permute-start | bytes 5505032 | tf_op jit(solution)/shard_map/ppermute | solution.py:36
  49.6 16.5 %collective-permute-start.10 = (f32[64,64]{1,0:T(8,128)S(1)}, f32[64,64]{1,0:T(8,128)S(1)}, u32[]{:S(2)}, u32[]{:S(2)}) collective-permute-start(f32[64,64]{1,0:T(8,128)S(1)} %get-tuple-element.104), channel_id=1, source_target_pairs={{0,4},{1,5},{2,6},{3,7},{4,0},{5,1},{6,2},{7,3},{8,12},{9,13},{10,... | collective-permute-start | bytes 49160 | tf_op jit(solution)/shard_map/ppermute | solution.py:36
  49.9 16.3 %collective-permute-start.9 = (f32[64,64]{1,0:T(8,128)S(1)}, f32[64,64]{1,0:T(8,128)S(1)}, u32[]{:S(2)}, u32[]{:S(2)}) collective-permute-start(f32[64,64]{1,0:T(8,128)S(1)} %get-tuple-element.103), channel_id=1, source_target_pairs={{0,2},{1,3},{2,0},{3,1},{4,6},{5,7},{6,4},{7,5},{8,10},{9,11},{10,... | collective-permute-start | bytes 49160 | tf_op jit(solution)/shard_map/ppermute | solution.py:36
  66.1 10.0 %collective-permute-start.3 = (bf16[2,128,3584]{2,1,0:T(8,128)(2,1)S(1)}, bf16[2,128,3584]{2,1,0:T(8,128)(2,1)S(1)}, u32[]{:S(2)}, u32[]{:S(2)}) collective-permute-start(bf16[2,128,3584]{2,1,0:T(8,128)(2,1)S(1)} %get-tuple-element.92), channel_id=1, source_target_pairs={{0,1},{1,0},{2,3},{3,2},{4,5},{5,4},{6,7},{7,6},{8,9},{9,8},{10,11... | collective-permute-start | bytes 5505032 | tf_op jit(solution)/shard_map/ppermute | solution.py:36
  71.7 32.1 %collective-permute-start.46 = (bf16[16,7168]{1,0:T(8,128)(2,1)S(1)}, bf16[16,7168]{1,0:T(8,128)(2,1)S(1)}, u32[]{:S(2)}, u32[]{:S(2)}) collective-permute-start(bf16[16,7168]{1,0:T(8,128)(2,1)S(1)} %get-tuple-element.144), channel_id=1, source_target_pairs={{0,2},{1,3},{2,0},{3,1},{4,6},{5,7},{6,4},{7,5},{8,10},{9,11},{10,... | collective-permute-start | bytes 688136 | tf_op jit(solution)/shard_map/ppermute | solution.py:36
  72.3 32.1 %collective-permute-start.47 = (bf16[16,7168]{1,0:T(8,128)(2,1)S(1)}, bf16[16,7168]{1,0:T(8,128)(2,1)S(1)}, u32[]{:S(2)}, u32[]{:S(2)}) collective-permute-start(bf16[16,7168]{1,0:T(8,128)(2,1)S(1)} %get-tuple-element.145), channel_id=1, source_target_pairs={{0,4},{1,5},{2,6},{3,7},{4,0},{5,1},{6,2},{7,3},{8,12},{9,13},{10,... | collective-permute-start | bytes 688136 | tf_op jit(solution)/shard_map/ppermute | solution.py:36
  72.8 17.3 %collective-permute-start.17 = (bf16[64,3584]{1,0:T(8,128)(2,1)S(1)}, bf16[64,3584]{1,0:T(8,128)(2,1)S(1)}, u32[]{:S(2)}, u32[]{:S(2)}) collective-permute-start(bf16[64,3584]{1,0:T(8,128)(2,1)S(1)} %get-tuple-element.114), channel_id=1, source_target_pairs={{0,2},{1,3},{2,0},{3,1},{4,6},{5,7},{6,4},{7,5},{8,10},{9,11},{10,... | collective-permute-start | bytes 1376264 | tf_op jit(solution)/shard_map/ppermute | solution.py:36
  74.6 16.1 %collective-permute-start.18 = (bf16[64,3584]{1,0:T(8,128)(2,1)S(1)}, bf16[64,3584]{1,0:T(8,128)(2,1)S(1)}, u32[]{:S(2)}, u32[]{:S(2)}) collective-permute-start(bf16[64,3584]{1,0:T(8,128)(2,1)S(1)} %get-tuple-element.115), channel_id=1, source_target_pairs={{0,4},{1,5},{2,6},{3,7},{4,0},{5,1},{6,2},{7,3},{8,12},{9,13},{10,... | collective-permute-start | bytes 1376264 | tf_op jit(solution)/shard_map/ppermute | solution.py:36
  76.3 21.7 %collective-permute-start.4 = (bf16[64,3584]{1,0:T(8,128)(2,1)S(1)}, bf16[64,3584]{1,0:T(8,128)(2,1)S(1)}, u32[]{:S(2)}, u32[]{:S(2)}) collective-permute-start(bf16[64,3584]{1,0:T(8,128)(2,1)S(1)} %get-tuple-element.93), channel_id=1, source_target_pairs={{0,2},{1,3},{2,0},{3,1},{4,6},{5,7},{6,4},{7,5},{8,10},{9,11},{10,... | collective-permute-start | bytes 1376264 | tf_op jit(solution)/shard_map/ppermute | solution.py:36
  90.1 12.9 %collective-permute-start.5 = (bf16[64,3584]{1,0:T(8,128)(2,1)S(1)}, bf16[64,3584]{1,0:T(8,128)(2,1)S(1)}, u32[]{:S(2)}, u32[]{:S(2)}) collective-permute-start(bf16[64,3584]{1,0:T(8,128)(2,1)S(1)} %get-tuple-element.94), channel_id=1, source_target_pairs={{0,4},{1,5},{2,6},{3,7},{4,0},{5,1},{6,2},{7,3},{8,12},{9,13},{10,... | collective-permute-start | bytes 1376264 | tf_op jit(solution)/shard_map/ppermute | solution.py:36
  90.8 15.3 %collective-permute-start.19 = (bf16[32,3584]{1,0:T(8,128)(2,1)S(1)}, bf16[32,3584]{1,0:T(8,128)(2,1)S(1)}, u32[]{:S(2)}, u32[]{:S(2)}) collective-permute-start(bf16[32,3584]{1,0:T(8,128)(2,1)S(1)} %get-tuple-element.118), channel_id=1, source_target_pairs={{0,4},{1,5},{2,6},{3,7},{4,0},{5,1},{6,2},{7,3},{8,12},{9,13},{10,... | collective-permute-start | bytes 688136 | tf_op jit(solution)/shard_map/ppermute | solution.py:36
  98.0 8.1 %collective-permute-start.20 = (bf16[32,3584]{1,0:T(8,128)(2,1)S(1)}, bf16[32,3584]{1,0:T(8,128)(2,1)S(1)}, u32[]{:S(2)}, u32[]{:S(2)}) collective-permute-start(bf16[32,3584]{1,0:T(8,128)(2,1)S(1)} %get-tuple-element.119), channel_id=1, source_target_pairs={{0,2},{1,3},{2,0},{3,1},{4,6},{5,7},{6,4},{7,5},{8,10},{9,11},{10,... | collective-permute-start | bytes 688136 | tf_op jit(solution)/shard_map/ppermute | solution.py:36
  103.2 8.7 %collective-permute-start.6 = (bf16[32,3584]{1,0:T(8,128)(2,1)S(1)}, bf16[32,3584]{1,0:T(8,128)(2,1)S(1)}, u32[]{:S(2)}, u32[]{:S(2)}) collective-permute-start(bf16[32,3584]{1,0:T(8,128)(2,1)S(1)} %get-tuple-element.97), channel_id=1, source_target_pairs={{0,4},{1,5},{2,6},{3,7},{4,0},{5,1},{6,2},{7,3},{8,12},{9,13},{10,... | collective-permute-start | bytes 688136 | tf_op jit(solution)/shard_map/ppermute | solution.py:36
  103.8 8.1 %collective-permute-start.7 = (bf16[32,3584]{1,0:T(8,128)(2,1)S(1)}, bf16[32,3584]{1,0:T(8,128)(2,1)S(1)}, u32[]{:S(2)}, u32[]{:S(2)}) collective-permute-start(bf16[32,3584]{1,0:T(8,128)(2,1)S(1)} %get-tuple-element.98), channel_id=1, source_target_pairs={{0,2},{1,3},{2,0},{3,1},{4,6},{5,7},{6,4},{7,5},{8,10},{9,11},{10,... | collective-permute-start | bytes 688136 | tf_op jit(solution)/shard_map/ppermute | solution.py:36
  111.9 8.2 %collective-permute-start.21 = (f32[2,1,3584]{2,1,0:T(1,128)S(1)}, f32[2,1,3584]{2,1,0:T(1,128)S(1)}, u32[]{:S(2)}, u32[]{:S(2)}) collective-permute-start(f32[2,1,3584]{2,1,0:T(1,128)S(1)} %get-tuple-element.124), channel_id=1, source_target_pairs={{0,1},{1,0},{2,3},{3,2},{4,5},{5,4},{6,7},{7,6},{8,9},{9,8},{10,11... | collective-permute-start | bytes 86024 | tf_op jit(solution)/shard_map/ppermute | solution.py:36
  128.5 31.4 %collective-permute-start.30 = (f32[2,32,64]{2,1,0:T(8,128)S(1)}, f32[2,32,64]{2,1,0:T(8,128)S(1)}, u32[]{:S(2)}, u32[]{:S(2)}) collective-permute-start(f32[2,32,64]{2,1,0:T(8,128)S(1)} %add.346.refs_6_), channel_id=1, source_target_pairs={{0,4},{1,5},{2,6},{3,7},{4,0},{5,1},{6,2},{7,3},{8,12},{9,13},{10,... | collective-permute-start | bytes 49160 | tf_op jit(solution)/shard_map/ppermute | solution.py:36
  130.1 35.5 %collective-permute-start.40 = (bf16[2,32,3584]{2,1,0:T(8,128)(2,1)S(1)}, bf16[2,32,3584]{2,1,0:T(8,128)(2,1)S(1)}, u32[]{:S(2)}, u32[]{:S(2)}) collective-permute-start(bf16[2,32,3584]{2,1,0:T(8,128)(2,1)S(1)} %get-tuple-element.133), channel_id=1, source_target_pairs={{0,1},{1,0},{2,3},{3,2},{4,5},{5,4},{6,7},{7,6},{8,9},{9,8},{10,11... | collective-permute-start | bytes 1376264 | tf_op jit(solution)/shard_map/ppermute | solution.py:36
  130.1 29.9 %collective-permute-start.31 = (f32[2,32,64]{2,1,0:T(8,128)S(1)}, f32[2,32,64]{2,1,0:T(8,128)S(1)}, u32[]{:S(2)}, u32[]{:S(2)}) collective-permute-start(f32[2,32,64]{2,1,0:T(8,128)S(1)} %collective-permute-done.27.refs_7_), channel_id=1, source_target_pairs={{0,4},{1,5},{2,6},{3,7},{4,0},{5,1},{6,2},{7,3},{8,12},{9,13},{10,... | collective-permute-start | bytes 49160 | tf_op jit(solution)/shard_map/ppermute | solution.py:36
  130.7 29.4 %collective-permute-start.32 = (f32[2,32,64]{2,1,0:T(8,128)S(1)}, f32[2,32,64]{2,1,0:T(8,128)S(1)}, u32[]{:S(2)}, u32[]{:S(2)}) collective-permute-start(f32[2,32,64]{2,1,0:T(8,128)S(1)} %collective-permute-done.28.refs_8_), channel_id=1, source_target_pairs={{0,4},{1,5},{2,6},{3,7},{4,0},{5,1},{6,2},{7,3},{8,12},{9,13},{10,... | collective-permute-start | bytes 49160 | tf_op jit(solution)/shard_map/ppermute | solution.py:36
  132.3 27.8 %collective-permute-start.33 = (f32[2,32,64]{2,1,0:T(8,128)S(1)}, f32[2,32,64]{2,1,0:T(8,128)S(1)}, u32[]{:S(2)}, u32[]{:S(2)}) collective-permute-start(f32[2,32,64]{2,1,0:T(8,128)S(1)} %collective-permute-done.29.refs_9_), channel_id=1, source_target_pairs={{0,4},{1,5},{2,6},{3,7},{4,0},{5,1},{6,2},{7,3},{8,12},{9,13},{10,... | collective-permute-start | bytes 49160 | tf_op jit(solution)/shard_map/ppermute | solution.py:36
  161.2 16.9 %collective-permute-start.34 = (bf16[32,1024]{1,0:T(8,128)(2,1)S(1)}, bf16[32,1024]{1,0:T(8,128)(2,1)S(1)}, u32[]{:S(2)}, u32[]{:S(2)}) collective-permute-start(bf16[32,1024]{1,0:T(8,128)(2,1)S(1)} %get-tuple-element.129), channel_id=1, source_target_pairs={{0,8},{8,0},{16,24},{24,16},{1,9},{9,1},{17,25},{25,17},{2,10},{10... | collective-permute-start | bytes 196616 | tf_op jit(solution)/shard_map/ppermute | solution.py:36
  161.9 17.8 %collective-permute-start.35 = (bf16[32,1024]{1,0:T(8,128)(2,1)S(1)}, bf16[32,1024]{1,0:T(8,128)(2,1)S(1)}, u32[]{:S(2)}, u32[]{:S(2)}) collective-permute-start(bf16[32,1024]{1,0:T(8,128)(2,1)S(1)} %get-tuple-element.130), channel_id=1, source_target_pairs={{0,16},{8,24},{16,0},{24,8},{1,17},{9,25},{17,1},{25,9},{2,18},{10... | collective-permute-start | bytes 196616 | tf_op jit(solution)/shard_map/ppermute | solution.py:36
  165.4 15.3 %collective-permute-start.36 = (bf16[32,1024]{1,0:T(8,128)(2,1)S(1)}, bf16[32,1024]{1,0:T(8,128)(2,1)S(1)}, u32[]{:S(2)}, u32[]{:S(2)}) collective-permute-start(bf16[32,1024]{1,0:T(8,128)(2,1)S(1)} %get-tuple-element.131), channel_id=1, source_target_pairs={{0,24},{8,16},{16,8},{24,0},{1,25},{9,17},{17,9},{25,1},{2,26},{10... | collective-permute-start | bytes 196616 | tf_op jit(solution)/shard_map/ppermute | solution.py:36
  180.8 25.9 %collective-permute-start.37 = (bf16[32,1024]{1,0:T(8,128)(2,1)S(1)}, bf16[32,1024]{1,0:T(8,128)(2,1)S(1)}, u32[]{:S(2)}, u32[]{:S(2)}) collective-permute-start(bf16[32,1024]{1,0:T(8,128)(2,1)S(1)} %add_convert_fusion.10.refs_0_), channel_id=1, source_target_pairs={{0,8},{8,0},{16,24},{24,16},{1,9},{9,1},{17,25},{25,17},{2,10},{10... | collective-permute-start | bytes 196616 | tf_op jit(solution)/shard_map/ppermute | solution.py:36
  181.3 25.3 %collective-permute-start.38 = (bf16[32,1024]{1,0:T(8,128)(2,1)S(1)}, bf16[32,1024]{1,0:T(8,128)(2,1)S(1)}, u32[]{:S(2)}, u32[]{:S(2)}) collective-permute-start(bf16[32,1024]{1,0:T(8,128)(2,1)S(1)} %add_convert_fusion.10.refs_0_), channel_id=1, source_target_pairs={{0,16},{8,24},{16,0},{24,8},{1,17},{9,25},{17,1},{25,9},{2,18},{10... | collective-permute-start | bytes 196616 | tf_op jit(solution)/shard_map/ppermute | solution.py:36
  185.0 21.6 %collective-permute-start.39 = (bf16[32,1024]{1,0:T(8,128)(2,1)S(1)}, bf16[32,1024]{1,0:T(8,128)(2,1)S(1)}, u32[]{:S(2)}, u32[]{:S(2)}) collective-permute-start(bf16[32,1024]{1,0:T(8,128)(2,1)S(1)} %add_convert_fusion.10.refs_0_), channel_id=1, source_target_pairs={{0,24},{8,16},{16,8},{24,0},{1,25},{9,17},{17,9},{25,1},{2,26},{10... | collective-permute-start | bytes 196616 | tf_op jit(solution)/shard_map/ppermute | solution.py:36
  (44 other events, 333.0 us)

commit v2 on v1

v2 whole, which is shorter than its diff:
```python
import functools
import math

import jax
import jax.numpy as jnp
from jax import lax
from jax.experimental import pallas as pl
from jax.experimental.pallas import tpu as pltpu
from jax.sharding import PartitionSpec as P

EPSILON = 1e-06
QUARTERS = (2, 2)
SLOTS = 4
STEP = 1792
VMEM_LIMIT = 48 * 1024 * 1024
VMEM_FIRST = 62 * 1024 * 1024
BF = jnp.bfloat16
F32 = jnp.float32


def tile_of(width, largest):
    for tile in (1792, 1024, 896, 512, 256, 128):
        if tile <= largest and width % tile == 0:
            return tile
    return width


def bit_orders(n):
    bits = [1 << i for i in range(n.bit_length() - 1)]
    return (bits, bits[:1] + bits[1:][::-1])


def block_at(n, order):
    steps = len(order)
    return [sum(order[i] for i in range(steps) if pos >> (steps - 1 - i) & 1) for pos in range(n)]


def swap(x, axis, bit):
    n = lax.axis_size(axis)
    return lax.ppermute(x, axis, [(i, i ^ bit) for i in range(n)])


def stream(w_ref, buf, sem, step, per, first):
    slots = buf.shape[0]
    ahead = max(slots - 2, 1)
    total = 2 * per
    at = pl.program_id(0) * per + pl.program_id(1)

    def copy(i):
        start = pl.multiple_of(first + (i % per) * step, step)
        return pltpu.make_async_copy(
            w_ref.at[i // per, :, pl.ds(start, step)], buf.at[i % slots], sem.at[i % slots]
        )

    @pl.when(at == 0)
    def _():
        for i in range(min(ahead, total)):
            copy(jnp.int32(i)).start()

    def wait():
        copy(at).wait()

        @pl.when(at + ahead < total)
        def _():
            copy(at + ahead).start()

    return buf.at[at % slots], wait


def stream_scratch(depth, step, total):
    slots = min(SLOTS, total + 1)
    return [pltpu.VMEM((slots, depth, step), BF), pltpu.SemaphoreType.DMA((slots,))]


def dot(a, b, dims=((1,), (0,))):
    return lax.dot_general(a, b, (dims, ((), ())), preferred_element_type=F32)


def split3(x):
    hi = x.astype(BF)
    rest = x - hi.astype(F32)
    mid = rest.astype(BF)
    return hi, mid, (rest - mid.astype(F32)).astype(BF)


def params(limit=VMEM_LIMIT):
    return pltpu.CompilerParams(vmem_limit_bytes=limit)


def row_choice(n_blocks, rows, me, order, transpose=False):
    size = n_blocks * rows
    dst = lax.broadcasted_iota(jnp.int32, (size, size), 1 if transpose else 0)
    src = lax.broadcasted_iota(jnp.int32, (size, size), 0 if transpose else 1)
    pos = dst // rows
    block = jnp.zeros_like(pos)
    steps = len(order)
    for i in range(steps):
        block = block + ((pos >> (steps - 1 - i)) & 1) * order[i]
    wanted = (block ^ me) * rows + dst % rows
    return (wanted == src).astype(F32).astype(BF)


def adapter_kernel(n, orders, step, per, me_ref, a_ref, w_ref, b_ref, ad_ref, sq_ref, aperm, gram, buf, sem):
    rank = a_ref.shape[1]
    w_tile, wait = stream(w_ref, buf, sem, step, per, 0)

    @pl.when(pl.program_id(1) == 0)
    def _():
        for p in range(2):

            @pl.when(pl.program_id(0) == p)
            def _(p=p):
                choice = row_choice(n, rank // n, me_ref[0], orders[p])
                aperm[...] = dot(choice, a_ref[p]).astype(BF)
                for i, part in enumerate(split3(dot(aperm[...], a_ref[p], ((1,), (1,))))):
                    gram[:rank, i * rank : (i + 1) * rank] = part
                gram[rank:, :rank] = choice

        gram[rank:, rank:] = jnp.zeros((rank, 2 * rank), BF)

    wait()
    b = b_ref[0]
    aw = dot(aperm[...], w_tile[...])
    both = dot(gram[...], jnp.concatenate([b, b, b], axis=0))
    ad = aw + both[:rank]
    ad_ref[0] = ad.astype(BF)
    cross = (aw + ad) * both[rank:]
    squares = jnp.zeros((8, step), F32)
    slab = 64
    for i in range(w_tile.shape[0] // slab):
        w = w_tile[i * slab : (i + 1) * slab, :].astype(F32)
        squares = squares + jnp.sum((w * w).reshape(slab // 8, 8, step), axis=0)
    sq_ref[0] = jnp.sum(squares, axis=0, keepdims=True) + jnp.sum(cross, axis=0, keepdims=True)


def adapter_call(n, orders, me, a, w, b):
    _, depth, width = w.shape
    rank = a.shape[1]
    tile = tile_of(width, STEP)
    return pl.pallas_call(
        functools.partial(adapter_kernel, n, orders, tile, width // tile),
        grid=(2, width // tile),
        in_specs=[
            pl.BlockSpec(memory_space=pltpu.SMEM),
            pl.BlockSpec(a.shape, lambda p, f: (0, 0, 0)),
            pl.BlockSpec(memory_space=pl.ANY),
            pl.BlockSpec((1, rank, tile), lambda p, f: (p, 0, f)),
        ],
        out_specs=[
            pl.BlockSpec((1, rank, tile), lambda p, f: (p, 0, f)),
            pl.BlockSpec((1, 1, tile), lambda p, f: (p, 0, f)),
        ],
        out_shape=[
            jax.ShapeDtypeStruct((2, rank, width), BF),
            jax.ShapeDtypeStruct((2, 1, width), F32),
        ],
        scratch_shapes=[pltpu.VMEM((rank, depth), BF), pltpu.VMEM((2 * rank, 3 * rank), BF)]
        + stream_scratch(depth, tile, 2 * (width // tile)),
        compiler_params=params(VMEM_FIRST),
        cost_estimate=pl.CostEstimate(
            flops=2 * 4 * rank * depth * width, bytes_accessed=w.size * 2, transcendentals=0
        ),
        name="adapter_pass",
    )(me, a, w, b)


def place_tokens(order, share, me, row, x_refs, x_all):
    steps = len(order)
    per = x_refs[0].shape[0] // share
    for k, x_ref in enumerate(x_refs):
        for h in range(per):
            block = ((row ^ k) * per + h) ^ me
            pos = jnp.int32(0)
            for i in range(steps):
                bit = order[i].bit_length() - 1
                pos = pos + (((block >> bit) & 1) << (steps - 1 - i))
            start = pl.multiple_of(pos * share, share)
            x_all[pl.ds(start, share), :] = x_ref[h * share : (h + 1) * share, :]


def token_kernel(n, share, orders, nx, emit_xa, step, per, first, me_ref, *refs):
    x_refs, (a_ref, w_ref, b_ref) = refs[:nx], refs[nx : nx + 3]
    outs = refs[nx + 3 :]
    keep_ref, send_ref = outs[:2]
    left, xa, buf, sem = outs[-4:]
    rank = a_ref.shape[1]
    rows = left.shape[0]
    half = rows // 2
    w_tile, wait = stream(w_ref, buf, sem, step, per, first)

    @pl.when(pl.program_id(1) == 0)
    def _():
        me, row = me_ref[0], me_ref[1]
        for p in range(2):

            @pl.when(pl.program_id(0) == p)
            def _(p=p):
                place_tokens(orders[p], share, me, row, x_refs, left)
                if emit_xa and p == 0:
                    both = dot(left[...], a_ref[...].reshape(2 * rank, -1), ((1,), (1,)))
                    outs[2][...] = both[:half]
                    outs[3][...] = both[half:]
                product = dot(left[...], a_ref[p], ((1,), (1,)))
                hi = product.astype(BF)
                xa[:, :rank] = hi
                xa[:, rank:] = (product - hi.astype(F32)).astype(BF)

    wait()
    b = b_ref[0]
    y = dot(left[...], w_tile[...]) + dot(xa[...], jnp.concatenate([b, b], axis=0))
    keep_ref[0] = y[:half].astype(BF)
    send_ref[0] = y[half:].astype(BF)


def token_call(n, share, orders, me, xs, a, w, b, first, size, emit_xa):
    _, depth, width = w.shape
    rank = a.shape[1]
    tile = tile_of(math.gcd(first, size), STEP)
    start = first // tile
    rows = n * share
    half = jax.ShapeDtypeStruct((2, rows // 2, size), BF)
    half_spec = pl.BlockSpec((1, rows // 2, tile), lambda p, f: (p, 0, f))
    out_shape, out_specs = [half, half], [half_spec, half_spec]
    if emit_xa:
        out_shape += [jax.ShapeDtypeStruct((rows // 2, 2 * rank), F32)] * 2
        out_specs += [pl.BlockSpec((rows // 2, 2 * rank), lambda p, f: (0, 0))] * 2
    return pl.pallas_call(
        functools.partial(token_kernel, n, share, orders, len(xs), emit_xa, tile, size // tile, first),
        grid=(2, size // tile),
        in_specs=[pl.BlockSpec(memory_space=pltpu.SMEM)]
        + [pl.BlockSpec(x.shape, lambda p, f: (0, 0)) for x in xs]
        + [
            pl.BlockSpec(a.shape, lambda p, f: (0, 0, 0)),
            pl.BlockSpec(memory_space=pl.ANY),
            pl.BlockSpec((1, rank, tile), lambda p, f: (p, 0, f + start)),
        ],
        out_specs=out_specs,
        out_shape=out_shape,
        scratch_shapes=[pltpu.VMEM((rows, depth), BF), pltpu.VMEM((rows, 2 * rank), BF)]
        + stream_scratch(depth, tile, 2 * (size // tile)),
        compiler_params=params(),
        cost_estimate=pl.CostEstimate(
            flops=4 * rows * depth * size, bytes_accessed=4 * depth * size, transcendentals=0
        ),
        name="token_pass",
    )(me, *xs, a, w, b)


def own_kernel(n, orders, n_parts, n_xa, has_prior, me_ref, *refs):
    y_refs = refs[: 2 * n_parts]
    xa_refs = refs[2 * n_parts : 2 * n_parts + n_xa]
    refs = refs[2 * n_parts + n_xa :]
    sq_ref, mag_ref, b_ref, cot_ref = refs[:4]
    outs = refs[4 + has_prior :]
    hid_ref, keep_ref, send_ref, stat_ref, ut_ref, xa = outs
    half = keep_ref.shape[1]
    ys, coefs = [], []
    for p in range(2):
        y = y_refs[p][0].astype(F32)
        for i in range(1, n_parts):
            part = y_refs[2 * i + p]
            y = y + (part[0] if len(part.shape) == 3 else part[...]).astype(F32)
        ys.append(y)
        coefs.append(mag_ref[p] * lax.rsqrt(sq_ref[p] + EPSILON))
    gate, up = ys[0] * coefs[0], ys[1] * coefs[1]
    sig = jax.nn.sigmoid(gate)
    cot = cot_ref[...].astype(F32)
    hid_ref[...] = (gate * sig * up).astype(BF)
    d_pre = (
        (cot * up * sig * (1.0 + gate * (1.0 - sig))).astype(BF),
        (cot * gate * sig).astype(BF),
    )

    @pl.when(pl.program_id(0) == 0)
    def _():
        ut_ref[...] = jnp.zeros_like(ut_ref)
        rank = xa.shape[2]
        product = xa_refs[0][...]
        for ref in xa_refs[1:]:
            product = product + ref[...]
        product = product.astype(BF)
        for p in range(2):
            choice = row_choice(n, rank // n, me_ref[0], orders[p])
            xa[p] = dot(product[:, p * rank : (p + 1) * rank], choice, ((1,), (1,))).astype(BF)

    for p in range(2):
        d = d_pre[p]
        stat_ref[p] = jnp.sum(d.astype(F32) * ys[p], axis=0, keepdims=True)
        ag = dot(xa[p], d, ((0,), (0,)))
        keep_ref[p] = ag[:half].astype(BF)
        send_ref[p] = ag[half:].astype(BF)
        scaled = (b_ref[p].astype(F32) * coefs[p]).astype(BF)
        ut_ref[p] += dot(d, scaled, ((1,), (1,)))


def own_call(n, orders, me, share, parts, xas, sq, mag, b, cot, prior, first, size):
    width = b.shape[2]
    rank = b.shape[1]
    tile = tile_of(math.gcd(first, size), 1792)
    start = first // tile
    y_args, y_specs = [], []
    for pair in parts:
        for p in range(2):
            part = pair[p]
            y_args.append(part)
            if part.ndim == 3:
                y_specs.append(pl.BlockSpec((1, share, tile), functools.partial(lambda p, f: (p, 0, f), p)))
            else:
                y_specs.append(pl.BlockSpec((share, tile), lambda f: (0, f)))
    half = jax.ShapeDtypeStruct((2, rank // 2, size), BF)
    half_spec = pl.BlockSpec((2, rank // 2, tile), lambda f: (0, 0, f))
    args = [me, *y_args, *xas, sq, mag, b, cot]
    specs = [pl.BlockSpec(memory_space=pltpu.SMEM)] + y_specs
    specs += [pl.BlockSpec((share, x.shape[1]), lambda f: (0, 0)) for x in xas]
    specs += [
        pl.BlockSpec((2, 1, tile), lambda f: (0, 0, f + start)),
        pl.BlockSpec((2, 1, tile), lambda f: (0, 0, f + start)),
        pl.BlockSpec((2, rank, tile), lambda f: (0, 0, f + start)),
        pl.BlockSpec((share, tile), lambda f: (0, f + start)),
    ]
    aliases = {}
    if prior is not None:
        aliases = {len(args): 0}
        args.append(prior)
        specs.append(pl.BlockSpec(memory_space=pl.ANY))
    return pl.pallas_call(
        functools.partial(own_kernel, n, orders, len(parts), len(xas), prior is not None),
        grid=(size // tile,),
        in_specs=specs,
        out_specs=[
            pl.BlockSpec((share, tile), lambda f: (0, f + start)),
            half_spec,
            half_spec,
            pl.BlockSpec((2, 1, tile), lambda f: (0, 0, f)),
            pl.BlockSpec((2, share, rank), lambda f: (0, 0, 0)),
        ],
        out_shape=[
            jax.ShapeDtypeStruct((share, width), BF),
            half,
            half,
            jax.ShapeDtypeStruct((2, 1, size), F32),
            jax.ShapeDtypeStruct((2, share, rank), F32),
        ],
        input_output_aliases=aliases,
        scratch_shapes=[pltpu.VMEM((2, share, rank), BF)],
        compiler_params=params(),
        cost_estimate=pl.CostEstimate(
            flops=4 * rank * share * size * 2, bytes_accessed=share * size * 20, transcendentals=share * size
        ),
        name="own_tokens",
    )(*args)


def second_kernel(step, per, first, token_ref, w_ref, b_ref, a_ref, cd_ref, out_ref, acc, small, buf, sem):
    w_tile, wait = stream(w_ref, buf, sem, step, per, first)
    last = pl.num_programs(1) - 1

    @pl.when(pl.program_id(1) == 0)
    def _():
        acc[...] = jnp.zeros_like(acc)
        small[...] = jnp.zeros_like(small)

    b = b_ref[0]
    scaled = (b.astype(F32) * cd_ref[0]).astype(BF)
    wait()
    acc[...] += dot(scaled, w_tile[...], ((1,), (1,)))
    small[...] += dot(scaled, b, ((1,), (1,)))

    @pl.when(pl.program_id(1) == last)
    def _():
        total = acc[...]
        for part in split3(small[...]):
            total = total + dot(part, a_ref[0])
        out_ref[0] = total


def second_call(w, b, a, cd, first, size, token):
    _, depth, width = w.shape
    rank = b.shape[1]
    tile = tile_of(math.gcd(first, size), STEP)
    start = first // tile
    return pl.pallas_call(
        functools.partial(second_kernel, tile, size // tile, first),
        grid=(2, size // tile),
        in_specs=[
            pl.BlockSpec(memory_space=pltpu.SMEM),
            pl.BlockSpec(memory_space=pl.ANY),
            pl.BlockSpec((1, rank, tile), lambda p, f: (p, 0, f + start)),
            pl.BlockSpec((1, rank, depth), lambda p, f: (p, 0, 0)),
            pl.BlockSpec((1, 1, tile), lambda p, f: (p, 0, f)),
        ],
        out_specs=pl.BlockSpec((1, rank, depth), lambda p, f: (p, 0, 0)),
        out_shape=jax.ShapeDtypeStruct((2, rank, depth), F32),
        scratch_shapes=[pltpu.VMEM((rank, depth), F32), pltpu.VMEM((rank, rank), F32)]
        + stream_scratch(depth, tile, 2 * (size // tile)),
        compiler_params=params(),
        cost_estimate=pl.CostEstimate(
            flops=4 * rank * depth * size, bytes_accessed=4 * depth * size, transcendentals=0
        ),
        name="second_pass",
    )(token, w, b, a, cd)


def join_kernel(share, order, nx, nc, me_ref, *refs):
    x_refs, seconds, ut_refs = refs[:nx], refs[nx : nx + nc], refs[nx + nc : -(nx + 2)]
    outs, (x_all, total) = refs[-(nx + 2) : -2], refs[-2:]
    me, row = me_ref[0], me_ref[1]
    place_tokens(order, share, me, row, x_refs, x_all)
    rank = total.shape[0] // 2
    x = x_all[...]
    for p in range(2):
        ut = ut_refs[0][p].astype(BF)
        away = seconds[0][p]
        for second in seconds[1:]:
            away = away + second[p]
        total[p * rank : (p + 1) * rank, :] = dot(ut, x, ((0,), (0,))) - away
    piece = 2 * rank // nx
    for k in range(nx):
        start = pl.multiple_of((row ^ k) * piece, piece)
        outs[k][...] = total[pl.ds(start, piece), :].astype(outs[k].dtype)


def join_call(share, order, me, xs, seconds, uts):
    depth = xs[0].shape[1]
    rank = seconds[0].shape[1]
    nx = len(xs)
    rows = sum(x.shape[0] for x in xs)
    piece = 2 * rank // nx
    vmem = pl.BlockSpec(memory_space=pltpu.VMEM)
    return pl.pallas_call(
        functools.partial(join_kernel, share, order, nx, len(seconds)),
        in_specs=[pl.BlockSpec(memory_space=pltpu.SMEM)] + [vmem] * (nx + len(seconds) + len(uts)),
        out_specs=[vmem] * nx,
        out_shape=[jax.ShapeDtypeStruct((piece, depth), F32 if k == 0 else BF) for k in range(nx)],
        scratch_shapes=[pltpu.VMEM((rows, depth), BF), pltpu.VMEM((2 * rank, depth), F32)],
        compiler_params=params(),
        name="join_grad_in",
    )(me, *xs, *seconds, *uts)


def lay_kernel(me_ref, *refs):
    out_ref = refs[-1]
    row = me_ref[1]
    for k, ref in enumerate(refs[:-1]):
        piece = ref.shape[0]
        start = pl.multiple_of((row ^ k) * piece, piece)
        out_ref[pl.ds(start, piece), :] = ref[...].astype(F32)


def lay_call(me, pieces):
    rows = sum(x.shape[0] for x in pieces)
    vmem = pl.BlockSpec(memory_space=pltpu.VMEM)
    return pl.pallas_call(
        lay_kernel,
        in_specs=[pl.BlockSpec(memory_space=pltpu.SMEM)] + [vmem] * len(pieces),
        out_specs=vmem,
        out_shape=jax.ShapeDtypeStruct((rows, pieces[0].shape[1]), F32),
        compiler_params=params(),
        name="lay_grad_in",
    )(me, *pieces)


def order_kernel(n, orders, has_prior, me_ref, low_ref, high_ref, *refs):
    out_ref = refs[-1]
    rank = out_ref.shape[1]
    for p in range(2):
        choice = row_choice(n, rank // n, me_ref[0], orders[p], transpose=True)
        both = jnp.concatenate([low_ref[p], high_ref[p]], axis=0)
        out_ref[p] = dot(choice, both)


def order_call(n, orders, me, low, high, prior, first, width):
    _, half, size = low.shape
    tile = tile_of(math.gcd(first, size), 1792)
    start = first // tile
    args = [me, low, high]
    specs = [
        pl.BlockSpec(memory_space=pltpu.SMEM),
        pl.BlockSpec((2, half, tile), lambda f: (0, 0, f)),
        pl.BlockSpec((2, half, tile), lambda f: (0, 0, f)),
    ]
    aliases = {}
    if prior is not None:
        aliases = {3: 0}
        args.append(prior)
        specs.append(pl.BlockSpec(memory_space=pl.ANY))
    return pl.pallas_call(
        functools.partial(order_kernel, n, orders, prior is not None),
        grid=(size // tile,),
        in_specs=specs,
        out_specs=pl.BlockSpec((2, 2 * half, tile), lambda f: (0, 0, f + start)),
        out_shape=jax.ShapeDtypeStruct((2, 2 * half, width), F32),
        input_output_aliases=aliases,
        compiler_params=params(),
        name="order_rows",
    )(*args)


def tied(*xs):
    return lax.optimization_barrier(xs)


class Turn:
    def __init__(self, token):
        self.token = token

    def pass_on(self, *xs):
        self.token, *xs = tied(self.token, *xs)
        return tuple(xs)


class Halving:
    def __init__(self, orders, keep, send, dtype=BF):
        self.flat = keep.ndim == 2
        self.orders, self.dtype = orders[:1] if self.flat else orders, dtype
        self.parts = [(keep,) if self.flat else (keep[0], keep[1])]
        self.whole = [keep]
        self.send, self.step, self.rows = [send], 0, keep.shape[0 if self.flat else 1]

    def sums(self, low, high):
        return [sum(part[p][low:high].astype(F32) for part in self.parts) for p in range(len(self.orders))]

    def prepare(self):
        if self.step:
            self.rows //= 2
            self.send = [x.astype(self.dtype) for x in self.sums(self.rows, 2 * self.rows)]
        return self.send

    def go(self, send):
        if self.step:
            self.got = [swap(x, "col", order[self.step]) for x, order in zip(send, self.orders)]
        else:
            self.got = [swap(send[0], "col", self.orders[0][0])]
        return self.got

    def arrived(self, got):
        if self.step or self.flat:
            self.parts.append(tuple(got))
            self.whole.append(tuple(got) if len(got) > 1 else got[0])
        else:
            self.parts.append((got[0][0], got[0][1]))
            self.whole.append(got[0])
        self.step += 1

    def done(self):
        return self.step == len(self.orders[0])

    def own(self):
        return self.sums(0, self.rows)

    def pairs(self):
        return [x if isinstance(x, tuple) else (x, x) for x in self.whole]


class Doubling:
    def __init__(self, bits, x, direct=False):
        self.bits, self.x, self.step = [[bit] for bit in bits], x, 0
        if direct:
            self.bits = [bits[:1], list(range(2, 1 << len(bits), 2))]

    def prepare(self):
        return [self.x]

    def go(self, send):
        self.x = send[0]
        return [swap(send[0], "col", bit) for bit in self.bits[self.step]]

    def arrived(self, got):
        self.x = self.x + sum(got)
        self.step += 1

    def done(self):
        return self.step == len(self.bits)


class Scattering:
    def __init__(self, orders, n, keep, send):
        self.orders, self.keep, self.step = orders, keep, 0
        self.send, self.n = send, n

    def prepare(self):
        if self.step == 0:
            return [self.send]
        self.sum = self.keep.astype(F32) + self.first.astype(F32)
        rows = self.sum.shape[1] * 2 // self.n
        out = []
        for j in range(2, self.n, 2):
            at = [block_at(self.n, order).index(j) * rows for order in self.orders]
            both = [self.sum[p, at[p] : at[p] + rows] for p in range(2)]
            out.append(jnp.concatenate(both, axis=0).astype(BF))
        self.rows = rows
        return out

    def go(self, send):
        if self.step == 0:
            return [swap(send[0], "col", 1)]
        return [swap(x, "col", j) for x, j in zip(send, range(2, self.n, 2))]

    def arrived(self, got):
        if self.step == 0:
            self.first = got[0]
        else:
            rows = self.rows
            total = sum(x.astype(F32) for x in got)
            self.own = [(self.sum[p, :rows] + total[p * rows : (p + 1) * rows]).astype(BF) for p in range(2)]
        self.step += 1

    def done(self):
        return self.step == 2


class Collecting:
    def __init__(self, bits, x):
        self.bits, self.x, self.step = bits, x, 0

    def prepare(self):
        return [self.x]

    def go(self, send):
        self.x = send[0]
        return [swap(send[0], "col", self.bits[self.step])]

    def arrived(self, got):
        self.x = jnp.concatenate([self.x, got[0]], axis=1)
        self.step += 1

    def done(self):
        return self.step == len(self.bits)


class Laying:
    def __init__(self, orders, own):
        self.orders, self.held, self.step = orders, own, len(orders[0]) - 1

    def prepare(self):
        return self.held if self.step else [jnp.stack(self.held)]

    def go(self, send):
        self.held = list(send)
        if self.step:
            return [swap(x, "col", order[self.step]) for x, order in zip(send, self.orders)]
        return [swap(send[0], "col", self.orders[0][0])]

    def arrived(self, got):
        if self.step:
            self.held = [jnp.concatenate(pair, axis=0) for pair in zip(self.held, got)]
        else:
            self.held += list(got)
        self.step -= 1

    def done(self):
        return self.step < 0


class Around:
    def __init__(self, n, xs):
        self.n, self.xs, self.got = n, xs, None

    def prepare(self):
        return self.xs

    def go(self, send):
        return [swap(x, "row", k) for k, x in enumerate(send, start=1)]

    def arrived(self, got):
        self.got = list(got)

    def done(self):
        return self.got is not None


def phase(turn, moves, kernel=None):
    moves = [move for move in moves if not move.done()]
    sends = [move.prepare() for move in moves]
    sent = list(turn.pass_on(*[x for send in sends for x in send]))
    got = [move.go([sent.pop(0) for _ in send]) for move, send in zip(moves, sends)]
    outs = kernel(turn.token) if kernel else ()
    flat = list(turn.pass_on(*[x for g in got for x in g], *outs))
    for move, g in zip(moves, got):
        move.arrived([flat.pop(0) for _ in g])
    return flat


def on_device(tokens, weights, adapter_in, adapter_out, magnitude, hidden_cot):
    n, n_row = lax.axis_size("col"), lax.axis_size("row")
    rank = adapter_in.shape[1]
    share = hidden_cot.shape[0]
    width = weights.shape[2]
    orders = bit_orders(n)
    bits = orders[0]
    steps = len(bits)
    me = jnp.stack([lax.axis_index("col"), lax.axis_index("row")]).astype(jnp.int32)
    mag = magnitude[:, None, :]
    sizes = [width * q // sum(QUARTERS) for q in QUARTERS]
    firsts = [sum(sizes[:c]) for c in range(len(sizes))]
    count = len(sizes)

    xs = [tokens] + [swap(tokens, "row", k) for k in range(1, n_row)]
    ad, sq = adapter_call(n, orders, me, adapter_in, weights, adapter_out)
    turn = Turn(me)
    *xs, sq = turn.pass_on(*xs, sq)
    squares = Doubling(bits, sq)

    def project(c):
        return lambda token: token_call(
            n, share, orders, token, xs, adapter_in, weights, adapter_out, firsts[c], sizes[c], c == 0
        )

    def elementwise(c):
        return lambda token: own_call(
            n, orders, token, share, halvings[c].pairs(), [x[0] for x in xa.parts], squares.x, mag, adapter_out,
            hidden_cot, hidden, firsts[c], sizes[c],
        )

    def second(c):
        first, size = firsts[c], sizes[c]
        return lambda token: [
            second_call(weights, adapter_out, adapter_in, cd[:, :, first : first + size], first, size, token)
        ]

    outs = phase(turn, [squares], project(0))
    halvings = [Halving(orders, outs[0], outs[1])]
    xa = Halving(orders, outs[2], outs[3], F32)
    moves = [squares, xa, halvings[0]]
    phase(turn, moves)
    for c in range(1, count):
        outs = phase(turn, moves, project(c))
        halvings.append(Halving(orders, outs[0], outs[1]))
        moves.append(halvings[-1])
        phase(turn, moves)
    hidden, results = None, []
    for c in range(count):
        while not (halvings[c].done() and squares.done() and xa.done()):
            phase(turn, moves)
        hidden, *outs = phase(turn, moves, elementwise(c))
        results.append(outs)
    stats = Doubling(bits, jnp.concatenate([r[2] for r in results], axis=2), direct=True)
    uts = Collecting(bits, sum(r[3] for r in results))
    while not stats.done():
        phase(turn, [stats, uts])

    norm = jnp.sqrt(squares.x + EPSILON)
    coef = mag / norm
    cd = coef * stats.x / (norm * norm)
    half = rank // 2
    folded = []
    for i in range(2):
        g = jnp.concatenate([r[i] for r in results], axis=2).astype(F32)
        folded.append((coef * g - cd * ad[:, i * half : (i + 1) * half].astype(F32)).astype(BF))
    turning = Scattering(orders, n, *folded)
    while not uts.done():
        phase(turn, [turning, uts])
    seconds = phase(
        turn,
        [turning],
        lambda token: [second_call(weights, adapter_out, adapter_in, cd, 0, width, token)],
    )
    laying = Laying(orders, turning.own)
    pieces = turn.pass_on(*join_call(share, bits[::-1], turn.token, xs, seconds, [uts.x]))
    away = Around(n_row, pieces[1:])
    phase(turn, [laying, away])
    total = (pieces[0] + sum(x.astype(F32) for x in away.got)).astype(BF)
    back = Around(n_row, [total] * (n_row - 1))
    while laying.step or not back.done():
        phase(turn, [laying, back])
    (grad_in,) = phase(turn, [laying], lambda token: [lay_call(token, [total] + back.got)])
    grad_in = grad_in.reshape(2, -1, grad_in.shape[1])
    low, high = laying.held
    grad_out = order_call(n, orders, me, low, high, None, 0, width)
    grad_mag = (stats.x / norm)[:, 0, :]
    return (hidden, grad_in, grad_out, grad_mag)


def solution(mesh):
    in_specs = (
        P("row", "col"),
        P(None, "col", "row"),
        P(None, None, "col"),
        P(None, None, "row"),
        P(None, "row"),
        P("col", "row"),
    )
    out_specs = (P("col", "row"), P(None, None, "col"), P(None, None, "row"), P(None, "row"))
    return jax.shard_map(
        on_device, mesh=mesh, in_specs=in_specs, out_specs=out_specs, check_vma=False
    )
```

time: 218 us -> 147 us (0.67)
  Pallas kernels: 97.7 us -> 58.6 us
  starting transfers between devices: 62.9 us -> 41.9 us
  waiting for transfers between devices: 48.4 us -> 40.8 us
  local copies, waits for them, and re-layouts: 3.27 us -> 0.85 us
    pallas_call x5 -> x4, Pallas kernels: 58.1 us -> 34.6 us  [the longest x1 14.4 us: second_call(): pl.pallas_call(functools.partial(second_kernel, tile, size // tile, first...]
    ppermute x65 -> x41, starting transfers between devices: 62.9 us -> 41.9 us  [swap(): return lax.ppermute(x, axis, [(i, i ^ bit) for i in range(n)])]
    pallas_call x2, Pallas kernels: 29 us -> 18.4 us  [token_call(): pl.pallas_call(functools.partial(token_kernel, n, share, orders, len(xs),...]
    ppermute x65 -> x41, waiting for transfers between devices: 48.4 us -> 40.8 us  [swap(): return lax.ppermute(x, axis, [(i, i ^ bit) for i in range(n)])]
    pallas_call x2 -> x1, Pallas kernels: 8.18 us -> 3.3 us  [order_call(): pl.pallas_call(functools.partial(order_kernel, n, orders, prior is not No...]
    unnamed x25 -> x22, local copies, waits for them, and re-layouts: 3.21 us -> 0.76 us
  transfers between devices with their start and end apart: 65 -> 41, of which waited for: 20 -> 16; matrix products, arithmetic and copies ran while one was open for 2% -> 1% of each run, Pallas kernels for 43% -> 35%
where the time goes in v2:
time: 147 us
  Pallas kernels  58.6 us (40%)
  starting transfers between devices  41.9 us (29%)
  waiting for transfers between devices  40.8 us (28%)
  other arithmetic  3.37 us (2%)
    ppermute x41, starting transfers between devices, swap(): return lax.ppermute(x, axis, [(i, i ^ bit) for i in range(n)])  41.9 us
    ppermute x41, waiting for transfers between devices, swap(): return lax.ppermute(x, axis, [(i, i ^ bit) for i in range(n)])  40.8 us
    pallas_call x2, Pallas kernels, token_call(): pl.pallas_call(functools.partial(token_kernel, n, share, orders, len(xs),...  18.4 us
    pallas_call x1, Pallas kernels, second_call(): pl.pallas_call(functools.partial(second_kernel, tile, size // tile, first...  14.4 us
    pallas_call x1, Pallas kernels, adapter_call(): pl.pallas_call(functools.partial(adapter_kernel, n, orders, tile, width /...  13.6 us
    pallas_call x2, Pallas kernels, own_call(): pl.pallas_call(functools.partial(own_kernel, n, orders, len(parts), len(x...  6.72 us
    pallas_call x1, Pallas kernels, order_call(): pl.pallas_call(functools.partial(order_kernel, n, orders, prior is not No...  3.3 us
  transfers between devices with their start and end apart: 41, of which 16 were waited for; matrix products, arithmetic and copies ran while one was open for 1% of the time, Pallas kernels for 35%

profile of v2, /device:TPU:0, one launch (start us, length us, event | category | flops | bytes accessed | tf_op | source)
XLA Modules:
  0.0 146.6 jit_solution(13127360980834802873)
XLA Ops:
  0.6 4.1 %collective-permute-start.1 = (bf16[64,1024]{1,0:T(8,128)(2,1)}, bf16[64,1024]{1,0:T(8,128)(2,1)S(1)}, u32[]{:S(2)}, u32[]{:S(2)}) collective-permute-start(bf16[64,1024]{1,0:T(8,128)(2,1)} %refs_0_.2), channel_id=1, source_target_pairs={{0,16},{8,24},{16,0},{24,8},{1,17},{9,25},{17,1},{25,9},{2,18},{10... | collective-permute-start | bytes 393224 | tf_op jit(solution)/shard_map/ppermute | solution.py:40
  4.7 1.6 %collective-permute-start = (bf16[64,1024]{1,0:T(8,128)(2,1)}, bf16[64,1024]{1,0:T(8,128)(2,1)S(1)}, u32[]{:S(2)}, u32[]{:S(2)}) collective-permute-start(bf16[64,1024]{1,0:T(8,128)(2,1)} %refs_0_.2), channel_id=1, source_target_pairs={{0,8},{8,0},{16,24},{24,16},{1,9},{9,1},{17,25},{25,17},{2,10},{10... | collective-permute-start | bytes 393224 | tf_op jit(solution)/shard_map/ppermute | solution.py:40
  6.9 13.6 %adapter_pass.1 = (bf16[2,64,7168]{2,1,0:T(8,128)(2,1)}, f32[2,1,7168]{2,1,0:T(1,128)}) custom-call(s32[2]{0:T(128)} %pad_add_fusion.me_ref.token_ref, bf16[2,64,1024]{2,1,0:T(8,128)(2,1)} %a_ref.3, bf16[2,1024,7168]{2,1,0:T(8,128)(2,1)} %w_ref.3, bf16[2,64,7168]{2,1,0:T(8,128)(2,1)} %b_ref.3), custom_call_target="tpu_custom_call" | custom-call | flops 3758096384 | bytes 29360128 | tf_op jit(solution)/shard_map/adapter_pass/pallas_call | solution.py:140
  20.6 9.2 %token_pass.2 = (bf16[2,128,3584]{2,1,0:T(8,128)(2,1)S(1)}, bf16[2,128,3584]{2,1,0:T(8,128)(2,1)S(1)}, f32[128,128]{1,0:T(8,128)S(1)}, f32[128,128]{1,0:T(8,128)S(1)}) custom-call(s32[2]{0:T(128)S(1)} %copy-done.4, bf16[64,1024]{1,0:T(8,128)(2,1)S(1)} %copy-done.3, bf16[64,1024]{1,0:T(8,128)(2,1)S(1)} %collective-permute-done.refs_1_, ...), custom_call_target="tpu_custom_call" | custom-call | flops 3758096384 | bytes 14680064 | tf_op jit(solution)/shard_map/token_pass/pallas_call | solution.py:227
  30.5 1.7 %collective-permute-start.4 = (f32[2,1,7168]{2,1,0:T(1,128)S(1)}, f32[2,1,7168]{2,1,0:T(1,128)S(1)}, u32[]{:S(2)}, u32[]{:S(2)}) collective-permute-start(f32[2,1,7168]{2,1,0:T(1,128)S(1)} %add.115), channel_id=1, source_target_pairs={{0,2},{1,3},{2,0},{3,1},{4,6},{5,7},{6,4},{7,5},{8,10},{9,11},{10,... | collective-permute-start | bytes 172040 | tf_op jit(solution)/shard_map/ppermute | solution.py:40
  32.3 2.6 %collective-permute-done.4 = f32[2,1,7168]{2,1,0:T(1,128)S(1)} collective-permute-done((f32[2,1,7168]{2,1,0:T(1,128)S(1)}, f32[2,1,7168]{2,1,0:T(1,128)S(1)}, u32[]{:S(2)}, u32[]{:S(2)}) %collective-permute-start.4) | collective-permute-done | bytes 57376 | tf_op jit(solution)/shard_map/ppermute | solution.py:40
  35.1 1.8 %collective-permute-start.9 = (bf16[64,3584]{1,0:T(8,128)(2,1)S(1)}, bf16[64,3584]{1,0:T(8,128)(2,1)S(1)}, u32[]{:S(2)}, u32[]{:S(2)}) collective-permute-start(bf16[64,3584]{1,0:T(8,128)(2,1)S(1)} %get-tuple-element.185), channel_id=1, source_target_pairs={{0,2},{1,3},{2,0},{3,1},{4,6},{5,7},{6,4},{7,5},{8,10},{9,11},{10,... | collective-permute-start | bytes 1376264 | tf_op jit(solution)/shard_map/ppermute | solution.py:40
  36.9 1.5 %collective-permute-start.10 = (bf16[64,3584]{1,0:T(8,128)(2,1)S(1)}, bf16[64,3584]{1,0:T(8,128)(2,1)S(1)}, u32[]{:S(2)}, u32[]{:S(2)}) collective-permute-start(bf16[64,3584]{1,0:T(8,128)(2,1)S(1)} %get-tuple-element.186), channel_id=1, source_target_pairs={{0,4},{1,5},{2,6},{3,7},{4,0},{5,1},{6,2},{7,3},{8,12},{9,13},{10,... | collective-permute-start | bytes 1376264 | tf_op jit(solution)/shard_map/ppermute | solution.py:40
  39.2 9.2 %token_pass.3 = (bf16[2,128,3584]{2,1,0:T(8,128)(2,1)S(1)}, bf16[2,128,3584]{2,1,0:T(8,128)(2,1)S(1)}) custom-call(s32[2]{0:T(128)S(1)} %copy-done.4, bf16[64,1024]{1,0:T(8,128)(2,1)S(1)} %copy-done.3, bf16[64,1024]{1,0:T(8,128)(2,1)S(1)} %collective-permute-done.refs_1_, bf16[64,1024]{1,0:T(8,128)(2,1)S(1)} %collective-permute-done.1.refs_2_, ...), custom_call_target="tpu_custom_call" | custom-call | flops 3758096384 | bytes 14680064 | tf_op jit(solution)/shard_map/token_pass/pallas_call | solution.py:227
  48.5 1.5 %collective-permute-done.7 = f32[2,1,7168]{2,1,0:T(1,128)S(1)} collective-permute-done((f32[2,1,7168]{2,1,0:T(1,128)S(1)}, f32[2,1,7168]{2,1,0:T(1,128)S(1)}, u32[]{:S(2)}, u32[]{:S(2)}) %collective-permute-start.7) | collective-permute-done | bytes 57376 | tf_op jit(solution)/shard_map/ppermute | solution.py:40
  50.2 1.6 %collective-permute-start.12 = (bf16[32,3584]{1,0:T(8,128)(2,1)S(1)}, bf16[32,3584]{1,0:T(8,128)(2,1)S(1)}, u32[]{:S(2)}, u32[]{:S(2)}) collective-permute-start(bf16[32,3584]{1,0:T(8,128)(2,1)S(1)} %get-tuple-element.196), channel_id=1, source_target_pairs={{0,4},{1,5},{2,6},{3,7},{4,0},{5,1},{6,2},{7,3},{8,12},{9,13},{10,... | collective-permute-start | bytes 688136 | tf_op jit(solution)/shard_map/ppermute | solution.py:40
  52.7 5.9 %collective-permute-done.11.refs_11_ = f32[32,128]{1,0:T(8,128)S(1)} collective-permute-done((f32[32,128]{1,0:T(8,128)S(1)}, f32[32,128]{1,0:T(8,128)S(1)}, u32[]{:S(2)}, u32[]{:S(2)}) %collective-permute-start.11) | collective-permute-done | bytes 16416 | tf_op jit(solution)/shard_map/ppermute | solution.py:40
  61.1 3.3 %own_tokens.2 = (bf16[32,7168]{1,0:T(8,128)(2,1)}, bf16[2,32,3584]{2,1,0:T(8,128)(2,1)S(1)}, bf16[2,32,3584]{2,1,0:T(8,128)(2,1)S(1)}, f32[2,1,3584]{2,1,0:T(1,128)S(1)}, f32[2,32,64]{2,1,0:T(8,128)S(1)}) custom-call(s32[2]{0:T(128)S(1)} %copy-done.4, bf16[2,128,3584]{2,1,0:T(8,128)(2,1)S(1)} %get-tuple-element.180.refs_0_.refs_1_, ...), custom_call_target="tpu_custom_call" | custom-call | flops 58720256 | bytes 2293760 | tf_op jit(solution)/shard_map/own_tokens/pallas_call | solution.py:326
  64.4 7.1 %collective-permute-done.15.refs_4_ = bf16[64,3584]{1,0:T(8,128)(2,1)S(1)} collective-permute-done((bf16[64,3584]{1,0:T(8,128)(2,1)S(1)}, bf16[64,3584]{1,0:T(8,128)(2,1)S(1)}, u32[]{:S(2)}, u32[]{:S(2)}) %collective-permute-start.15) | collective-permute-done | bytes 458784 | tf_op jit(solution)/shard_map/ppermute | solution.py:40
  73.0 1.5 %collective-permute-start.18 = (bf16[32,3584]{1,0:T(8,128)(2,1)S(1)}, bf16[32,3584]{1,0:T(8,128)(2,1)S(1)}, u32[]{:S(2)}, u32[]{:S(2)}) collective-permute-start(bf16[32,3584]{1,0:T(8,128)(2,1)S(1)} %get-tuple-element.219), channel_id=1, source_target_pairs={{0,2},{1,3},{2,0},{3,1},{4,6},{5,7},{6,4},{7,5},{8,10},{9,11},{10,... | collective-permute-start | bytes 688136 | tf_op jit(solution)/shard_map/ppermute | solution.py:40
  74.5 3.6 %collective-permute-done.17.refs_6_ = bf16[32,3584]{1,0:T(8,128)(2,1)S(1)} collective-permute-done((bf16[32,3584]{1,0:T(8,128)(2,1)S(1)}, bf16[32,3584]{1,0:T(8,128)(2,1)S(1)}, u32[]{:S(2)}, u32[]{:S(2)}) %collective-permute-start.17) | collective-permute-done | bytes 229408 | tf_op jit(solution)/shard_map/ppermute | solution.py:40
  79.1 3.4 %own_tokens.3 = (bf16[32,7168]{1,0:T(8,128)(2,1)}, bf16[2,32,3584]{2,1,0:T(8,128)(2,1)S(1)}, bf16[2,32,3584]{2,1,0:T(8,128)(2,1)S(1)}, f32[2,1,3584]{2,1,0:T(1,128)S(1)}, f32[2,32,64]{2,1,0:T(8,128)S(1)}) custom-call(s32[2]{0:T(128)S(1)} %copy-done.4, bf16[2,128,3584]{2,1,0:T(8,128)(2,1)S(1)} %get-tuple-element.200.refs_0_.refs_1_, ...), custom_call_target="tpu_custom_call", output_to_operand_aliasing={{0}: (17, {})} | custom-call | flops 58720256 | bytes 2293760 | tf_op jit(solution)/shard_map/own_tokens/pallas_call | solution.py:326
  84.1 2.0 %collective-permute-start.23 = (f32[2,1,7168]{2,1,0:T(1,128)S(1)}, f32[2,1,7168]{2,1,0:T(1,128)S(1)}, u32[]{:S(2)}, u32[]{:S(2)}) collective-permute-start(f32[2,1,7168]{2,1,0:T(1,128)S(1)} %add.138), channel_id=1, source_target_pairs={{0,6},{1,7},{2,4},{3,5},{4,2},{5,3},{6,0},{7,1},{8,14},{9,15},{10,... | collective-permute-start | bytes 172040 | tf_op jit(solution)/shard_map/ppermute | solution.py:40
  87.6 1.5 %collective-permute-start.24 = (f32[2,64,64]{2,1,0:T(8,128)S(1)}, f32[2,64,64]{2,1,0:T(8,128)S(1)}, u32[]{:S(2)}, u32[]{:S(2)}) collective-permute-start(f32[2,64,64]{2,1,0:T(8,128)S(1)} %pad_maximum_fusion.8), channel_id=1, source_target_pairs={{0,2},{1,3},{2,0},{3,1},{4,6},{5,7},{6,4},{7,5},{8,10},{9,11},{10,... | collective-permute-start | bytes 98312 | tf_op jit(solution)/shard_map/ppermute | solution.py:40
  89.1 3.0 %collective-permute-done.24 = f32[2,64,64]{2,1,0:T(8,128)S(1)} collective-permute-done((f32[2,64,64]{2,1,0:T(8,128)S(1)}, f32[2,64,64]{2,1,0:T(8,128)S(1)}, u32[]{:S(2)}, u32[]{:S(2)}) %collective-permute-start.24) | collective-permute-done | bytes 32800 | tf_op jit(solution)/shard_map/ppermute | solution.py:40
  94.2 4.8 %collective-permute-done.26 = f32[2,128,64]{2,1,0:T(8,128)S(1)} collective-permute-done((f32[2,128,64]{2,1,0:T(8,128)S(1)}, f32[2,128,64]{2,1,0:T(8,128)S(1)}, u32[]{:S(2)}, u32[]{:S(2)}) %collective-permute-start.26) | collective-permute-done | bytes 65568 | tf_op jit(solution)/shard_map/ppermute | solution.py:40
  99.6 1.3 collective-permute-start.27
  103.2 14.4 %second_pass.1.refs_4_ = f32[2,64,1024]{2,1,0:T(8,128)S(1)} custom-call(s32[2]{0:T(128)S(1)} %copy-done.4, bf16[2,1024,7168]{2,1,0:T(8,128)(2,1)} %w_ref.3, bf16[2,64,7168]{2,1,0:T(8,128)(2,1)S(1)} %copy-done, bf16[2,64,1024]{2,1,0:T(8,128)(2,1)S(1)} %copy-done.1, f32[2,1,7168]{2,1,0:T(1,128)S(1)} %get-tuple-element.310.cd_ref), custom_call_target="tpu_custom_call" | custom-call | flops 1879048192 | bytes 29360128 | tf_op jit(solution)/shard_map/second_pass/pallas_call | solution.py:382
  119.8 1.3 collective-permute-start.31
  121.7 3.5 %collective-permute-start.33 = (bf16[32,1024]{1,0:T(8,128)(2,1)S(1)}, bf16[32,1024]{1,0:T(8,128)(2,1)S(1)}, u32[]{:S(2)}, u32[]{:S(2)}) collective-permute-start(bf16[32,1024]{1,0:T(8,128)(2,1)S(1)} %get-tuple-element.281), channel_id=1, source_target_pairs={{0,16},{8,24},{16,0},{24,8},{1,17},{9,25},{17,1},{25,9},{2,18},{10... | collective-permute-start | bytes 196616 | tf_op jit(solution)/shard_map/ppermute | solution.py:40
  125.5 3.4 %collective-permute-done.33 = bf16[32,1024]{1,0:T(8,128)(2,1)S(1)} collective-permute-done((bf16[32,1024]{1,0:T(8,128)(2,1)S(1)}, bf16[32,1024]{1,0:T(8,128)(2,1)S(1)}, u32[]{:S(2)}, u32[]{:S(2)}) %collective-permute-start.33) | collective-permute-done | bytes 65568 | tf_op jit(solution)/shard_map/ppermute | solution.py:40
  128.9 2.4 %collective-permute-done.34 = bf16[32,1024]{1,0:T(8,128)(2,1)S(1)} collective-permute-done((bf16[32,1024]{1,0:T(8,128)(2,1)S(1)}, bf16[32,1024]{1,0:T(8,128)(2,1)S(1)}, u32[]{:S(2)}, u32[]{:S(2)}) %collective-permute-start.34) | collective-permute-done | bytes 65568 | tf_op jit(solution)/shard_map/ppermute | solution.py:40
  133.2 1.3 collective-permute-start.38
  134.5 3.0 %collective-permute-start.39 = (bf16[32,1024]{1,0:T(8,128)(2,1)S(1)}, bf16[32,1024]{1,0:T(8,128)(2,1)S(1)}, u32[]{:S(2)}, u32[]{:S(2)}) collective-permute-start(bf16[32,1024]{1,0:T(8,128)(2,1)S(1)} %add_convert_fusion.4.refs_0_), channel_id=1, source_target_pairs={{0,24},{8,16},{16,8},{24,0},{1,25},{9,17},{17,9},{25,1},{2,26},{10... | collective-permute-start | bytes 196616 | tf_op jit(solution)/shard_map/ppermute | solution.py:40
  138.4 2.2 %collective-permute-done.39.refs_3_ = bf16[32,1024]{1,0:T(8,128)(2,1)S(1)} collective-permute-done((bf16[32,1024]{1,0:T(8,128)(2,1)S(1)}, bf16[32,1024]{1,0:T(8,128)(2,1)S(1)}, u32[]{:S(2)}, u32[]{:S(2)}) %collective-permute-start.39) | collective-permute-done | bytes 65568 | tf_op jit(solution)/shard_map/ppermute | solution.py:40
  141.5 1.4 lay_grad_in.1
  143.3 3.3 %order_rows.1 = f32[2,64,7168]{2,1,0:T(8,128)} custom-call(s32[2]{0:T(128)S(1)} %copy-done.4, bf16[2,32,7168]{2,1,0:T(8,128)(2,1)S(1)} %pad_maximum_fusion.low_ref, bf16[2,32,7168]{2,1,0:T(8,128)(2,1)S(1)} %collective-permute-done.40.high_ref), custom_call_target="tpu_custom_call" | custom-call | tf_op jit(solution)/shard_map/order_rows/pallas_call | solution.py:487
  (114 shorter events, 23.5 us)
Async XLA Ops:
  0.6 19.8 %collective-permute-start.1 = (bf16[64,1024]{1,0:T(8,128)(2,1)}, bf16[64,1024]{1,0:T(8,128)(2,1)S(1)}, u32[]{:S(2)}, u32[]{:S(2)}) collective-permute-start(bf16[64,1024]{1,0:T(8,128)(2,1)} %refs_0_.2), channel_id=1, source_target_pairs={{0,16},{8,24},{16,0},{24,8},{1,17},{9,25},{17,1},{25,9},{2,18},{10... | collective-permute-start | bytes 393224 | tf_op jit(solution)/shard_map/ppermute | solution.py:40
  4.7 15.7 %collective-permute-start = (bf16[64,1024]{1,0:T(8,128)(2,1)}, bf16[64,1024]{1,0:T(8,128)(2,1)S(1)}, u32[]{:S(2)}, u32[]{:S(2)}) collective-permute-start(bf16[64,1024]{1,0:T(8,128)(2,1)} %refs_0_.2), channel_id=1, source_target_pairs={{0,8},{8,0},{16,24},{24,16},{1,9},{9,1},{17,25},{25,17},{2,10},{10... | collective-permute-start | bytes 393224 | tf_op jit(solution)/shard_map/ppermute | solution.py:40
  6.3 14.2 %collective-permute-start.2 = (bf16[64,1024]{1,0:T(8,128)(2,1)}, bf16[64,1024]{1,0:T(8,128)(2,1)S(1)}, u32[]{:S(2)}, u32[]{:S(2)}) collective-permute-start(bf16[64,1024]{1,0:T(8,128)(2,1)} %refs_0_.2), channel_id=1, source_target_pairs={{0,24},{8,16},{16,8},{24,0},{1,25},{9,17},{17,9},{25,1},{2,26},{10... | collective-permute-start | bytes 393224 | tf_op jit(solution)/shard_map/ppermute | solution.py:40
  20.5 9.3 %collective-permute-start.3 = (f32[2,1,7168]{2,1,0:T(1,128)}, f32[2,1,7168]{2,1,0:T(1,128)S(1)}, u32[]{:S(2)}, u32[]{:S(2)}) collective-permute-start(f32[2,1,7168]{2,1,0:T(1,128)} %get-tuple-element.159), channel_id=1, source_target_pairs={{0,1},{1,0},{2,3},{3,2},{4,5},{5,4},{6,7},{7,6},{8,9},{9,8},{10,11... | collective-permute-start | bytes 172040 | tf_op jit(solution)/shard_map/ppermute | solution.py:40
  35.1 14.8 %collective-permute-start.9 = (bf16[64,3584]{1,0:T(8,128)(2,1)S(1)}, bf16[64,3584]{1,0:T(8,128)(2,1)S(1)}, u32[]{:S(2)}, u32[]{:S(2)}) collective-permute-start(bf16[64,3584]{1,0:T(8,128)(2,1)S(1)} %get-tuple-element.185), channel_id=1, source_target_pairs={{0,2},{1,3},{2,0},{3,1},{4,6},{5,7},{6,4},{7,5},{8,10},{9,11},{10,... | collective-permute-start | bytes 1376264 | tf_op jit(solution)/shard_map/ppermute | solution.py:40
  36.9 13.0 %collective-permute-start.10 = (bf16[64,3584]{1,0:T(8,128)(2,1)S(1)}, bf16[64,3584]{1,0:T(8,128)(2,1)S(1)}, u32[]{:S(2)}, u32[]{:S(2)}) collective-permute-start(bf16[64,3584]{1,0:T(8,128)(2,1)S(1)} %get-tuple-element.186), channel_id=1, source_target_pairs={{0,4},{1,5},{2,6},{3,7},{4,0},{5,1},{6,2},{7,3},{8,12},{9,13},{10,... | collective-permute-start | bytes 1376264 | tf_op jit(solution)/shard_map/ppermute | solution.py:40
  38.4 10.0 %collective-permute-start.8 = (f32[64,128]{1,0:T(8,128)S(1)}, f32[64,128]{1,0:T(8,128)S(1)}, u32[]{:S(2)}, u32[]{:S(2)}) collective-permute-start(f32[64,128]{1,0:T(8,128)S(1)} %slice_add_fusion.2), channel_id=1, source_target_pairs={{0,2},{1,3},{2,0},{3,1},{4,6},{5,7},{6,4},{7,5},{8,10},{9,11},{10,... | collective-permute-start | bytes 98312 | tf_op jit(solution)/shard_map/ppermute | solution.py:40
  39.0 11.0 %collective-permute-start.7 = (f32[2,1,7168]{2,1,0:T(1,128)S(1)}, f32[2,1,7168]{2,1,0:T(1,128)S(1)}, u32[]{:S(2)}, u32[]{:S(2)}) collective-permute-start(f32[2,1,7168]{2,1,0:T(1,128)S(1)} %add.116), channel_id=1, source_target_pairs={{0,4},{1,5},{2,6},{3,7},{4,0},{5,1},{6,2},{7,3},{8,12},{9,13},{10,... | collective-permute-start | bytes 172040 | tf_op jit(solution)/shard_map/ppermute | solution.py:40
  50.2 9.3 %collective-permute-start.14 = (bf16[2,128,3584]{2,1,0:T(8,128)(2,1)S(1)}, bf16[2,128,3584]{2,1,0:T(8,128)(2,1)S(1)}, u32[]{:S(2)}, u32[]{:S(2)}) collective-permute-start(bf16[2,128,3584]{2,1,0:T(8,128)(2,1)S(1)} %get-tuple-element.198), channel_id=1, source_target_pairs={{0,1},{1,0},{2,3},{3,2},{4,5},{5,4},{6,7},{7,6},{8,9},{9,8},{10,11... | collective-permute-start | bytes 5505032 | tf_op jit(solution)/shard_map/ppermute | solution.py:40
  50.2 8.4 %collective-permute-start.12 = (bf16[32,3584]{1,0:T(8,128)(2,1)S(1)}, bf16[32,3584]{1,0:T(8,128)(2,1)S(1)}, u32[]{:S(2)}, u32[]{:S(2)}) collective-permute-start(bf16[32,3584]{1,0:T(8,128)(2,1)S(1)} %get-tuple-element.196), channel_id=1, source_target_pairs={{0,4},{1,5},{2,6},{3,7},{4,0},{5,1},{6,2},{7,3},{8,12},{9,13},{10,... | collective-permute-start | bytes 688136 | tf_op jit(solution)/shard_map/ppermute | solution.py:40
  51.8 7.7 %collective-permute-start.13 = (bf16[32,3584]{1,0:T(8,128)(2,1)S(1)}, bf16[32,3584]{1,0:T(8,128)(2,1)S(1)}, u32[]{:S(2)}, u32[]{:S(2)}) collective-permute-start(bf16[32,3584]{1,0:T(8,128)(2,1)S(1)} %get-tuple-element.197), channel_id=1, source_target_pairs={{0,2},{1,3},{2,0},{3,1},{4,6},{5,7},{6,4},{7,5},{8,10},{9,11},{10,... | collective-permute-start | bytes 688136 | tf_op jit(solution)/shard_map/ppermute | solution.py:40
  52.4 6.2 %collective-permute-start.11 = (f32[32,128]{1,0:T(8,128)S(1)}, f32[32,128]{1,0:T(8,128)S(1)}, u32[]{:S(2)}, u32[]{:S(2)}) collective-permute-start(f32[32,128]{1,0:T(8,128)S(1)} %slice_add_fusion.3), channel_id=1, source_target_pairs={{0,4},{1,5},{2,6},{3,7},{4,0},{5,1},{6,2},{7,3},{8,12},{9,13},{10,... | collective-permute-start | bytes 49160 | tf_op jit(solution)/shard_map/ppermute | solution.py:40
  59.7 11.8 %collective-permute-start.15 = (bf16[64,3584]{1,0:T(8,128)(2,1)S(1)}, bf16[64,3584]{1,0:T(8,128)(2,1)S(1)}, u32[]{:S(2)}, u32[]{:S(2)}) collective-permute-start(bf16[64,3584]{1,0:T(8,128)(2,1)S(1)} %get-tuple-element.203), channel_id=1, source_target_pairs={{0,2},{1,3},{2,0},{3,1},{4,6},{5,7},{6,4},{7,5},{8,10},{9,11},{10,... | collective-permute-start | bytes 1376264 | tf_op jit(solution)/shard_map/ppermute | solution.py:40
  60.3 11.5 %collective-permute-start.16 = (bf16[64,3584]{1,0:T(8,128)(2,1)S(1)}, bf16[64,3584]{1,0:T(8,128)(2,1)S(1)}, u32[]{:S(2)}, u32[]{:S(2)}) collective-permute-start(bf16[64,3584]{1,0:T(8,128)(2,1)S(1)} %get-tuple-element.204), channel_id=1, source_target_pairs={{0,4},{1,5},{2,6},{3,7},{4,0},{5,1},{6,2},{7,3},{8,12},{9,13},{10,... | collective-permute-start | bytes 1376264 | tf_op jit(solution)/shard_map/ppermute | solution.py:40
  72.0 6.1 %collective-permute-start.17 = (bf16[32,3584]{1,0:T(8,128)(2,1)S(1)}, bf16[32,3584]{1,0:T(8,128)(2,1)S(1)}, u32[]{:S(2)}, u32[]{:S(2)}) collective-permute-start(bf16[32,3584]{1,0:T(8,128)(2,1)S(1)} %get-tuple-element.218), channel_id=1, source_target_pairs={{0,4},{1,5},{2,6},{3,7},{4,0},{5,1},{6,2},{7,3},{8,12},{9,13},{10,... | collective-permute-start | bytes 688136 | tf_op jit(solution)/shard_map/ppermute | solution.py:40
  73.0 6.0 %collective-permute-start.18 = (bf16[32,3584]{1,0:T(8,128)(2,1)S(1)}, bf16[32,3584]{1,0:T(8,128)(2,1)S(1)}, u32[]{:S(2)}, u32[]{:S(2)}) collective-permute-start(bf16[32,3584]{1,0:T(8,128)(2,1)S(1)} %get-tuple-element.219), channel_id=1, source_target_pairs={{0,2},{1,3},{2,0},{3,1},{4,6},{5,7},{6,4},{7,5},{8,10},{9,11},{10,... | collective-permute-start | bytes 688136 | tf_op jit(solution)/shard_map/ppermute | solution.py:40
  84.1 8.0 %collective-permute-start.23 = (f32[2,1,7168]{2,1,0:T(1,128)S(1)}, f32[2,1,7168]{2,1,0:T(1,128)S(1)}, u32[]{:S(2)}, u32[]{:S(2)}) collective-permute-start(f32[2,1,7168]{2,1,0:T(1,128)S(1)} %add.138), channel_id=1, source_target_pairs={{0,6},{1,7},{2,4},{3,5},{4,2},{5,3},{6,0},{7,1},{8,14},{9,15},{10,... | collective-permute-start | bytes 172040 | tf_op jit(solution)/shard_map/ppermute | solution.py:40
  86.1 6.0 %collective-permute-start.22 = (f32[2,1,7168]{2,1,0:T(1,128)S(1)}, f32[2,1,7168]{2,1,0:T(1,128)S(1)}, u32[]{:S(2)}, u32[]{:S(2)}) collective-permute-start(f32[2,1,7168]{2,1,0:T(1,128)S(1)} %add.138), channel_id=1, source_target_pairs={{0,4},{1,5},{2,6},{3,7},{4,0},{5,1},{6,2},{7,3},{8,12},{9,13},{10,... | collective-permute-start | bytes 172040 | tf_op jit(solution)/shard_map/ppermute | solution.py:40
  87.1 5.0 %collective-permute-start.21 = (f32[2,1,7168]{2,1,0:T(1,128)S(1)}, f32[2,1,7168]{2,1,0:T(1,128)S(1)}, u32[]{:S(2)}, u32[]{:S(2)}) collective-permute-start(f32[2,1,7168]{2,1,0:T(1,128)S(1)} %add.138), channel_id=1, source_target_pairs={{0,2},{1,3},{2,0},{3,1},{4,6},{5,7},{6,4},{7,5},{8,10},{9,11},{10,... | collective-permute-start | bytes 172040 | tf_op jit(solution)/shard_map/ppermute | solution.py:40
  93.0 6.0 %collective-permute-start.25 = (bf16[2,32,7168]{2,1,0:T(8,128)(2,1)S(1)}, bf16[2,32,7168]{2,1,0:T(8,128)(2,1)S(1)}, u32[]{:S(2)}, u32[]{:S(2)}) collective-permute-start(bf16[2,32,7168]{2,1,0:T(8,128)(2,1)S(1)} %subtract_convert_fusion.1), channel_id=1, source_target_pairs={{0,1},{1,0},{2,3},{3,2},{4,5},{5,4},{6,7},{7,6},{8,9},{9,8},{10,11... | collective-permute-start | bytes 2752520 | tf_op jit(solution)/shard_map/ppermute | solution.py:40
  93.1 5.9 %collective-permute-start.26 = (f32[2,128,64]{2,1,0:T(8,128)S(1)}, f32[2,128,64]{2,1,0:T(8,128)S(1)}, u32[]{:S(2)}, u32[]{:S(2)}) collective-permute-start(f32[2,128,64]{2,1,0:T(8,128)S(1)} %pad_maximum_fusion.7), channel_id=1, source_target_pairs={{0,4},{1,5},{2,6},{3,7},{4,0},{5,1},{6,2},{7,3},{8,12},{9,13},{10,... | collective-permute-start | bytes 196616 | tf_op jit(solution)/shard_map/ppermute | solution.py:40
  99.6 18.0 %collective-permute-start.27 = (bf16[16,7168]{1,0:T(8,128)(2,1)S(1)}, bf16[16,7168]{1,0:T(8,128)(2,1)S(1)}, u32[]{:S(2)}, u32[]{:S(2)}) collective-permute-start(bf16[16,7168]{1,0:T(8,128)(2,1)S(1)} %pad_maximum_fusion.2), channel_id=1, source_target_pairs={{0,2},{1,3},{2,0},{3,1},{4,6},{5,7},{6,4},{7,5},{8,10},{9,11},{10,... | collective-permute-start | bytes 688136 | tf_op jit(solution)/shard_map/ppermute | solution.py:40
  101.0 16.6 %collective-permute-start.28 = (bf16[16,7168]{1,0:T(8,128)(2,1)S(1)}, bf16[16,7168]{1,0:T(8,128)(2,1)S(1)}, u32[]{:S(2)}, u32[]{:S(2)}) collective-permute-start(bf16[16,7168]{1,0:T(8,128)(2,1)S(1)} %pad_maximum_fusion.3), channel_id=1, source_target_pairs={{0,4},{1,5},{2,6},{3,7},{4,0},{5,1},{6,2},{7,3},{8,12},{9,13},{10,... | collective-permute-start | bytes 688136 | tf_op jit(solution)/shard_map/ppermute | solution.py:40
  102.0 15.6 %collective-permute-start.29 = (bf16[16,7168]{1,0:T(8,128)(2,1)S(1)}, bf16[16,7168]{1,0:T(8,128)(2,1)S(1)}, u32[]{:S(2)}, u32[]{:S(2)}) collective-permute-start(bf16[16,7168]{1,0:T(8,128)(2,1)S(1)} %pad_maximum_fusion.4), channel_id=1, source_target_pairs={{0,6},{1,7},{2,4},{3,5},{4,2},{5,3},{6,0},{7,1},{8,14},{9,15},{10,... | collective-permute-start | bytes 688136 | tf_op jit(solution)/shard_map/ppermute | solution.py:40
  118.7 12.6 %collective-permute-start.30 = (bf16[8,7168]{1,0:T(8,128)(2,1)S(1)}, bf16[8,7168]{1,0:T(8,128)(2,1)S(1)}, u32[]{:S(2)}, u32[]{:S(2)}) collective-permute-start(bf16[8,7168]{1,0:T(8,128)(2,1)S(1)} %get-tuple-element.278), channel_id=1, source_target_pairs={{0,4},{1,5},{2,6},{3,7},{4,0},{5,1},{6,2},{7,3},{8,12},{9,13},{10,... | collective-permute-start | bytes 344072 | tf_op jit(solution)/shard_map/ppermute | solution.py:40
  119.8 11.5 %collective-permute-start.31 = (bf16[8,7168]{1,0:T(8,128)(2,1)S(1)}, bf16[8,7168]{1,0:T(8,128)(2,1)S(1)}, u32[]{:S(2)}, u32[]{:S(2)}) collective-permute-start(bf16[8,7168]{1,0:T(8,128)(2,1)S(1)} %get-tuple-element.279), channel_id=1, source_target_pairs={{0,2},{1,3},{2,0},{3,1},{4,6},{5,7},{6,4},{7,5},{8,10},{9,11},{10,... | collective-permute-start | bytes 344072 | tf_op jit(solution)/shard_map/ppermute | solution.py:40
  121.7 7.1 %collective-permute-start.33 = (bf16[32,1024]{1,0:T(8,128)(2,1)S(1)}, bf16[32,1024]{1,0:T(8,128)(2,1)S(1)}, u32[]{:S(2)}, u32[]{:S(2)}) collective-permute-start(bf16[32,1024]{1,0:T(8,128)(2,1)S(1)} %get-tuple-element.281), channel_id=1, source_target_pairs={{0,16},{8,24},{16,0},{24,8},{1,17},{9,25},{17,1},{25,9},{2,18},{10... | collective-permute-start | bytes 196616 | tf_op jit(solution)/shard_map/ppermute | solution.py:40
  125.2 6.1 %collective-permute-start.34 = (bf16[32,1024]{1,0:T(8,128)(2,1)S(1)}, bf16[32,1024]{1,0:T(8,128)(2,1)S(1)}, u32[]{:S(2)}, u32[]{:S(2)}) collective-permute-start(bf16[32,1024]{1,0:T(8,128)(2,1)S(1)} %get-tuple-element.282), channel_id=1, source_target_pairs={{0,24},{8,16},{16,8},{24,0},{1,25},{9,17},{17,9},{25,1},{2,26},{10... | collective-permute-start | bytes 196616 | tf_op jit(solution)/shard_map/ppermute | solution.py:40
  131.4 9.2 %collective-permute-start.35 = (bf16[16,7168]{1,0:T(8,128)(2,1)S(1)}, bf16[16,7168]{1,0:T(8,128)(2,1)S(1)}, u32[]{:S(2)}, u32[]{:S(2)}) collective-permute-start(bf16[16,7168]{1,0:T(8,128)(2,1)S(1)} %pad_maximum_fusion.5), channel_id=1, source_target_pairs={{0,2},{1,3},{2,0},{3,1},{4,6},{5,7},{6,4},{7,5},{8,10},{9,11},{10,... | collective-permute-start | bytes 688136 | tf_op jit(solution)/shard_map/ppermute | solution.py:40
  132.2 8.4 %collective-permute-start.36 = (bf16[16,7168]{1,0:T(8,128)(2,1)S(1)}, bf16[16,7168]{1,0:T(8,128)(2,1)S(1)}, u32[]{:S(2)}, u32[]{:S(2)}) collective-permute-start(bf16[16,7168]{1,0:T(8,128)(2,1)S(1)} %pad_maximum_fusion.6), channel_id=1, source_target_pairs={{0,4},{1,5},{2,6},{3,7},{4,0},{5,1},{6,2},{7,3},{8,12},{9,13},{10,... | collective-permute-start | bytes 688136 | tf_op jit(solution)/shard_map/ppermute | solution.py:40
  133.2 5.2 %collective-permute-start.38 = (bf16[32,1024]{1,0:T(8,128)(2,1)S(1)}, bf16[32,1024]{1,0:T(8,128)(2,1)S(1)}, u32[]{:S(2)}, u32[]{:S(2)}) collective-permute-start(bf16[32,1024]{1,0:T(8,128)(2,1)S(1)} %add_convert_fusion.4.refs_0_), channel_id=1, source_target_pairs={{0,16},{8,24},{16,0},{24,8},{1,17},{9,25},{17,1},{25,9},{2,18},{10... | collective-permute-start | bytes 196616 | tf_op jit(solution)/shard_map/ppermute | solution.py:40
  134.5 6.1 %collective-permute-start.39 = (bf16[32,1024]{1,0:T(8,128)(2,1)S(1)}, bf16[32,1024]{1,0:T(8,128)(2,1)S(1)}, u32[]{:S(2)}, u32[]{:S(2)}) collective-permute-start(bf16[32,1024]{1,0:T(8,128)(2,1)S(1)} %add_convert_fusion.4.refs_0_), channel_id=1, source_target_pairs={{0,24},{8,16},{16,8},{24,0},{1,25},{9,17},{17,9},{25,1},{2,26},{10... | collective-permute-start | bytes 196616 | tf_op jit(solution)/shard_map/ppermute | solution.py:40
  (19 other events, 149.1 us)

commit v3 on v2

--- a/solution.py
+++ b/solution.py
@@ -19,7 +19,7 @@
 
 
 def tile_of(width, largest):
-    for tile in (1792, 1024, 896, 512, 256, 128):
+    for tile in (3584, 1792, 1024, 896, 512, 256, 128):
         if tile <= largest and width % tile == 0:
             return tile
     return width
@@ -65,6 +65,37 @@
             copy(at + ahead).start()
 
     return buf.at[at % slots], wait
+
+
+class Stream:
+    def __init__(self, w_ref, buf, sem, step, per, first):
+        self.w_ref, self.buf, self.sem = w_ref, buf, sem
+        self.step, self.per, self.first = step, per, first
+        self.slots, self.total = buf.shape[0], 2 * per
+        self.ahead = max(self.slots - 2, 1)
+        for i in range(min(self.ahead, self.total)):
+            self.copy(jnp.int32(i)).start()
+
+    def copy(self, i):
+        start = pl.multiple_of(self.first + (i % self.per) * self.step, self.step)
+        slot = i % self.slots
+        return pltpu.make_async_copy(
+            self.w_ref.at[i // self.per, :, pl.ds(start, self.step)], self.buf.at[slot], self.sem.at[slot]
+        )
+
+    def over(self, p, body):
+        @pl.loop(0, self.per)
+        def _(f):
+            at = p * self.per + f
+            self.copy(at).wait()
+
+            @pl.when(at + self.ahead < self.total)
+            def _():
+                self.copy(at + self.ahead).start()
+
+            start = pl.multiple_of(f * self.step, self.step)
+            whole = pl.ds(pl.multiple_of(self.first + start, self.step), self.step)
+            body(self.buf.at[at % self.slots], whole, pl.ds(start, self.step))
 
 
 def stream_scratch(depth, step, total):
@@ -100,7 +131,7 @@
     return (wanted == src).astype(F32).astype(BF)
 
 
-def adapter_kernel(n, orders, step, per, me_ref, a_ref, w_ref, b_ref, ad_ref, sq_ref, aperm, gram, buf, sem):
+def adapter_kernel(n, orders, step, per, me_ref, a_ref, w_ref, b_ref, keep_ref, send_ref, sq_ref, aperm, gram, buf, sem):
     rank = a_ref.shape[1]
     w_tile, wait = stream(w_ref, buf, sem, step, per, 0)
 
@@ -121,15 +152,16 @@
     wait()
     b = b_ref[0]
     aw = dot(aperm[...], w_tile[...])
-    both = dot(gram[...], jnp.concatenate([b, b, b], axis=0))
-    ad = aw + both[:rank]
-    ad_ref[0] = ad.astype(BF)
-    cross = (aw + ad) * both[rank:]
     squares = jnp.zeros((8, step), F32)
     slab = 64
     for i in range(w_tile.shape[0] // slab):
         w = w_tile[i * slab : (i + 1) * slab, :].astype(F32)
         squares = squares + jnp.sum((w * w).reshape(slab // 8, 8, step), axis=0)
+    both = dot(gram[...], jnp.concatenate([b, b, b], axis=0))
+    ad = aw + both[:rank]
+    keep_ref[0] = ad[: rank // 2].astype(BF)
+    send_ref[0] = ad[rank // 2 :].astype(BF)
+    cross = (aw + ad) * both[rank:]
     sq_ref[0] = jnp.sum(squares, axis=0, keepdims=True) + jnp.sum(cross, axis=0, keepdims=True)
 
 
@@ -147,11 +179,13 @@
             pl.BlockSpec((1, rank, tile), lambda p, f: (p, 0, f)),
         ],
         out_specs=[
-            pl.BlockSpec((1, rank, tile), lambda p, f: (p, 0, f)),
+            pl.BlockSpec((1, rank // 2, tile), lambda p, f: (p, 0, f)),
+            pl.BlockSpec((1, rank // 2, tile), lambda p, f: (p, 0, f)),
             pl.BlockSpec((1, 1, tile), lambda p, f: (p, 0, f)),
         ],
         out_shape=[
-            jax.ShapeDtypeStruct((2, rank, width), BF),
+            jax.ShapeDtypeStruct((2, rank // 2, width), BF),
+            jax.ShapeDtypeStruct((2, rank // 2, width), BF),
             jax.ShapeDtypeStruct((2, 1, width), F32),
         ],
         scratch_shapes=[pltpu.VMEM((rank, depth), BF), pltpu.VMEM((2 * rank, 3 * rank), BF)]
@@ -290,13 +324,14 @@
         keep_ref[p] = ag[:half].astype(BF)
         send_ref[p] = ag[half:].astype(BF)
         scaled = (b_ref[p].astype(F32) * coefs[p]).astype(BF)
-        ut_ref[p] += dot(d, scaled, ((1,), (1,)))
+        rank = scaled.shape[0]
+        ut_ref[:, p * rank : (p + 1) * rank] += dot(d, scaled, ((1,), (1,)))
 
 
 def own_call(n, orders, me, share, parts, xas, sq, mag, b, cot, prior, first, size):
     width = b.shape[2]
     rank = b.shape[1]
-    tile = tile_of(math.gcd(first, size), 1792)
+    tile = tile_of(math.gcd(first, size), 3584)
     start = first // tile
     y_args, y_specs = [], []
     for pair in parts:
@@ -332,14 +367,14 @@
             half_spec,
             half_spec,
             pl.BlockSpec((2, 1, tile), lambda f: (0, 0, f)),
-            pl.BlockSpec((2, share, rank), lambda f: (0, 0, 0)),
+            pl.BlockSpec((share, 2 * rank), lambda f: (0, 0)),
         ],
         out_shape=[
             jax.ShapeDtypeStruct((share, width), BF),
             half,
             half,
             jax.ShapeDtypeStruct((2, 1, size), F32),
-            jax.ShapeDtypeStruct((2, share, rank), F32),
+            jax.ShapeDtypeStruct((share, 2 * rank), F32),
         ],
         input_output_aliases=aliases,
         scratch_shapes=[pltpu.VMEM((2, share, rank), BF)],
@@ -351,48 +386,34 @@
     )(*args)
 
 
-def second_kernel(step, per, first, token_ref, w_ref, b_ref, a_ref, cd_ref, out_ref, acc, small, buf, sem):
-    w_tile, wait = stream(w_ref, buf, sem, step, per, first)
-    last = pl.num_programs(1) - 1
-
-    @pl.when(pl.program_id(1) == 0)
-    def _():
-        acc[...] = jnp.zeros_like(acc)
+def second_kernel(step, per, first, token_ref, w_ref, b_ref, a_ref, cd_ref, out_ref, small, buf, sem):
+    tiles = Stream(w_ref, buf, sem, step, per, first)
+    for p in range(2):
+        out_ref[p] = jnp.zeros(out_ref.shape[1:], F32)
         small[...] = jnp.zeros_like(small)
 
-    b = b_ref[0]
-    scaled = (b.astype(F32) * cd_ref[0]).astype(BF)
-    wait()
-    acc[...] += dot(scaled, w_tile[...], ((1,), (1,)))
-    small[...] += dot(scaled, b, ((1,), (1,)))
-
-    @pl.when(pl.program_id(1) == last)
-    def _():
-        total = acc[...]
-        for part in split3(small[...]):
-            total = total + dot(part, a_ref[0])
-        out_ref[0] = total
+        def body(w_tile, whole, _, p=p):
+            b = b_ref[p, :, whole]
+            scaled = (b.astype(F32) * cd_ref[p, :, whole]).astype(BF)
+            out_ref[p] += dot(scaled, w_tile[...], ((1,), (1,)))
+            small[...] += dot(scaled, b, ((1,), (1,)))
+
+        tiles.over(p, body)
+        parts = jnp.concatenate(split3(small[...]), axis=1)
+        out_ref[p] += dot(parts, jnp.concatenate([a_ref[p]] * 3, axis=0))
 
 
 def second_call(w, b, a, cd, first, size, token):
     _, depth, width = w.shape
     rank = b.shape[1]
     tile = tile_of(math.gcd(first, size), STEP)
-    start = first // tile
+    vmem = pl.BlockSpec(memory_space=pltpu.VMEM)
     return pl.pallas_call(
         functools.partial(second_kernel, tile, size // tile, first),
-        grid=(2, size // tile),
-        in_specs=[
-            pl.BlockSpec(memory_space=pltpu.SMEM),
-            pl.BlockSpec(memory_space=pl.ANY),
-            pl.BlockSpec((1, rank, tile), lambda p, f: (p, 0, f + start)),
-            pl.BlockSpec((1, rank, depth), lambda p, f: (p, 0, 0)),
-            pl.BlockSpec((1, 1, tile), lambda p, f: (p, 0, f)),
-        ],
-        out_specs=pl.BlockSpec((1, rank, depth), lambda p, f: (p, 0, 0)),
+        in_specs=[pl.BlockSpec(memory_space=pltpu.SMEM), pl.BlockSpec(memory_space=pl.ANY), vmem, vmem, vmem],
+        out_specs=vmem,
         out_shape=jax.ShapeDtypeStruct((2, rank, depth), F32),
-        scratch_shapes=[pltpu.VMEM((rank, depth), F32), pltpu.VMEM((rank, rank), F32)]
-        + stream_scratch(depth, tile, 2 * (size // tile)),
+        scratch_shapes=[pltpu.VMEM((rank, rank), F32)] + stream_scratch(depth, tile, 2 * (size // tile)),
         compiler_params=params(),
         cost_estimate=pl.CostEstimate(
             flops=4 * rank * depth * size, bytes_accessed=4 * depth * size, transcendentals=0
@@ -409,7 +430,7 @@
     rank = total.shape[0] // 2
     x = x_all[...]
     for p in range(2):
-        ut = ut_refs[0][p].astype(BF)
+        ut = ut_refs[0][:, p * rank : (p + 1) * rank].astype(BF)
         away = seconds[0][p]
         for second in seconds[1:]:
             away = away + second[p]
@@ -460,6 +481,43 @@
     )(me, *pieces)
 
 
+def fold_kernel(n, orders, *refs):
+    (ad_keep, ad_got, g_keep, g_got, sq_ref, stat_ref, mag_ref), outs = refs[:7], refs[7:]
+    cd_ref, blocks = outs[0], outs[1:]
+    rows = g_keep.shape[1] * 2 // n
+    totals = []
+    for p in range(2):
+        inverse = lax.rsqrt(sq_ref[p] + EPSILON)
+        coef = mag_ref[p] * inverse
+        cd = coef * stat_ref[p] * (inverse * inverse)
+        cd_ref[p] = cd
+        g = g_keep[p].astype(F32) + g_got[p].astype(F32)
+        ad = ad_keep[p].astype(F32) + ad_got[p].astype(F32)
+        totals.append(coef * g - cd * ad)
+    for i, j in enumerate(range(0, n, 2)):
+        at = [block_at(n, order).index(j) * rows for order in orders]
+        both = [totals[p][at[p] : at[p] + rows] for p in range(2)]
+        blocks[i][...] = jnp.concatenate(both, axis=0).astype(blocks[i].dtype)
+
+
+def fold_call(n, orders, ad_keep, ad_got, g_keep, g_got, sq, stat, mag):
+    _, half, width = ad_keep.shape
+    tile = tile_of(width, 1792)
+    rows = half * 4 // n
+    big = pl.BlockSpec((2, half, tile), lambda f: (0, 0, f))
+    line = pl.BlockSpec((2, 1, tile), lambda f: (0, 0, f))
+    return pl.pallas_call(
+        functools.partial(fold_kernel, n, orders),
+        grid=(width // tile,),
+        in_specs=[big] * 4 + [line] * 3,
+        out_specs=[line] + [pl.BlockSpec((rows, tile), lambda f: (0, f))] * (n // 2),
+        out_shape=[jax.ShapeDtypeStruct((2, 1, width), F32)]
+        + [jax.ShapeDtypeStruct((rows, width), F32 if j == 0 else BF) for j in range(n // 2)],
+        compiler_params=params(),
+        name="fold_rows",
+    )(ad_keep, ad_got, g_keep, g_got, sq, stat, mag)
+
+
 def order_kernel(n, orders, has_prior, me_ref, low_ref, high_ref, *refs):
     out_ref = refs[-1]
     rank = out_ref.shape[1]
@@ -471,7 +529,7 @@
 
 def order_call(n, orders, me, low, high, prior, first, width):
     _, half, size = low.shape
-    tile = tile_of(math.gcd(first, size), 1792)
+    tile = tile_of(math.gcd(first, size), 3584)
     start = first // tile
     args = [me, low, high]
     specs = [
@@ -552,80 +610,80 @@
         return [x if isinstance(x, tuple) else (x, x) for x in self.whole]
 
 
-class Doubling:
-    def __init__(self, bits, x, direct=False):
-        self.bits, self.x, self.step = [[bit] for bit in bits], x, 0
-        if direct:
-            self.bits = [bits[:1], list(range(2, 1 << len(bits), 2))]
+class Lanes:
+    def __init__(self, bits, squares, xa):
+        self.bits, self.squares, self.xa = bits, squares, xa
 
     def prepare(self):
-        return [self.x]
+        return [jnp.concatenate([self.squares, *self.xa.prepare()], axis=0)]
 
     def go(self, send):
-        self.x = send[0]
-        return [swap(send[0], "col", bit) for bit in self.bits[self.step]]
+        return [swap(send[0], "col", self.bits[self.xa.step])]
 
     def arrived(self, got):
-        self.x = self.x + sum(got)
-        self.step += 1
+        rows = self.squares.shape[0]
+        self.squares = self.squares + got[0][:rows]
+        self.xa.arrived([got[0][rows:]])
 
     def done(self):
-        return self.step == len(self.bits)
-
-
-class Scattering:
-    def __init__(self, orders, n, keep, send):
-        self.orders, self.keep, self.step = orders, keep, 0
-        self.send, self.n = send, n
+        return self.xa.done()
+
+
+class Statistic:
+    def __init__(self, n, stat, u):
+        self.n, self.stat, self.u, self.step = n, stat, u, 0
 
     def prepare(self):
-        if self.step == 0:
-            return [self.send]
-        self.sum = self.keep.astype(F32) + self.first.astype(F32)
-        rows = self.sum.shape[1] * 2 // self.n
-        out = []
-        for j in range(2, self.n, 2):
-            at = [block_at(self.n, order).index(j) * rows for order in self.orders]
-            both = [self.sum[p, at[p] : at[p] + rows] for p in range(2)]
-            out.append(jnp.concatenate(both, axis=0).astype(BF))
-        self.rows = rows
-        return out
+        both = jnp.concatenate([self.stat, self.u], axis=0)
+        return [both.astype(BF) if self.step else both]
 
     def go(self, send):
-        if self.step == 0:
-            return [swap(send[0], "col", 1)]
-        return [swap(x, "col", j) for x, j in zip(send, range(2, self.n, 2))]
+        return [swap(send[0], "col", j) for j in ([1], range(2, self.n, 2))[self.step]]
 
     def arrived(self, got):
-        if self.step == 0:
-            self.first = got[0]
-        else:
-            rows = self.rows
-            total = sum(x.astype(F32) for x in got)
-            self.own = [(self.sum[p, :rows] + total[p * rows : (p + 1) * rows]).astype(BF) for p in range(2)]
+        rows = self.stat.shape[0]
+        self.stat = self.stat + sum(x[:rows].astype(F32) for x in got)
+        self.u = jnp.concatenate([self.u] + [x[rows:].astype(F32) for x in got], axis=0)
         self.step += 1
 
     def done(self):
         return self.step == 2
 
 
-class Collecting:
-    def __init__(self, bits, x):
-        self.bits, self.x, self.step = bits, x, 0
+class First:
+    def __init__(self, send):
+        self.send, self.got = send, None
 
     def prepare(self):
-        return [self.x]
+        return [self.send]
 
     def go(self, send):
-        self.x = send[0]
-        return [swap(send[0], "col", self.bits[self.step])]
+        return [swap(send[0], "col", 1)]
 
     def arrived(self, got):
-        self.x = jnp.concatenate([self.x, got[0]], axis=1)
-        self.step += 1
+        self.got = got[0]
 
     def done(self):
-        return self.step == len(self.bits)
+        return self.got is not None
+
+
+class Scattering:
+    def __init__(self, n, blocks):
+        self.n, self.blocks, self.own = n, blocks, None
+
+    def prepare(self):
+        return self.blocks[1:]
+
+    def go(self, send):
+        return [swap(x, "col", j) for x, j in zip(send, range(2, self.n, 2))]
+
+    def arrived(self, got):
+        total = sum(x.astype(F32) for x in [self.blocks[0], *got])
+        rows = total.shape[0] // 2
+        self.own = [total[p * rows : (p + 1) * rows].astype(BF) for p in range(2)]
+
+    def done(self):
+        return self.own is not None
 
 
 class Laying:
@@ -669,14 +727,20 @@
         return self.got is not None
 
 
-def phase(turn, moves, kernel=None):
+def phase(turn, moves, kernel=None, late=(), ready=()):
     moves = [move for move in moves if not move.done()]
-    sends = [move.prepare() for move in moves]
+    late = [move for move in late if not move.done()]
+    ready = [move for move in ready if not move.done()]
+    sends = [move.prepare() for move in moves + late]
     sent = list(turn.pass_on(*[x for send in sends for x in send]))
-    got = [move.go([sent.pop(0) for _ in send]) for move, send in zip(moves, sends)]
+    got = [move.go([sent.pop(0) for _ in send]) for move, send in zip(moves + late, sends)]
+    for move, g in zip(late, got[len(moves) :]):
+        move.pending = g
+    waited = moves + ready
+    got = got[: len(moves)] + [move.pending for move in ready]
     outs = kernel(turn.token) if kernel else ()
     flat = list(turn.pass_on(*[x for g in got for x in g], *outs))
-    for move, g in zip(moves, got):
+    for move, g in zip(waited, got):
         move.arrived([flat.pop(0) for _ in g])
     return flat
 
@@ -696,10 +760,10 @@
     count = len(sizes)
 
     xs = [tokens] + [swap(tokens, "row", k) for k in range(1, n_row)]
-    ad, sq = adapter_call(n, orders, me, adapter_in, weights, adapter_out)
+    ad_keep, ad_send, sq = adapter_call(n, orders, me, adapter_in, weights, adapter_out)
     turn = Turn(me)
-    *xs, sq = turn.pass_on(*xs, sq)
-    squares = Doubling(bits, sq)
+    *xs, sq, ad_send = turn.pass_on(*xs, sq, ad_send)
+    sq_first, ad_first = First(sq.reshape(-1, 128)), First(ad_send)
 
     def project(c):
         return lambda token: token_call(
@@ -708,55 +772,42 @@
 
     def elementwise(c):
         return lambda token: own_call(
-            n, orders, token, share, halvings[c].pairs(), [x[0] for x in xa.parts], squares.x, mag, adapter_out,
+            n, orders, token, share, halvings[c].pairs(), [x[0] for x in xa.parts], squares, mag, adapter_out,
             hidden_cot, hidden, firsts[c], sizes[c],
         )
 
-    def second(c):
-        first, size = firsts[c], sizes[c]
-        return lambda token: [
-            second_call(weights, adapter_out, adapter_in, cd[:, :, first : first + size], first, size, token)
-        ]
-
-    outs = phase(turn, [squares], project(0))
+    outs = phase(turn, [sq_first, ad_first], project(0))
     halvings = [Halving(orders, outs[0], outs[1])]
     xa = Halving(orders, outs[2], outs[3], F32)
-    moves = [squares, xa, halvings[0]]
-    phase(turn, moves)
+    phase(turn, [xa, halvings[0]])
+    lanes = Lanes(bits, sq_first.send + sq_first.got, xa)
     for c in range(1, count):
-        outs = phase(turn, moves, project(c))
+        outs = phase(turn, [lanes, halvings[c - 1]], project(c))
         halvings.append(Halving(orders, outs[0], outs[1]))
-        moves.append(halvings[-1])
-        phase(turn, moves)
+        phase(turn, [lanes, *halvings])
     hidden, results = None, []
     for c in range(count):
-        while not (halvings[c].done() and squares.done() and xa.done()):
-            phase(turn, moves)
-        hidden, *outs = phase(turn, moves, elementwise(c))
+        while not (lanes.done() and halvings[c].done()):
+            phase(turn, [lanes, halvings[c]])
+        squares = lanes.squares.reshape(2, 1, -1)
+        hidden, *outs = phase(turn, halvings[c + 1 : c + 2], elementwise(c))
         results.append(outs)
-    stats = Doubling(bits, jnp.concatenate([r[2] for r in results], axis=2), direct=True)
-    uts = Collecting(bits, sum(r[3] for r in results))
-    while not stats.done():
-        phase(turn, [stats, uts])
-
-    norm = jnp.sqrt(squares.x + EPSILON)
-    coef = mag / norm
-    cd = coef * stats.x / (norm * norm)
-    half = rank // 2
-    folded = []
-    for i in range(2):
-        g = jnp.concatenate([r[i] for r in results], axis=2).astype(F32)
-        folded.append((coef * g - cd * ad[:, i * half : (i + 1) * half].astype(F32)).astype(BF))
-    turning = Scattering(orders, n, *folded)
-    while not uts.done():
-        phase(turn, [turning, uts])
+    g_keep, g_send = [jnp.concatenate([r[i] for r in results], axis=2) for i in range(2)]
+    g_first = First(g_send)
+    stat = jnp.concatenate([r[2] for r in results], axis=2).reshape(-1, 128)
+    statistic = Statistic(n, stat, sum(r[3] for r in results))
+    phase(turn, [statistic, g_first])
+    phase(turn, [statistic])
+    stat = statistic.stat.reshape(2, 1, -1)
+    cd, *blocks = fold_call(n, orders, ad_keep, ad_first.got, g_keep, g_first.got, squares, stat, mag)
+    scattering = Scattering(n, blocks)
     seconds = phase(
         turn,
-        [turning],
+        [scattering],
         lambda token: [second_call(weights, adapter_out, adapter_in, cd, 0, width, token)],
     )
-    laying = Laying(orders, turning.own)
-    pieces = turn.pass_on(*join_call(share, bits[::-1], turn.token, xs, seconds, [uts.x]))
+    laying = Laying(orders, scattering.own)
+    pieces = turn.pass_on(*join_call(share, bits[::-1], turn.token, xs, seconds, [statistic.u]))
     away = Around(n_row, pieces[1:])
     phase(turn, [laying, away])
     total = (pieces[0] + sum(x.astype(F32) for x in away.got)).astype(BF)
@@ -764,10 +815,10 @@
     while laying.step or not back.done():
         phase(turn, [laying, back])
     (grad_in,) = phase(turn, [laying], lambda token: [lay_call(token, [total] + back.got)])
+    low, high = laying.held
+    grad_out = order_call(n, orders, turn.token, low, high, None, 0, width)
     grad_in = grad_in.reshape(2, -1, grad_in.shape[1])
-    low, high = laying.held
-    grad_out = order_call(n, orders, me, low, high, None, 0, width)
-    grad_mag = (stats.x / norm)[:, 0, :]
+    grad_mag = (stat / jnp.sqrt(squares + EPSILON))[:, 0, :]
     return (hidden, grad_in, grad_out, grad_mag)
 
 

time: 147 us -> 140 us (0.952)
  waiting for transfers between devices: 40.8 us -> 37.2 us
    ppermute x41 -> x37, waiting for transfers between devices: 40.8 us -> 37.2 us  [swap(): return lax.ppermute(x, axis, [(i, i ^ bit) for i in range(n)])]
    ppermute x41 -> x37, starting transfers between devices: 41.9 us -> 40.9 us  [swap(): return lax.ppermute(x, axis, [(i, i ^ bit) for i in range(n)])]
  transfers between devices with their start and end apart: 41 -> 37, of which waited for: 16 -> 15; matrix products, arithmetic and copies ran while one was open for 1% -> 1% of each run, Pallas kernels for 35% -> 36%
where the time goes in v3:
time: 140 us
  Pallas kernels  57.8 us (41%)
  starting transfers between devices  40.9 us (29%)
  waiting for transfers between devices  37.2 us (27%)
  other arithmetic  2.08 us (1%)
    ppermute x37, starting transfers between devices, swap(): return lax.ppermute(x, axis, [(i, i ^ bit) for i in range(n)])  40.9 us
    ppermute x37, waiting for transfers between devices, swap(): return lax.ppermute(x, axis, [(i, i ^ bit) for i in range(n)])  37.2 us
    pallas_call x2, Pallas kernels, token_call(): pl.pallas_call(functools.partial(token_kernel, n, share, orders, len(xs),...  18.4 us
    pallas_call x1, Pallas kernels, second_call(): pl.pallas_call(functools.partial(second_kernel, tile, size // tile, first...  13.6 us
    pallas_call x1, Pallas kernels, adapter_call(): pl.pallas_call(functools.partial(adapter_kernel, n, orders, tile, width /...  13.5 us
    pallas_call x2, Pallas kernels, own_call(): pl.pallas_call(functools.partial(own_kernel, n, orders, len(parts), len(x...  6 us
    pallas_call x1, Pallas kernels, order_call(): pl.pallas_call(functools.partial(order_kernel, n, orders, prior is not No...  2.83 us
  transfers between devices with their start and end apart: 37, of which 15 were waited for; matrix products, arithmetic and copies ran while one was open for 1% of the time, Pallas kernels for 36%

profile of v3, /device:TPU:0, one launch (start us, length us, event | category | flops | bytes accessed | tf_op | source)
XLA Modules:
  0.0 139.8 jit_solution(16593539083467437864)
XLA Ops:
  0.6 4.1 %collective-permute-start.1 = (bf16[64,1024]{1,0:T(8,128)(2,1)}, bf16[64,1024]{1,0:T(8,128)(2,1)S(1)}, u32[]{:S(2)}, u32[]{:S(2)}) collective-permute-start(bf16[64,1024]{1,0:T(8,128)(2,1)} %refs_0_.2), channel_id=1, source_target_pairs={{0,16},{8,24},{16,0},{24,8},{1,17},{9,25},{17,1},{25,9},{2,18},{10... | collective-permute-start | bytes 393224 | tf_op jit(solution)/shard_map/ppermute | solution.py:40
  4.7 1.6 %collective-permute-start = (bf16[64,1024]{1,0:T(8,128)(2,1)}, bf16[64,1024]{1,0:T(8,128)(2,1)S(1)}, u32[]{:S(2)}, u32[]{:S(2)}) collective-permute-start(bf16[64,1024]{1,0:T(8,128)(2,1)} %refs_0_.2), channel_id=1, source_target_pairs={{0,8},{8,0},{16,24},{24,16},{1,9},{9,1},{17,25},{25,17},{2,10},{10... | collective-permute-start | bytes 393224 | tf_op jit(solution)/shard_map/ppermute | solution.py:40
  6.9 13.5 %adapter_pass.1 = (bf16[2,32,7168]{2,1,0:T(8,128)(2,1)}, bf16[2,32,7168]{2,1,0:T(8,128)(2,1)}, f32[2,1,7168]{2,1,0:T(1,128)}) custom-call(s32[2]{0:T(128)} %pad_add_fusion.me_ref.token_ref, bf16[2,64,1024]{2,1,0:T(8,128)(2,1)} %a_ref.3, bf16[2,1024,7168]{2,1,0:T(8,128)(2,1)} %w_ref.3, bf16[2,64,7168]{2,1,0:T(8,128)(2,1)} %b_ref.3), custom_call_target="tpu_custom_call" | custom-call | flops 3758096384 | bytes 29360128 | tf_op jit(solution)/shard_map/adapter_pass/pallas_call | solution.py:172
  21.1 9.2 %token_pass.2 = (bf16[2,128,3584]{2,1,0:T(8,128)(2,1)S(1)}, bf16[2,128,3584]{2,1,0:T(8,128)(2,1)S(1)}, f32[128,128]{1,0:T(8,128)S(1)}, f32[128,128]{1,0:T(8,128)S(1)}) custom-call(s32[2]{0:T(128)S(1)} %copy-done.5, bf16[64,1024]{1,0:T(8,128)(2,1)S(1)} %copy-done.3, bf16[64,1024]{1,0:T(8,128)(2,1)S(1)} %collective-permute-done.refs_1_, ...), custom_call_target="tpu_custom_call" | custom-call | flops 3758096384 | bytes 14680064 | tf_op jit(solution)/shard_map/token_pass/pallas_call | solution.py:261
  30.9 3.4 %collective-permute-done.5.refs_9_ = f32[128,128]{1,0:T(8,128)S(1)} collective-permute-done((f32[128,128]{1,0:T(8,128)S(1)}, f32[128,128]{1,0:T(8,128)S(1)}, u32[]{:S(2)}, u32[]{:S(2)}) %collective-permute-start.5) | collective-permute-done | bytes 65568 | tf_op jit(solution)/shard_map/ppermute | solution.py:40
  34.5 1.8 %collective-permute-start.8 = (bf16[64,3584]{1,0:T(8,128)(2,1)S(1)}, bf16[64,3584]{1,0:T(8,128)(2,1)S(1)}, u32[]{:S(2)}, u32[]{:S(2)}) collective-permute-start(bf16[64,3584]{1,0:T(8,128)(2,1)S(1)} %get-tuple-element.183), channel_id=1, source_target_pairs={{0,2},{1,3},{2,0},{3,1},{4,6},{5,7},{6,4},{7,5},{8,10},{9,11},{10,... | collective-permute-start | bytes 1376264 | tf_op jit(solution)/shard_map/ppermute | solution.py:40
  36.3 1.5 %collective-permute-start.9 = (bf16[64,3584]{1,0:T(8,128)(2,1)S(1)}, bf16[64,3584]{1,0:T(8,128)(2,1)S(1)}, u32[]{:S(2)}, u32[]{:S(2)}) collective-permute-start(bf16[64,3584]{1,0:T(8,128)(2,1)S(1)} %get-tuple-element.184), channel_id=1, source_target_pairs={{0,4},{1,5},{2,6},{3,7},{4,0},{5,1},{6,2},{7,3},{8,12},{9,13},{10,... | collective-permute-start | bytes 1376264 | tf_op jit(solution)/shard_map/ppermute | solution.py:40
  38.4 9.2 %token_pass.3 = (bf16[2,128,3584]{2,1,0:T(8,128)(2,1)S(1)}, bf16[2,128,3584]{2,1,0:T(8,128)(2,1)S(1)}) custom-call(s32[2]{0:T(128)S(1)} %copy-done.5, bf16[64,1024]{1,0:T(8,128)(2,1)S(1)} %copy-done.3, bf16[64,1024]{1,0:T(8,128)(2,1)S(1)} %collective-permute-done.refs_1_, bf16[64,1024]{1,0:T(8,128)(2,1)S(1)} %collective-permute-done.1.refs_2_, ...), custom_call_target="tpu_custom_call" | custom-call | flops 3758096384 | bytes 14680064 | tf_op jit(solution)/shard_map/token_pass/pallas_call | solution.py:261
  47.6 1.5 %collective-permute-done.7 = f32[176,128]{1,0:T(8,128)S(1)} collective-permute-done((f32[176,128]{1,0:T(8,128)S(1)}, f32[176,128]{1,0:T(8,128)S(1)}, u32[]{:S(2)}, u32[]{:S(2)}) %collective-permute-start.7) | collective-permute-done | bytes 90144 | tf_op jit(solution)/shard_map/ppermute | solution.py:40
  49.4 1.8 %collective-permute-start.11 = (bf16[32,3584]{1,0:T(8,128)(2,1)S(1)}, bf16[32,3584]{1,0:T(8,128)(2,1)S(1)}, u32[]{:S(2)}, u32[]{:S(2)}) collective-permute-start(bf16[32,3584]{1,0:T(8,128)(2,1)S(1)} %get-tuple-element.194), channel_id=1, source_target_pairs={{0,4},{1,5},{2,6},{3,7},{4,0},{5,1},{6,2},{7,3},{8,12},{9,13},{10,... | collective-permute-start | bytes 688136 | tf_op jit(solution)/shard_map/ppermute | solution.py:40
  53.2 5.8 %collective-permute-done.10 = f32[144,128]{1,0:T(8,128)S(1)} collective-permute-done((f32[144,128]{1,0:T(8,128)S(1)}, f32[144,128]{1,0:T(8,128)S(1)}, u32[]{:S(2)}, u32[]{:S(2)}) %collective-permute-start.10) | collective-permute-done | bytes 73760 | tf_op jit(solution)/shard_map/ppermute | solution.py:40
  59.3 1.8 %collective-permute-start.14 = (bf16[64,3584]{1,0:T(8,128)(2,1)S(1)}, bf16[64,3584]{1,0:T(8,128)(2,1)S(1)}, u32[]{:S(2)}, u32[]{:S(2)}) collective-permute-start(bf16[64,3584]{1,0:T(8,128)(2,1)S(1)} %get-tuple-element.201), channel_id=1, source_target_pairs={{0,2},{1,3},{2,0},{3,1},{4,6},{5,7},{6,4},{7,5},{8,10},{9,11},{10,... | collective-permute-start | bytes 1376264 | tf_op jit(solution)/shard_map/ppermute | solution.py:40
  61.1 1.5 %collective-permute-start.15 = (bf16[64,3584]{1,0:T(8,128)(2,1)S(1)}, bf16[64,3584]{1,0:T(8,128)(2,1)S(1)}, u32[]{:S(2)}, u32[]{:S(2)}) collective-permute-start(bf16[64,3584]{1,0:T(8,128)(2,1)S(1)} %get-tuple-element.202), channel_id=1, source_target_pairs={{0,4},{1,5},{2,6},{3,7},{4,0},{5,1},{6,2},{7,3},{8,12},{9,13},{10,... | collective-permute-start | bytes 1376264 | tf_op jit(solution)/shard_map/ppermute | solution.py:40
  62.7 3.2 %own_tokens.2 = (bf16[32,7168]{1,0:T(8,128)(2,1)}, bf16[2,32,3584]{2,1,0:T(8,128)(2,1)S(1)}, bf16[2,32,3584]{2,1,0:T(8,128)(2,1)S(1)}, f32[2,1,3584]{2,1,0:T(1,128)S(1)}, f32[32,128]{1,0:T(8,128)S(1)}) custom-call(s32[2]{0:T(128)S(1)} %copy-done.5, bf16[2,128,3584]{2,1,0:T(8,128)(2,1)S(1)} %get-tuple-element.179.refs_0_.refs_1_, ...), custom_call_target="tpu_custom_call" | custom-call | flops 58720256 | bytes 2293760 | tf_op jit(solution)/shard_map/own_tokens/pallas_call | solution.py:361
  65.9 5.6 %collective-permute-done.14.refs_4_ = bf16[64,3584]{1,0:T(8,128)(2,1)S(1)} collective-permute-done((bf16[64,3584]{1,0:T(8,128)(2,1)S(1)}, bf16[64,3584]{1,0:T(8,128)(2,1)S(1)}, u32[]{:S(2)}, u32[]{:S(2)}) %collective-permute-start.14) | collective-permute-done | bytes 458784 | tf_op jit(solution)/shard_map/ppermute | solution.py:40
  73.0 1.6 %collective-permute-start.16 = (bf16[32,3584]{1,0:T(8,128)(2,1)S(1)}, bf16[32,3584]{1,0:T(8,128)(2,1)S(1)}, u32[]{:S(2)}, u32[]{:S(2)}) collective-permute-start(bf16[32,3584]{1,0:T(8,128)(2,1)S(1)} %get-tuple-element.215), channel_id=1, source_target_pairs={{0,4},{1,5},{2,6},{3,7},{4,0},{5,1},{6,2},{7,3},{8,12},{9,13},{10,... | collective-permute-start | bytes 688136 | tf_op jit(solution)/shard_map/ppermute | solution.py:40
  75.2 4.0 %collective-permute-done.16.refs_6_ = bf16[32,3584]{1,0:T(8,128)(2,1)S(1)} collective-permute-done((bf16[32,3584]{1,0:T(8,128)(2,1)S(1)}, bf16[32,3584]{1,0:T(8,128)(2,1)S(1)}, u32[]{:S(2)}, u32[]{:S(2)}) %collective-permute-start.16) | collective-permute-done | bytes 229408 | tf_op jit(solution)/shard_map/ppermute | solution.py:40
  79.1 1.5 %collective-permute-done.17.refs_7_ = bf16[32,3584]{1,0:T(8,128)(2,1)S(1)} collective-permute-done((bf16[32,3584]{1,0:T(8,128)(2,1)S(1)}, bf16[32,3584]{1,0:T(8,128)(2,1)S(1)}, u32[]{:S(2)}, u32[]{:S(2)}) %collective-permute-start.17) | collective-permute-done | bytes 229408 | tf_op jit(solution)/shard_map/ppermute | solution.py:40
  80.7 2.8 %own_tokens.3 = (bf16[32,7168]{1,0:T(8,128)(2,1)}, bf16[2,32,3584]{2,1,0:T(8,128)(2,1)S(1)}, bf16[2,32,3584]{2,1,0:T(8,128)(2,1)S(1)}, f32[2,1,3584]{2,1,0:T(1,128)S(1)}, f32[32,128]{1,0:T(8,128)S(1)}) custom-call(s32[2]{0:T(128)S(1)} %copy-done.5, bf16[2,128,3584]{2,1,0:T(8,128)(2,1)S(1)} %get-tuple-element.198.refs_0_.refs_1_, ...), custom_call_target="tpu_custom_call", output_to_operand_aliasing={{0}: (17, {})} | custom-call | flops 58720256 | bytes 2293760 | tf_op jit(solution)/shard_map/own_tokens/pallas_call | solution.py:361
  84.3 2.1 %collective-permute-done.18 = f32[144,128]{1,0:T(8,128)S(1)} collective-permute-done((f32[144,128]{1,0:T(8,128)S(1)}, f32[144,128]{1,0:T(8,128)S(1)}, u32[]{:S(2)}, u32[]{:S(2)}) %collective-permute-start.18) | collective-permute-done | bytes 73760 | tf_op jit(solution)/shard_map/ppermute | solution.py:40
  86.7 1.7 %collective-permute-start.21 = (bf16[176,128]{1,0:T(8,128)(2,1)S(1)}, bf16[176,128]{1,0:T(8,128)(2,1)S(1)}, u32[]{:S(2)}, u32[]{:S(2)}) collective-permute-start(bf16[176,128]{1,0:T(8,128)(2,1)S(1)} %pad_maximum_fusion.9), channel_id=1, source_target_pairs={{0,4},{1,5},{2,6},{3,7},{4,0},{5,1},{6,2},{7,3},{8,12},{9,13},{10,... | collective-permute-start | bytes 135176 | tf_op jit(solution)/shard_map/ppermute | solution.py:40
  89.9 1.6 %collective-permute-done.22 = bf16[176,128]{1,0:T(8,128)(2,1)S(1)} collective-permute-done((bf16[176,128]{1,0:T(8,128)(2,1)S(1)}, bf16[176,128]{1,0:T(8,128)(2,1)S(1)}, u32[]{:S(2)}, u32[]{:S(2)}) %collective-permute-start.22) | collective-permute-done | bytes 45088 | tf_op jit(solution)/shard_map/ppermute | solution.py:40
  93.7 1.6 %collective-permute-start.23 = (bf16[16,7168]{1,0:T(8,128)(2,1)S(1)}, bf16[16,7168]{1,0:T(8,128)(2,1)S(1)}, u32[]{:S(2)}, u32[]{:S(2)}) collective-permute-start(bf16[16,7168]{1,0:T(8,128)(2,1)S(1)} %get-tuple-element.254), channel_id=1, source_target_pairs={{0,2},{1,3},{2,0},{3,1},{4,6},{5,7},{6,4},{7,5},{8,10},{9,11},{10,... | collective-permute-start | bytes 688136 | tf_op jit(solution)/shard_map/ppermute | solution.py:40
  97.3 13.6 %second_pass.1.refs_4_ = f32[2,64,1024]{2,1,0:T(8,128)S(1)} custom-call(s32[2]{0:T(128)S(1)} %copy-done.5, bf16[2,1024,7168]{2,1,0:T(8,128)(2,1)} %w_ref.3, bf16[2,64,7168]{2,1,0:T(8,128)(2,1)S(1)} %copy-done, bf16[2,64,1024]{2,1,0:T(8,128)(2,1)S(1)} %copy-done.1, f32[2,1,7168]{2,1,0:T(1,128)S(1)} %get-tuple-element.257.cd_ref), custom_call_target="tpu_custom_call" | custom-call | flops 1879048192 | bytes 29360128 | tf_op jit(solution)/shard_map/second_pass/pallas_call | solution.py:411
  112.3 1.7 %collective-permute-start.27 = (bf16[8,7168]{1,0:T(8,128)(2,1)S(1)}, bf16[8,7168]{1,0:T(8,128)(2,1)S(1)}, u32[]{:S(2)}, u32[]{:S(2)}) collective-permute-start(bf16[8,7168]{1,0:T(8,128)(2,1)S(1)} %get-tuple-element.274), channel_id=1, source_target_pairs={{0,2},{1,3},{2,0},{3,1},{4,6},{5,7},{6,4},{7,5},{8,10},{9,11},{10,... | collective-permute-start | bytes 344072 | tf_op jit(solution)/shard_map/ppermute | solution.py:40
  114.7 3.5 %collective-permute-start.29 = (bf16[32,1024]{1,0:T(8,128)(2,1)S(1)}, bf16[32,1024]{1,0:T(8,128)(2,1)S(1)}, u32[]{:S(2)}, u32[]{:S(2)}) collective-permute-start(bf16[32,1024]{1,0:T(8,128)(2,1)S(1)} %get-tuple-element.276), channel_id=1, source_target_pairs={{0,16},{8,24},{16,0},{24,8},{1,17},{9,25},{17,1},{25,9},{2,18},{10... | collective-permute-start | bytes 196616 | tf_op jit(solution)/shard_map/ppermute | solution.py:40
  118.4 3.1 %collective-permute-done.29 = bf16[32,1024]{1,0:T(8,128)(2,1)S(1)} collective-permute-done((bf16[32,1024]{1,0:T(8,128)(2,1)S(1)}, bf16[32,1024]{1,0:T(8,128)(2,1)S(1)}, u32[]{:S(2)}, u32[]{:S(2)}) %collective-permute-start.29) | collective-permute-done | bytes 65568 | tf_op jit(solution)/shard_map/ppermute | solution.py:40
  121.5 2.9 %collective-permute-done.30 = bf16[32,1024]{1,0:T(8,128)(2,1)S(1)} collective-permute-done((bf16[32,1024]{1,0:T(8,128)(2,1)S(1)}, bf16[32,1024]{1,0:T(8,128)(2,1)S(1)}, u32[]{:S(2)}, u32[]{:S(2)}) %collective-permute-start.30) | collective-permute-done | bytes 65568 | tf_op jit(solution)/shard_map/ppermute | solution.py:40
  124.9 1.9 %collective-permute-start.32 = (bf16[16,7168]{1,0:T(8,128)(2,1)S(1)}, bf16[16,7168]{1,0:T(8,128)(2,1)S(1)}, u32[]{:S(2)}, u32[]{:S(2)}) collective-permute-start(bf16[16,7168]{1,0:T(8,128)(2,1)S(1)} %pad_maximum_fusion.4), channel_id=1, source_target_pairs={{0,4},{1,5},{2,6},{3,7},{4,0},{5,1},{6,2},{7,3},{8,12},{9,13},{10,... | collective-permute-start | bytes 688136 | tf_op jit(solution)/shard_map/ppermute | solution.py:40
  127.7 3.5 %collective-permute-start.35 = (bf16[32,1024]{1,0:T(8,128)(2,1)S(1)}, bf16[32,1024]{1,0:T(8,128)(2,1)S(1)}, u32[]{:S(2)}, u32[]{:S(2)}) collective-permute-start(bf16[32,1024]{1,0:T(8,128)(2,1)S(1)} %add_convert_fusion.5.refs_0_), channel_id=1, source_target_pairs={{0,24},{8,16},{16,8},{24,0},{1,25},{9,17},{17,9},{25,1},{2,26},{10... | collective-permute-start | bytes 196616 | tf_op jit(solution)/shard_map/ppermute | solution.py:40
  132.1 2.2 %collective-permute-done.35.refs_3_ = bf16[32,1024]{1,0:T(8,128)(2,1)S(1)} collective-permute-done((bf16[32,1024]{1,0:T(8,128)(2,1)S(1)}, bf16[32,1024]{1,0:T(8,128)(2,1)S(1)}, u32[]{:S(2)}, u32[]{:S(2)}) %collective-permute-start.35) | collective-permute-done | bytes 65568 | tf_op jit(solution)/shard_map/ppermute | solution.py:40
  136.9 2.8 %order_rows.1 = f32[2,64,7168]{2,1,0:T(8,128)} custom-call(s32[2]{0:T(128)S(1)} %copy-done.5, bf16[2,32,7168]{2,1,0:T(8,128)(2,1)S(1)} %pad_maximum_fusion.2.low_ref, bf16[2,32,7168]{2,1,0:T(8,128)(2,1)S(1)} %collective-permute-done.36.high_ref), custom_call_target="tpu_custom_call" | custom-call | tf_op jit(solution)/shard_map/order_rows/pallas_call | solution.py:545
  (109 shorter events, 21.3 us)
Async XLA Ops:
  0.6 19.8 %collective-permute-start.1 = (bf16[64,1024]{1,0:T(8,128)(2,1)}, bf16[64,1024]{1,0:T(8,128)(2,1)S(1)}, u32[]{:S(2)}, u32[]{:S(2)}) collective-permute-start(bf16[64,1024]{1,0:T(8,128)(2,1)} %refs_0_.2), channel_id=1, source_target_pairs={{0,16},{8,24},{16,0},{24,8},{1,17},{9,25},{17,1},{25,9},{2,18},{10... | collective-permute-start | bytes 393224 | tf_op jit(solution)/shard_map/ppermute | solution.py:40
  4.7 15.7 %collective-permute-start = (bf16[64,1024]{1,0:T(8,128)(2,1)}, bf16[64,1024]{1,0:T(8,128)(2,1)S(1)}, u32[]{:S(2)}, u32[]{:S(2)}) collective-permute-start(bf16[64,1024]{1,0:T(8,128)(2,1)} %refs_0_.2), channel_id=1, source_target_pairs={{0,8},{8,0},{16,24},{24,16},{1,9},{9,1},{17,25},{25,17},{2,10},{10... | collective-permute-start | bytes 393224 | tf_op jit(solution)/shard_map/ppermute | solution.py:40
  6.3 14.2 %collective-permute-start.2 = (bf16[64,1024]{1,0:T(8,128)(2,1)}, bf16[64,1024]{1,0:T(8,128)(2,1)S(1)}, u32[]{:S(2)}, u32[]{:S(2)}) collective-permute-start(bf16[64,1024]{1,0:T(8,128)(2,1)} %refs_0_.2), channel_id=1, source_target_pairs={{0,24},{8,16},{16,8},{24,0},{1,25},{9,17},{17,9},{25,1},{2,26},{10... | collective-permute-start | bytes 393224 | tf_op jit(solution)/shard_map/ppermute | solution.py:40
  20.5 9.8 %collective-permute-start.4 = (bf16[2,32,7168]{2,1,0:T(8,128)(2,1)}, bf16[2,32,7168]{2,1,0:T(8,128)(2,1)S(1)}, u32[]{:S(2)}, u32[]{:S(2)}) collective-permute-start(bf16[2,32,7168]{2,1,0:T(8,128)(2,1)} %get-tuple-element.160), channel_id=1, source_target_pairs={{0,1},{1,0},{2,3},{3,2},{4,5},{5,4},{6,7},{7,6},{8,9},{9,8},{10,11... | collective-permute-start | bytes 2752520 | tf_op jit(solution)/shard_map/ppermute | solution.py:40
  20.6 9.7 %collective-permute-start.3 = (f32[112,128]{1,0:T(8,128)}, f32[112,128]{1,0:T(8,128)S(1)}, u32[]{:S(2)}, u32[]{:S(2)}) collective-permute-start(f32[112,128]{1,0:T(8,128)} %bitcast.43), channel_id=1, source_target_pairs={{0,1},{1,0},{2,3},{3,2},{4,5},{5,4},{6,7},{7,6},{8,9},{9,8},{10,11... | collective-permute-start | bytes 172040 | tf_op jit(solution)/shard_map/ppermute | solution.py:40
  34.5 14.6 %collective-permute-start.8 = (bf16[64,3584]{1,0:T(8,128)(2,1)S(1)}, bf16[64,3584]{1,0:T(8,128)(2,1)S(1)}, u32[]{:S(2)}, u32[]{:S(2)}) collective-permute-start(bf16[64,3584]{1,0:T(8,128)(2,1)S(1)} %get-tuple-element.183), channel_id=1, source_target_pairs={{0,2},{1,3},{2,0},{3,1},{4,6},{5,7},{6,4},{7,5},{8,10},{9,11},{10,... | collective-permute-start | bytes 1376264 | tf_op jit(solution)/shard_map/ppermute | solution.py:40
  36.3 12.8 %collective-permute-start.9 = (bf16[64,3584]{1,0:T(8,128)(2,1)S(1)}, bf16[64,3584]{1,0:T(8,128)(2,1)S(1)}, u32[]{:S(2)}, u32[]{:S(2)}) collective-permute-start(bf16[64,3584]{1,0:T(8,128)(2,1)S(1)} %get-tuple-element.184), channel_id=1, source_target_pairs={{0,4},{1,5},{2,6},{3,7},{4,0},{5,1},{6,2},{7,3},{8,12},{9,13},{10,... | collective-permute-start | bytes 1376264 | tf_op jit(solution)/shard_map/ppermute | solution.py:40
  37.8 11.3 %collective-permute-start.7 = (f32[176,128]{1,0:T(8,128)S(1)}, f32[176,128]{1,0:T(8,128)S(1)}, u32[]{:S(2)}, u32[]{:S(2)}) collective-permute-start(f32[176,128]{1,0:T(8,128)S(1)} %pad_maximum_fusion.5), channel_id=1, source_target_pairs={{0,2},{1,3},{2,0},{3,1},{4,6},{5,7},{6,4},{7,5},{8,10},{9,11},{10,... | collective-permute-start | bytes 270344 | tf_op jit(solution)/shard_map/ppermute | solution.py:40
  49.3 9.7 %collective-permute-start.13 = (bf16[2,128,3584]{2,1,0:T(8,128)(2,1)S(1)}, bf16[2,128,3584]{2,1,0:T(8,128)(2,1)S(1)}, u32[]{:S(2)}, u32[]{:S(2)}) collective-permute-start(bf16[2,128,3584]{2,1,0:T(8,128)(2,1)S(1)} %get-tuple-element.196), channel_id=1, source_target_pairs={{0,1},{1,0},{2,3},{3,2},{4,5},{5,4},{6,7},{7,6},{8,9},{9,8},{10,11... | collective-permute-start | bytes 5505032 | tf_op jit(solution)/shard_map/ppermute | solution.py:40
  49.4 9.6 %collective-permute-start.11 = (bf16[32,3584]{1,0:T(8,128)(2,1)S(1)}, bf16[32,3584]{1,0:T(8,128)(2,1)S(1)}, u32[]{:S(2)}, u32[]{:S(2)}) collective-permute-start(bf16[32,3584]{1,0:T(8,128)(2,1)S(1)} %get-tuple-element.194), channel_id=1, source_target_pairs={{0,4},{1,5},{2,6},{3,7},{4,0},{5,1},{6,2},{7,3},{8,12},{9,13},{10,... | collective-permute-start | bytes 688136 | tf_op jit(solution)/shard_map/ppermute | solution.py:40
  51.2 7.8 %collective-permute-start.12 = (bf16[32,3584]{1,0:T(8,128)(2,1)S(1)}, bf16[32,3584]{1,0:T(8,128)(2,1)S(1)}, u32[]{:S(2)}, u32[]{:S(2)}) collective-permute-start(bf16[32,3584]{1,0:T(8,128)(2,1)S(1)} %get-tuple-element.195), channel_id=1, source_target_pairs={{0,2},{1,3},{2,0},{3,1},{4,6},{5,7},{6,4},{7,5},{8,10},{9,11},{10,... | collective-permute-start | bytes 688136 | tf_op jit(solution)/shard_map/ppermute | solution.py:40
  52.7 6.3 %collective-permute-start.10 = (f32[144,128]{1,0:T(8,128)S(1)}, f32[144,128]{1,0:T(8,128)S(1)}, u32[]{:S(2)}, u32[]{:S(2)}) collective-permute-start(f32[144,128]{1,0:T(8,128)S(1)} %pad_maximum_fusion.6), channel_id=1, source_target_pairs={{0,4},{1,5},{2,6},{3,7},{4,0},{5,1},{6,2},{7,3},{8,12},{9,13},{10,... | collective-permute-start | bytes 221192 | tf_op jit(solution)/shard_map/ppermute | solution.py:40
  59.3 12.1 %collective-permute-start.14 = (bf16[64,3584]{1,0:T(8,128)(2,1)S(1)}, bf16[64,3584]{1,0:T(8,128)(2,1)S(1)}, u32[]{:S(2)}, u32[]{:S(2)}) collective-permute-start(bf16[64,3584]{1,0:T(8,128)(2,1)S(1)} %get-tuple-element.201), channel_id=1, source_target_pairs={{0,2},{1,3},{2,0},{3,1},{4,6},{5,7},{6,4},{7,5},{8,10},{9,11},{10,... | collective-permute-start | bytes 1376264 | tf_op jit(solution)/shard_map/ppermute | solution.py:40
  61.1 11.8 %collective-permute-start.15 = (bf16[64,3584]{1,0:T(8,128)(2,1)S(1)}, bf16[64,3584]{1,0:T(8,128)(2,1)S(1)}, u32[]{:S(2)}, u32[]{:S(2)}) collective-permute-start(bf16[64,3584]{1,0:T(8,128)(2,1)S(1)} %get-tuple-element.202), channel_id=1, source_target_pairs={{0,4},{1,5},{2,6},{3,7},{4,0},{5,1},{6,2},{7,3},{8,12},{9,13},{10,... | collective-permute-start | bytes 1376264 | tf_op jit(solution)/shard_map/ppermute | solution.py:40
  73.0 6.1 %collective-permute-start.16 = (bf16[32,3584]{1,0:T(8,128)(2,1)S(1)}, bf16[32,3584]{1,0:T(8,128)(2,1)S(1)}, u32[]{:S(2)}, u32[]{:S(2)}) collective-permute-start(bf16[32,3584]{1,0:T(8,128)(2,1)S(1)} %get-tuple-element.215), channel_id=1, source_target_pairs={{0,4},{1,5},{2,6},{3,7},{4,0},{5,1},{6,2},{7,3},{8,12},{9,13},{10,... | collective-permute-start | bytes 688136 | tf_op jit(solution)/shard_map/ppermute | solution.py:40
  74.6 6.0 %collective-permute-start.17 = (bf16[32,3584]{1,0:T(8,128)(2,1)S(1)}, bf16[32,3584]{1,0:T(8,128)(2,1)S(1)}, u32[]{:S(2)}, u32[]{:S(2)}) collective-permute-start(bf16[32,3584]{1,0:T(8,128)(2,1)S(1)} %get-tuple-element.216), channel_id=1, source_target_pairs={{0,2},{1,3},{2,0},{3,1},{4,6},{5,7},{6,4},{7,5},{8,10},{9,11},{10,... | collective-permute-start | bytes 688136 | tf_op jit(solution)/shard_map/ppermute | solution.py:40
  86.4 5.1 %collective-permute-start.22 = (bf16[176,128]{1,0:T(8,128)(2,1)S(1)}, bf16[176,128]{1,0:T(8,128)(2,1)S(1)}, u32[]{:S(2)}, u32[]{:S(2)}) collective-permute-start(bf16[176,128]{1,0:T(8,128)(2,1)S(1)} %pad_maximum_fusion.9), channel_id=1, source_target_pairs={{0,6},{1,7},{2,4},{3,5},{4,2},{5,3},{6,0},{7,1},{8,14},{9,15},{10,... | collective-permute-start | bytes 135176 | tf_op jit(solution)/shard_map/ppermute | solution.py:40
  86.7 4.8 %collective-permute-start.21 = (bf16[176,128]{1,0:T(8,128)(2,1)S(1)}, bf16[176,128]{1,0:T(8,128)(2,1)S(1)}, u32[]{:S(2)}, u32[]{:S(2)}) collective-permute-start(bf16[176,128]{1,0:T(8,128)(2,1)S(1)} %pad_maximum_fusion.9), channel_id=1, source_target_pairs={{0,4},{1,5},{2,6},{3,7},{4,0},{5,1},{6,2},{7,3},{8,12},{9,13},{10,... | collective-permute-start | bytes 135176 | tf_op jit(solution)/shard_map/ppermute | solution.py:40
  88.4 4.0 %collective-permute-start.20 = (bf16[176,128]{1,0:T(8,128)(2,1)S(1)}, bf16[176,128]{1,0:T(8,128)(2,1)S(1)}, u32[]{:S(2)}, u32[]{:S(2)}) collective-permute-start(bf16[176,128]{1,0:T(8,128)(2,1)S(1)} %pad_maximum_fusion.9), channel_id=1, source_target_pairs={{0,2},{1,3},{2,0},{3,1},{4,6},{5,7},{6,4},{7,5},{8,10},{9,11},{10,... | collective-permute-start | bytes 135176 | tf_op jit(solution)/shard_map/ppermute | solution.py:40
  93.7 17.1 %collective-permute-start.23 = (bf16[16,7168]{1,0:T(8,128)(2,1)S(1)}, bf16[16,7168]{1,0:T(8,128)(2,1)S(1)}, u32[]{:S(2)}, u32[]{:S(2)}) collective-permute-start(bf16[16,7168]{1,0:T(8,128)(2,1)S(1)} %get-tuple-element.254), channel_id=1, source_target_pairs={{0,2},{1,3},{2,0},{3,1},{4,6},{5,7},{6,4},{7,5},{8,10},{9,11},{10,... | collective-permute-start | bytes 688136 | tf_op jit(solution)/shard_map/ppermute | solution.py:40
  95.3 15.6 %collective-permute-start.24 = (bf16[16,7168]{1,0:T(8,128)(2,1)S(1)}, bf16[16,7168]{1,0:T(8,128)(2,1)S(1)}, u32[]{:S(2)}, u32[]{:S(2)}) collective-permute-start(bf16[16,7168]{1,0:T(8,128)(2,1)S(1)} %get-tuple-element.255), channel_id=1, source_target_pairs={{0,4},{1,5},{2,6},{3,7},{4,0},{5,1},{6,2},{7,3},{8,12},{9,13},{10,... | collective-permute-start | bytes 688136 | tf_op jit(solution)/shard_map/ppermute | solution.py:40
  95.8 15.1 %collective-permute-start.25 = (bf16[16,7168]{1,0:T(8,128)(2,1)S(1)}, bf16[16,7168]{1,0:T(8,128)(2,1)S(1)}, u32[]{:S(2)}, u32[]{:S(2)}) collective-permute-start(bf16[16,7168]{1,0:T(8,128)(2,1)S(1)} %get-tuple-element.256), channel_id=1, source_target_pairs={{0,6},{1,7},{2,4},{3,5},{4,2},{5,3},{6,0},{7,1},{8,14},{9,15},{10,... | collective-permute-start | bytes 688136 | tf_op jit(solution)/shard_map/ppermute | solution.py:40
  111.9 12.4 %collective-permute-start.26 = (bf16[8,7168]{1,0:T(8,128)(2,1)S(1)}, bf16[8,7168]{1,0:T(8,128)(2,1)S(1)}, u32[]{:S(2)}, u32[]{:S(2)}) collective-permute-start(bf16[8,7168]{1,0:T(8,128)(2,1)S(1)} %get-tuple-element.273), channel_id=1, source_target_pairs={{0,4},{1,5},{2,6},{3,7},{4,0},{5,1},{6,2},{7,3},{8,12},{9,13},{10,... | collective-permute-start | bytes 344072 | tf_op jit(solution)/shard_map/ppermute | solution.py:40
  112.3 12.1 %collective-permute-start.27 = (bf16[8,7168]{1,0:T(8,128)(2,1)S(1)}, bf16[8,7168]{1,0:T(8,128)(2,1)S(1)}, u32[]{:S(2)}, u32[]{:S(2)}) collective-permute-start(bf16[8,7168]{1,0:T(8,128)(2,1)S(1)} %get-tuple-element.274), channel_id=1, source_target_pairs={{0,2},{1,3},{2,0},{3,1},{4,6},{5,7},{6,4},{7,5},{8,10},{9,11},{10,... | collective-permute-start | bytes 344072 | tf_op jit(solution)/shard_map/ppermute | solution.py:40
  114.0 4.4 %collective-permute-start.28 = (bf16[32,1024]{1,0:T(8,128)(2,1)S(1)}, bf16[32,1024]{1,0:T(8,128)(2,1)S(1)}, u32[]{:S(2)}, u32[]{:S(2)}) collective-permute-start(bf16[32,1024]{1,0:T(8,128)(2,1)S(1)} %get-tuple-element.275), channel_id=1, source_target_pairs={{0,8},{8,0},{16,24},{24,16},{1,9},{9,1},{17,25},{25,17},{2,10},{10... | collective-permute-start | bytes 196616 | tf_op jit(solution)/shard_map/ppermute | solution.py:40
  114.7 6.8 %collective-permute-start.29 = (bf16[32,1024]{1,0:T(8,128)(2,1)S(1)}, bf16[32,1024]{1,0:T(8,128)(2,1)S(1)}, u32[]{:S(2)}, u32[]{:S(2)}) collective-permute-start(bf16[32,1024]{1,0:T(8,128)(2,1)S(1)} %get-tuple-element.276), channel_id=1, source_target_pairs={{0,16},{8,24},{16,0},{24,8},{1,17},{9,25},{17,1},{25,9},{2,18},{10... | collective-permute-start | bytes 196616 | tf_op jit(solution)/shard_map/ppermute | solution.py:40
  118.2 6.2 %collective-permute-start.30 = (bf16[32,1024]{1,0:T(8,128)(2,1)S(1)}, bf16[32,1024]{1,0:T(8,128)(2,1)S(1)}, u32[]{:S(2)}, u32[]{:S(2)}) collective-permute-start(bf16[32,1024]{1,0:T(8,128)(2,1)S(1)} %get-tuple-element.277), channel_id=1, source_target_pairs={{0,24},{8,16},{16,8},{24,0},{1,25},{9,17},{17,9},{25,1},{2,26},{10... | collective-permute-start | bytes 196616 | tf_op jit(solution)/shard_map/ppermute | solution.py:40
  124.5 9.7 %collective-permute-start.31 = (bf16[16,7168]{1,0:T(8,128)(2,1)S(1)}, bf16[16,7168]{1,0:T(8,128)(2,1)S(1)}, u32[]{:S(2)}, u32[]{:S(2)}) collective-permute-start(bf16[16,7168]{1,0:T(8,128)(2,1)S(1)} %pad_maximum_fusion.3), channel_id=1, source_target_pairs={{0,2},{1,3},{2,0},{3,1},{4,6},{5,7},{6,4},{7,5},{8,10},{9,11},{10,... | collective-permute-start | bytes 688136 | tf_op jit(solution)/shard_map/ppermute | solution.py:40
  124.9 9.3 %collective-permute-start.32 = (bf16[16,7168]{1,0:T(8,128)(2,1)S(1)}, bf16[16,7168]{1,0:T(8,128)(2,1)S(1)}, u32[]{:S(2)}, u32[]{:S(2)}) collective-permute-start(bf16[16,7168]{1,0:T(8,128)(2,1)S(1)} %pad_maximum_fusion.4), channel_id=1, source_target_pairs={{0,4},{1,5},{2,6},{3,7},{4,0},{5,1},{6,2},{7,3},{8,12},{9,13},{10,... | collective-permute-start | bytes 688136 | tf_op jit(solution)/shard_map/ppermute | solution.py:40
  126.9 4.4 %collective-permute-start.33 = (bf16[32,1024]{1,0:T(8,128)(2,1)S(1)}, bf16[32,1024]{1,0:T(8,128)(2,1)S(1)}, u32[]{:S(2)}, u32[]{:S(2)}) collective-permute-start(bf16[32,1024]{1,0:T(8,128)(2,1)S(1)} %add_convert_fusion.5.refs_0_), channel_id=1, source_target_pairs={{0,8},{8,0},{16,24},{24,16},{1,9},{9,1},{17,25},{25,17},{2,10},{10... | collective-permute-start | bytes 196616 | tf_op jit(solution)/shard_map/ppermute | solution.py:40
  126.9 5.2 %collective-permute-start.34 = (bf16[32,1024]{1,0:T(8,128)(2,1)S(1)}, bf16[32,1024]{1,0:T(8,128)(2,1)S(1)}, u32[]{:S(2)}, u32[]{:S(2)}) collective-permute-start(bf16[32,1024]{1,0:T(8,128)(2,1)S(1)} %add_convert_fusion.5.refs_0_), channel_id=1, source_target_pairs={{0,16},{8,24},{16,0},{24,8},{1,17},{9,25},{17,1},{25,9},{2,18},{10... | collective-permute-start | bytes 196616 | tf_op jit(solution)/shard_map/ppermute | solution.py:40
  127.7 6.5 %collective-permute-start.35 = (bf16[32,1024]{1,0:T(8,128)(2,1)S(1)}, bf16[32,1024]{1,0:T(8,128)(2,1)S(1)}, u32[]{:S(2)}, u32[]{:S(2)}) collective-permute-start(bf16[32,1024]{1,0:T(8,128)(2,1)S(1)} %add_convert_fusion.5.refs_0_), channel_id=1, source_target_pairs={{0,24},{8,16},{16,8},{24,0},{1,25},{9,17},{17,9},{25,1},{2,26},{10... | collective-permute-start | bytes 196616 | tf_op jit(solution)/shard_map/ppermute | solution.py:40
  (15 other events, 137.5 us)

commit v4 on v3

--- a/solution.py
+++ b/solution.py
@@ -13,6 +13,7 @@
 SLOTS = 4
 STEP = 1792
 VMEM_LIMIT = 48 * 1024 * 1024
+VMEM_REST = 30 * 1024 * 1024
 VMEM_FIRST = 62 * 1024 * 1024
 BF = jnp.bfloat16
 F32 = jnp.float32
@@ -272,7 +273,7 @@
         out_shape=out_shape,
         scratch_shapes=[pltpu.VMEM((rows, depth), BF), pltpu.VMEM((rows, 2 * rank), BF)]
         + stream_scratch(depth, tile, 2 * (size // tile)),
-        compiler_params=params(),
+        compiler_params=params(VMEM_LIMIT if emit_xa else VMEM_REST),
         cost_estimate=pl.CostEstimate(
             flops=4 * rows * depth * size, bytes_accessed=4 * depth * size, transcendentals=0
         ),
@@ -378,7 +379,7 @@
         ],
         input_output_aliases=aliases,
         scratch_shapes=[pltpu.VMEM((2, share, rank), BF)],
-        compiler_params=params(),
+        compiler_params=params(VMEM_REST),
         cost_estimate=pl.CostEstimate(
             flops=4 * rank * share * size * 2, bytes_accessed=share * size * 20, transcendentals=share * size
         ),
@@ -414,7 +415,7 @@
         out_specs=vmem,
         out_shape=jax.ShapeDtypeStruct((2, rank, depth), F32),
         scratch_shapes=[pltpu.VMEM((rank, rank), F32)] + stream_scratch(depth, tile, 2 * (size // tile)),
-        compiler_params=params(),
+        compiler_params=params(VMEM_REST),
         cost_estimate=pl.CostEstimate(
             flops=4 * rank * depth * size, bytes_accessed=4 * depth * size, transcendentals=0
         ),
@@ -454,7 +455,7 @@
         out_specs=[vmem] * nx,
         out_shape=[jax.ShapeDtypeStruct((piece, depth), F32 if k == 0 else BF) for k in range(nx)],
         scratch_shapes=[pltpu.VMEM((rows, depth), BF), pltpu.VMEM((2 * rank, depth), F32)],
-        compiler_params=params(),
+        compiler_params=params(VMEM_REST),
         name="join_grad_in",
     )(me, *xs, *seconds, *uts)
 
@@ -476,7 +477,7 @@
         in_specs=[pl.BlockSpec(memory_space=pltpu.SMEM)] + [vmem] * len(pieces),
         out_specs=vmem,
         out_shape=jax.ShapeDtypeStruct((rows, pieces[0].shape[1]), F32),
-        compiler_params=params(),
+        compiler_params=params(VMEM_REST),
         name="lay_grad_in",
     )(me, *pieces)
 
@@ -513,7 +514,7 @@
         out_specs=[line] + [pl.BlockSpec((rows, tile), lambda f: (0, f))] * (n // 2),
         out_shape=[jax.ShapeDtypeStruct((2, 1, width), F32)]
         + [jax.ShapeDtypeStruct((rows, width), F32 if j == 0 else BF) for j in range(n // 2)],
-        compiler_params=params(),
+        compiler_params=params(VMEM_REST),
         name="fold_rows",
     )(ad_keep, ad_got, g_keep, g_got, sq, stat, mag)
 
@@ -549,7 +550,7 @@
         out_specs=pl.BlockSpec((2, 2 * half, tile), lambda f: (0, 0, f + start)),
         out_shape=jax.ShapeDtypeStruct((2, 2 * half, width), F32),
         input_output_aliases=aliases,
-        compiler_params=params(),
+        compiler_params=params(VMEM_REST),
         name="order_rows",
     )(*args)
 

time: 140 us -> 139 us (level)
  Pallas kernels: 57.8 us -> 55.8 us
    pallas_call x2, Pallas kernels: 6 us -> 4.37 us  [own_call(): pl.pallas_call(functools.partial(own_kernel, n, orders, len(parts), len(x...]
  transfers between devices with their start and end apart: 37 -> 37, of which waited for: 15 -> 15; matrix products, arithmetic and copies ran while one was open for 1% -> 1% of each run, Pallas kernels for 36% -> 35%
where the time goes in v4:
time: 139 us
  Pallas kernels  55.8 us (40%)
  starting transfers between devices  40.9 us (29%)
  waiting for transfers between devices  38.3 us (28%)
  other arithmetic  1.99 us (1%)
    ppermute x37, starting transfers between devices, swap(): return lax.ppermute(x, axis, [(i, i ^ bit) for i in range(n)])  40.9 us
    ppermute x37, waiting for transfers between devices, swap(): return lax.ppermute(x, axis, [(i, i ^ bit) for i in range(n)])  38.3 us
    pallas_call x2, Pallas kernels, token_call(): pl.pallas_call(functools.partial(token_kernel, n, share, orders, len(xs),...  18 us
    pallas_call x1, Pallas kernels, second_call(): pl.pallas_call(functools.partial(second_kernel, tile, size // tile, first...  13.6 us
    pallas_call x1, Pallas kernels, adapter_call(): pl.pallas_call(functools.partial(adapter_kernel, n, orders, tile, width /...  13.6 us
    pallas_call x2, Pallas kernels, own_call(): pl.pallas_call(functools.partial(own_kernel, n, orders, len(parts), len(x...  4.37 us
    pallas_call x1, Pallas kernels, order_call(): pl.pallas_call(functools.partial(order_kernel, n, orders, prior is not No...  2.83 us
  transfers between devices with their start and end apart: 37, of which 15 were waited for; matrix products, arithmetic and copies ran while one was open for 1% of the time, Pallas kernels for 35%

profile of v4, /device:TPU:0, one launch (start us, length us, event | category | flops | bytes accessed | tf_op | source)
XLA Modules:
  0.0 138.9 jit_solution(16101246564928422449)
XLA Ops:
  0.6 4.1 %collective-permute-start.1 = (bf16[64,1024]{1,0:T(8,128)(2,1)}, bf16[64,1024]{1,0:T(8,128)(2,1)S(1)}, u32[]{:S(2)}, u32[]{:S(2)}) collective-permute-start(bf16[64,1024]{1,0:T(8,128)(2,1)} %refs_0_.2), channel_id=1, source_target_pairs={{0,16},{8,24},{16,0},{24,8},{1,17},{9,25},{17,1},{25,9},{2,18},{10... | collective-permute-start | bytes 393224 | tf_op jit(solution)/shard_map/ppermute | solution.py:41
  4.7 1.6 %collective-permute-start = (bf16[64,1024]{1,0:T(8,128)(2,1)}, bf16[64,1024]{1,0:T(8,128)(2,1)S(1)}, u32[]{:S(2)}, u32[]{:S(2)}) collective-permute-start(bf16[64,1024]{1,0:T(8,128)(2,1)} %refs_0_.2), channel_id=1, source_target_pairs={{0,8},{8,0},{16,24},{24,16},{1,9},{9,1},{17,25},{25,17},{2,10},{10... | collective-permute-start | bytes 393224 | tf_op jit(solution)/shard_map/ppermute | solution.py:41
  6.9 13.6 %adapter_pass.1 = (bf16[2,32,7168]{2,1,0:T(8,128)(2,1)}, bf16[2,32,7168]{2,1,0:T(8,128)(2,1)}, f32[2,1,7168]{2,1,0:T(1,128)}) custom-call(s32[2]{0:T(128)} %pad_add_fusion.me_ref.token_ref, bf16[2,64,1024]{2,1,0:T(8,128)(2,1)} %a_ref.3, bf16[2,1024,7168]{2,1,0:T(8,128)(2,1)} %w_ref.3, bf16[2,64,7168]{2,1,0:T(8,128)(2,1)} %b_ref.3), custom_call_target="tpu_custom_call" | custom-call | flops 3758096384 | bytes 29360128 | tf_op jit(solution)/shard_map/adapter_pass/pallas_call | solution.py:173
  21.1 9.2 %token_pass.2 = (bf16[2,128,3584]{2,1,0:T(8,128)(2,1)S(1)}, bf16[2,128,3584]{2,1,0:T(8,128)(2,1)S(1)}, f32[128,128]{1,0:T(8,128)S(1)}, f32[128,128]{1,0:T(8,128)S(1)}) custom-call(s32[2]{0:T(128)S(1)} %copy-done.5, bf16[64,1024]{1,0:T(8,128)(2,1)S(1)} %copy-done.3, bf16[64,1024]{1,0:T(8,128)(2,1)S(1)} %collective-permute-done.refs_1_, ...), custom_call_target="tpu_custom_call" | custom-call | flops 3758096384 | bytes 14680064 | tf_op jit(solution)/shard_map/token_pass/pallas_call | solution.py:262
  30.9 3.4 %collective-permute-done.5.refs_9_ = f32[128,128]{1,0:T(8,128)S(1)} collective-permute-done((f32[128,128]{1,0:T(8,128)S(1)}, f32[128,128]{1,0:T(8,128)S(1)}, u32[]{:S(2)}, u32[]{:S(2)}) %collective-permute-start.5) | collective-permute-done | bytes 65568 | tf_op jit(solution)/shard_map/ppermute | solution.py:41
  34.5 1.8 %collective-permute-start.8 = (bf16[64,3584]{1,0:T(8,128)(2,1)S(1)}, bf16[64,3584]{1,0:T(8,128)(2,1)S(1)}, u32[]{:S(2)}, u32[]{:S(2)}) collective-permute-start(bf16[64,3584]{1,0:T(8,128)(2,1)S(1)} %get-tuple-element.183), channel_id=1, source_target_pairs={{0,2},{1,3},{2,0},{3,1},{4,6},{5,7},{6,4},{7,5},{8,10},{9,11},{10,... | collective-permute-start | bytes 1376264 | tf_op jit(solution)/shard_map/ppermute | solution.py:41
  36.3 1.5 %collective-permute-start.9 = (bf16[64,3584]{1,0:T(8,128)(2,1)S(1)}, bf16[64,3584]{1,0:T(8,128)(2,1)S(1)}, u32[]{:S(2)}, u32[]{:S(2)}) collective-permute-start(bf16[64,3584]{1,0:T(8,128)(2,1)S(1)} %get-tuple-element.184), channel_id=1, source_target_pairs={{0,4},{1,5},{2,6},{3,7},{4,0},{5,1},{6,2},{7,3},{8,12},{9,13},{10,... | collective-permute-start | bytes 1376264 | tf_op jit(solution)/shard_map/ppermute | solution.py:41
  38.4 8.8 %token_pass.3 = (bf16[2,128,3584]{2,1,0:T(8,128)(2,1)S(1)}, bf16[2,128,3584]{2,1,0:T(8,128)(2,1)S(1)}) custom-call(s32[2]{0:T(128)S(1)} %copy-done.5, bf16[64,1024]{1,0:T(8,128)(2,1)S(1)} %copy-done.3, bf16[64,1024]{1,0:T(8,128)(2,1)S(1)} %collective-permute-done.refs_1_, bf16[64,1024]{1,0:T(8,128)(2,1)S(1)} %collective-permute-done.1.refs_2_, ...), custom_call_target="tpu_custom_call" | custom-call | flops 3758096384 | bytes 14680064 | tf_op jit(solution)/shard_map/token_pass/pallas_call | solution.py:262
  47.2 1.9 %collective-permute-done.7 = f32[176,128]{1,0:T(8,128)S(1)} collective-permute-done((f32[176,128]{1,0:T(8,128)S(1)}, f32[176,128]{1,0:T(8,128)S(1)}, u32[]{:S(2)}, u32[]{:S(2)}) %collective-permute-start.7) | collective-permute-done | bytes 90144 | tf_op jit(solution)/shard_map/ppermute | solution.py:41
  49.4 1.8 %collective-permute-start.11 = (bf16[32,3584]{1,0:T(8,128)(2,1)S(1)}, bf16[32,3584]{1,0:T(8,128)(2,1)S(1)}, u32[]{:S(2)}, u32[]{:S(2)}) collective-permute-start(bf16[32,3584]{1,0:T(8,128)(2,1)S(1)} %get-tuple-element.194), channel_id=1, source_target_pairs={{0,4},{1,5},{2,6},{3,7},{4,0},{5,1},{6,2},{7,3},{8,12},{9,13},{10,... | collective-permute-start | bytes 688136 | tf_op jit(solution)/shard_map/ppermute | solution.py:41
  53.2 5.8 %collective-permute-done.10 = f32[144,128]{1,0:T(8,128)S(1)} collective-permute-done((f32[144,128]{1,0:T(8,128)S(1)}, f32[144,128]{1,0:T(8,128)S(1)}, u32[]{:S(2)}, u32[]{:S(2)}) %collective-permute-start.10) | collective-permute-done | bytes 73760 | tf_op jit(solution)/shard_map/ppermute | solution.py:41
  59.2 1.8 %collective-permute-start.14 = (bf16[64,3584]{1,0:T(8,128)(2,1)S(1)}, bf16[64,3584]{1,0:T(8,128)(2,1)S(1)}, u32[]{:S(2)}, u32[]{:S(2)}) collective-permute-start(bf16[64,3584]{1,0:T(8,128)(2,1)S(1)} %get-tuple-element.201), channel_id=1, source_target_pairs={{0,2},{1,3},{2,0},{3,1},{4,6},{5,7},{6,4},{7,5},{8,10},{9,11},{10,... | collective-permute-start | bytes 1376264 | tf_op jit(solution)/shard_map/ppermute | solution.py:41
  61.0 1.5 %collective-permute-start.15 = (bf16[64,3584]{1,0:T(8,128)(2,1)S(1)}, bf16[64,3584]{1,0:T(8,128)(2,1)S(1)}, u32[]{:S(2)}, u32[]{:S(2)}) collective-permute-start(bf16[64,3584]{1,0:T(8,128)(2,1)S(1)} %get-tuple-element.202), channel_id=1, source_target_pairs={{0,4},{1,5},{2,6},{3,7},{4,0},{5,1},{6,2},{7,3},{8,12},{9,13},{10,... | collective-permute-start | bytes 1376264 | tf_op jit(solution)/shard_map/ppermute | solution.py:41
  62.6 2.4 %own_tokens.2 = (bf16[32,7168]{1,0:T(8,128)(2,1)}, bf16[2,32,3584]{2,1,0:T(8,128)(2,1)S(1)}, bf16[2,32,3584]{2,1,0:T(8,128)(2,1)S(1)}, f32[2,1,3584]{2,1,0:T(1,128)S(1)}, f32[32,128]{1,0:T(8,128)S(1)}) custom-call(s32[2]{0:T(128)S(1)} %copy-done.5, bf16[2,128,3584]{2,1,0:T(8,128)(2,1)S(1)} %get-tuple-element.179.refs_0_.refs_1_, ...), custom_call_target="tpu_custom_call" | custom-call | flops 58720256 | bytes 2293760 | tf_op jit(solution)/shard_map/own_tokens/pallas_call | solution.py:362
  65.0 6.4 %collective-permute-done.14.refs_4_ = bf16[64,3584]{1,0:T(8,128)(2,1)S(1)} collective-permute-done((bf16[64,3584]{1,0:T(8,128)(2,1)S(1)}, bf16[64,3584]{1,0:T(8,128)(2,1)S(1)}, u32[]{:S(2)}, u32[]{:S(2)}) %collective-permute-start.14) | collective-permute-done | bytes 458784 | tf_op jit(solution)/shard_map/ppermute | solution.py:41
  73.0 1.6 %collective-permute-start.16 = (bf16[32,3584]{1,0:T(8,128)(2,1)S(1)}, bf16[32,3584]{1,0:T(8,128)(2,1)S(1)}, u32[]{:S(2)}, u32[]{:S(2)}) collective-permute-start(bf16[32,3584]{1,0:T(8,128)(2,1)S(1)} %get-tuple-element.215), channel_id=1, source_target_pairs={{0,4},{1,5},{2,6},{3,7},{4,0},{5,1},{6,2},{7,3},{8,12},{9,13},{10,... | collective-permute-start | bytes 688136 | tf_op jit(solution)/shard_map/ppermute | solution.py:41
  75.1 4.0 %collective-permute-done.16.refs_6_ = bf16[32,3584]{1,0:T(8,128)(2,1)S(1)} collective-permute-done((bf16[32,3584]{1,0:T(8,128)(2,1)S(1)}, bf16[32,3584]{1,0:T(8,128)(2,1)S(1)}, u32[]{:S(2)}, u32[]{:S(2)}) %collective-permute-start.16) | collective-permute-done | bytes 229408 | tf_op jit(solution)/shard_map/ppermute | solution.py:41
  79.1 1.5 %collective-permute-done.17.refs_7_ = bf16[32,3584]{1,0:T(8,128)(2,1)S(1)} collective-permute-done((bf16[32,3584]{1,0:T(8,128)(2,1)S(1)}, bf16[32,3584]{1,0:T(8,128)(2,1)S(1)}, u32[]{:S(2)}, u32[]{:S(2)}) %collective-permute-start.17) | collective-permute-done | bytes 229408 | tf_op jit(solution)/shard_map/ppermute | solution.py:41
  80.6 2.0 %own_tokens.3 = (bf16[32,7168]{1,0:T(8,128)(2,1)}, bf16[2,32,3584]{2,1,0:T(8,128)(2,1)S(1)}, bf16[2,32,3584]{2,1,0:T(8,128)(2,1)S(1)}, f32[2,1,3584]{2,1,0:T(1,128)S(1)}, f32[32,128]{1,0:T(8,128)S(1)}) custom-call(s32[2]{0:T(128)S(1)} %copy-done.5, bf16[2,128,3584]{2,1,0:T(8,128)(2,1)S(1)} %get-tuple-element.198.refs_0_.refs_1_, ...), custom_call_target="tpu_custom_call", output_to_operand_aliasing={{0}: (17, {})} | custom-call | flops 58720256 | bytes 2293760 | tf_op jit(solution)/shard_map/own_tokens/pallas_call | solution.py:362
  83.4 2.1 %collective-permute-done.18 = f32[144,128]{1,0:T(8,128)S(1)} collective-permute-done((f32[144,128]{1,0:T(8,128)S(1)}, f32[144,128]{1,0:T(8,128)S(1)}, u32[]{:S(2)}, u32[]{:S(2)}) %collective-permute-start.18) | collective-permute-done | bytes 73760 | tf_op jit(solution)/shard_map/ppermute | solution.py:41
  85.9 1.7 %collective-permute-start.21 = (bf16[176,128]{1,0:T(8,128)(2,1)S(1)}, bf16[176,128]{1,0:T(8,128)(2,1)S(1)}, u32[]{:S(2)}, u32[]{:S(2)}) collective-permute-start(bf16[176,128]{1,0:T(8,128)(2,1)S(1)} %pad_maximum_fusion.9), channel_id=1, source_target_pairs={{0,4},{1,5},{2,6},{3,7},{4,0},{5,1},{6,2},{7,3},{8,12},{9,13},{10,... | collective-permute-start | bytes 135176 | tf_op jit(solution)/shard_map/ppermute | solution.py:41
  89.1 1.6 %collective-permute-done.22 = bf16[176,128]{1,0:T(8,128)(2,1)S(1)} collective-permute-done((bf16[176,128]{1,0:T(8,128)(2,1)S(1)}, bf16[176,128]{1,0:T(8,128)(2,1)S(1)}, u32[]{:S(2)}, u32[]{:S(2)}) %collective-permute-start.22) | collective-permute-done | bytes 45088 | tf_op jit(solution)/shard_map/ppermute | solution.py:41
  92.8 1.6 %collective-permute-start.23 = (bf16[16,7168]{1,0:T(8,128)(2,1)S(1)}, bf16[16,7168]{1,0:T(8,128)(2,1)S(1)}, u32[]{:S(2)}, u32[]{:S(2)}) collective-permute-start(bf16[16,7168]{1,0:T(8,128)(2,1)S(1)} %get-tuple-element.254), channel_id=1, source_target_pairs={{0,2},{1,3},{2,0},{3,1},{4,6},{5,7},{6,4},{7,5},{8,10},{9,11},{10,... | collective-permute-start | bytes 688136 | tf_op jit(solution)/shard_map/ppermute | solution.py:41
  96.4 13.6 %second_pass.1.refs_4_ = f32[2,64,1024]{2,1,0:T(8,128)S(1)} custom-call(s32[2]{0:T(128)S(1)} %copy-done.5, bf16[2,1024,7168]{2,1,0:T(8,128)(2,1)} %w_ref.3, bf16[2,64,7168]{2,1,0:T(8,128)(2,1)S(1)} %copy-done, bf16[2,64,1024]{2,1,0:T(8,128)(2,1)S(1)} %copy-done.1, f32[2,1,7168]{2,1,0:T(1,128)S(1)} %get-tuple-element.257.cd_ref), custom_call_target="tpu_custom_call" | custom-call | flops 1879048192 | bytes 29360128 | tf_op jit(solution)/shard_map/second_pass/pallas_call | solution.py:412
  111.5 1.7 %collective-permute-start.27 = (bf16[8,7168]{1,0:T(8,128)(2,1)S(1)}, bf16[8,7168]{1,0:T(8,128)(2,1)S(1)}, u32[]{:S(2)}, u32[]{:S(2)}) collective-permute-start(bf16[8,7168]{1,0:T(8,128)(2,1)S(1)} %get-tuple-element.274), channel_id=1, source_target_pairs={{0,2},{1,3},{2,0},{3,1},{4,6},{5,7},{6,4},{7,5},{8,10},{9,11},{10,... | collective-permute-start | bytes 344072 | tf_op jit(solution)/shard_map/ppermute | solution.py:41
  113.8 3.5 %collective-permute-start.29 = (bf16[32,1024]{1,0:T(8,128)(2,1)S(1)}, bf16[32,1024]{1,0:T(8,128)(2,1)S(1)}, u32[]{:S(2)}, u32[]{:S(2)}) collective-permute-start(bf16[32,1024]{1,0:T(8,128)(2,1)S(1)} %get-tuple-element.276), channel_id=1, source_target_pairs={{0,16},{8,24},{16,0},{24,8},{1,17},{9,25},{17,1},{25,9},{2,18},{10... | collective-permute-start | bytes 196616 | tf_op jit(solution)/shard_map/ppermute | solution.py:41
  117.5 3.1 %collective-permute-done.29 = bf16[32,1024]{1,0:T(8,128)(2,1)S(1)} collective-permute-done((bf16[32,1024]{1,0:T(8,128)(2,1)S(1)}, bf16[32,1024]{1,0:T(8,128)(2,1)S(1)}, u32[]{:S(2)}, u32[]{:S(2)}) %collective-permute-start.29) | collective-permute-done | bytes 65568 | tf_op jit(solution)/shard_map/ppermute | solution.py:41
  120.6 2.9 %collective-permute-done.30 = bf16[32,1024]{1,0:T(8,128)(2,1)S(1)} collective-permute-done((bf16[32,1024]{1,0:T(8,128)(2,1)S(1)}, bf16[32,1024]{1,0:T(8,128)(2,1)S(1)}, u32[]{:S(2)}, u32[]{:S(2)}) %collective-permute-start.30) | collective-permute-done | bytes 65568 | tf_op jit(solution)/shard_map/ppermute | solution.py:41
  124.1 1.9 %collective-permute-start.32 = (bf16[16,7168]{1,0:T(8,128)(2,1)S(1)}, bf16[16,7168]{1,0:T(8,128)(2,1)S(1)}, u32[]{:S(2)}, u32[]{:S(2)}) collective-permute-start(bf16[16,7168]{1,0:T(8,128)(2,1)S(1)} %pad_maximum_fusion.4), channel_id=1, source_target_pairs={{0,4},{1,5},{2,6},{3,7},{4,0},{5,1},{6,2},{7,3},{8,12},{9,13},{10,... | collective-permute-start | bytes 688136 | tf_op jit(solution)/shard_map/ppermute | solution.py:41
  126.8 3.5 %collective-permute-start.35 = (bf16[32,1024]{1,0:T(8,128)(2,1)S(1)}, bf16[32,1024]{1,0:T(8,128)(2,1)S(1)}, u32[]{:S(2)}, u32[]{:S(2)}) collective-permute-start(bf16[32,1024]{1,0:T(8,128)(2,1)S(1)} %add_convert_fusion.5.refs_0_), channel_id=1, source_target_pairs={{0,24},{8,16},{16,8},{24,0},{1,25},{9,17},{17,9},{25,1},{2,26},{10... | collective-permute-start | bytes 196616 | tf_op jit(solution)/shard_map/ppermute | solution.py:41
  131.2 2.2 %collective-permute-done.35.refs_3_ = bf16[32,1024]{1,0:T(8,128)(2,1)S(1)} collective-permute-done((bf16[32,1024]{1,0:T(8,128)(2,1)S(1)}, bf16[32,1024]{1,0:T(8,128)(2,1)S(1)}, u32[]{:S(2)}, u32[]{:S(2)}) %collective-permute-start.35) | collective-permute-done | bytes 65568 | tf_op jit(solution)/shard_map/ppermute | solution.py:41
  136.0 2.8 %order_rows.1 = f32[2,64,7168]{2,1,0:T(8,128)} custom-call(s32[2]{0:T(128)S(1)} %copy-done.5, bf16[2,32,7168]{2,1,0:T(8,128)(2,1)S(1)} %pad_maximum_fusion.2.low_ref, bf16[2,32,7168]{2,1,0:T(8,128)(2,1)S(1)} %collective-permute-done.36.high_ref), custom_call_target="tpu_custom_call" | custom-call | tf_op jit(solution)/shard_map/order_rows/pallas_call | solution.py:546
  (105 shorter events, 21.3 us)
Async XLA Ops:
  0.6 19.8 %collective-permute-start.1 = (bf16[64,1024]{1,0:T(8,128)(2,1)}, bf16[64,1024]{1,0:T(8,128)(2,1)S(1)}, u32[]{:S(2)}, u32[]{:S(2)}) collective-permute-start(bf16[64,1024]{1,0:T(8,128)(2,1)} %refs_0_.2), channel_id=1, source_target_pairs={{0,16},{8,24},{16,0},{24,8},{1,17},{9,25},{17,1},{25,9},{2,18},{10... | collective-permute-start | bytes 393224 | tf_op jit(solution)/shard_map/ppermute | solution.py:41
  4.7 15.7 %collective-permute-start = (bf16[64,1024]{1,0:T(8,128)(2,1)}, bf16[64,1024]{1,0:T(8,128)(2,1)S(1)}, u32[]{:S(2)}, u32[]{:S(2)}) collective-permute-start(bf16[64,1024]{1,0:T(8,128)(2,1)} %refs_0_.2), channel_id=1, source_target_pairs={{0,8},{8,0},{16,24},{24,16},{1,9},{9,1},{17,25},{25,17},{2,10},{10... | collective-permute-start | bytes 393224 | tf_op jit(solution)/shard_map/ppermute | solution.py:41
  6.3 14.2 %collective-permute-start.2 = (bf16[64,1024]{1,0:T(8,128)(2,1)}, bf16[64,1024]{1,0:T(8,128)(2,1)S(1)}, u32[]{:S(2)}, u32[]{:S(2)}) collective-permute-start(bf16[64,1024]{1,0:T(8,128)(2,1)} %refs_0_.2), channel_id=1, source_target_pairs={{0,24},{8,16},{16,8},{24,0},{1,25},{9,17},{17,9},{25,1},{2,26},{10... | collective-permute-start | bytes 393224 | tf_op jit(solution)/shard_map/ppermute | solution.py:41
  20.5 9.8 %collective-permute-start.4 = (bf16[2,32,7168]{2,1,0:T(8,128)(2,1)}, bf16[2,32,7168]{2,1,0:T(8,128)(2,1)S(1)}, u32[]{:S(2)}, u32[]{:S(2)}) collective-permute-start(bf16[2,32,7168]{2,1,0:T(8,128)(2,1)} %get-tuple-element.160), channel_id=1, source_target_pairs={{0,1},{1,0},{2,3},{3,2},{4,5},{5,4},{6,7},{7,6},{8,9},{9,8},{10,11... | collective-permute-start | bytes 2752520 | tf_op jit(solution)/shard_map/ppermute | solution.py:41
  20.6 9.7 %collective-permute-start.3 = (f32[112,128]{1,0:T(8,128)}, f32[112,128]{1,0:T(8,128)S(1)}, u32[]{:S(2)}, u32[]{:S(2)}) collective-permute-start(f32[112,128]{1,0:T(8,128)} %bitcast.43), channel_id=1, source_target_pairs={{0,1},{1,0},{2,3},{3,2},{4,5},{5,4},{6,7},{7,6},{8,9},{9,8},{10,11... | collective-permute-start | bytes 172040 | tf_op jit(solution)/shard_map/ppermute | solution.py:41
  34.5 14.6 %collective-permute-start.8 = (bf16[64,3584]{1,0:T(8,128)(2,1)S(1)}, bf16[64,3584]{1,0:T(8,128)(2,1)S(1)}, u32[]{:S(2)}, u32[]{:S(2)}) collective-permute-start(bf16[64,3584]{1,0:T(8,128)(2,1)S(1)} %get-tuple-element.183), channel_id=1, source_target_pairs={{0,2},{1,3},{2,0},{3,1},{4,6},{5,7},{6,4},{7,5},{8,10},{9,11},{10,... | collective-permute-start | bytes 1376264 | tf_op jit(solution)/shard_map/ppermute | solution.py:41
  36.3 12.8 %collective-permute-start.9 = (bf16[64,3584]{1,0:T(8,128)(2,1)S(1)}, bf16[64,3584]{1,0:T(8,128)(2,1)S(1)}, u32[]{:S(2)}, u32[]{:S(2)}) collective-permute-start(bf16[64,3584]{1,0:T(8,128)(2,1)S(1)} %get-tuple-element.184), channel_id=1, source_target_pairs={{0,4},{1,5},{2,6},{3,7},{4,0},{5,1},{6,2},{7,3},{8,12},{9,13},{10,... | collective-permute-start | bytes 1376264 | tf_op jit(solution)/shard_map/ppermute | solution.py:41
  37.8 11.3 %collective-permute-start.7 = (f32[176,128]{1,0:T(8,128)S(1)}, f32[176,128]{1,0:T(8,128)S(1)}, u32[]{:S(2)}, u32[]{:S(2)}) collective-permute-start(f32[176,128]{1,0:T(8,128)S(1)} %pad_maximum_fusion.5), channel_id=1, source_target_pairs={{0,2},{1,3},{2,0},{3,1},{4,6},{5,7},{6,4},{7,5},{8,10},{9,11},{10,... | collective-permute-start | bytes 270344 | tf_op jit(solution)/shard_map/ppermute | solution.py:41
  49.3 9.7 %collective-permute-start.13 = (bf16[2,128,3584]{2,1,0:T(8,128)(2,1)S(1)}, bf16[2,128,3584]{2,1,0:T(8,128)(2,1)S(1)}, u32[]{:S(2)}, u32[]{:S(2)}) collective-permute-start(bf16[2,128,3584]{2,1,0:T(8,128)(2,1)S(1)} %get-tuple-element.196), channel_id=1, source_target_pairs={{0,1},{1,0},{2,3},{3,2},{4,5},{5,4},{6,7},{7,6},{8,9},{9,8},{10,11... | collective-permute-start | bytes 5505032 | tf_op jit(solution)/shard_map/ppermute | solution.py:41
  49.4 9.6 %collective-permute-start.11 = (bf16[32,3584]{1,0:T(8,128)(2,1)S(1)}, bf16[32,3584]{1,0:T(8,128)(2,1)S(1)}, u32[]{:S(2)}, u32[]{:S(2)}) collective-permute-start(bf16[32,3584]{1,0:T(8,128)(2,1)S(1)} %get-tuple-element.194), channel_id=1, source_target_pairs={{0,4},{1,5},{2,6},{3,7},{4,0},{5,1},{6,2},{7,3},{8,12},{9,13},{10,... | collective-permute-start | bytes 688136 | tf_op jit(solution)/shard_map/ppermute | solution.py:41
  51.2 7.8 %collective-permute-start.12 = (bf16[32,3584]{1,0:T(8,128)(2,1)S(1)}, bf16[32,3584]{1,0:T(8,128)(2,1)S(1)}, u32[]{:S(2)}, u32[]{:S(2)}) collective-permute-start(bf16[32,3584]{1,0:T(8,128)(2,1)S(1)} %get-tuple-element.195), channel_id=1, source_target_pairs={{0,2},{1,3},{2,0},{3,1},{4,6},{5,7},{6,4},{7,5},{8,10},{9,11},{10,... | collective-permute-start | bytes 688136 | tf_op jit(solution)/shard_map/ppermute | solution.py:41
  52.7 6.3 %collective-permute-start.10 = (f32[144,128]{1,0:T(8,128)S(1)}, f32[144,128]{1,0:T(8,128)S(1)}, u32[]{:S(2)}, u32[]{:S(2)}) collective-permute-start(f32[144,128]{1,0:T(8,128)S(1)} %pad_maximum_fusion.6), channel_id=1, source_target_pairs={{0,4},{1,5},{2,6},{3,7},{4,0},{5,1},{6,2},{7,3},{8,12},{9,13},{10,... | collective-permute-start | bytes 221192 | tf_op jit(solution)/shard_map/ppermute | solution.py:41
  59.2 12.1 %collective-permute-start.14 = (bf16[64,3584]{1,0:T(8,128)(2,1)S(1)}, bf16[64,3584]{1,0:T(8,128)(2,1)S(1)}, u32[]{:S(2)}, u32[]{:S(2)}) collective-permute-start(bf16[64,3584]{1,0:T(8,128)(2,1)S(1)} %get-tuple-element.201), channel_id=1, source_target_pairs={{0,2},{1,3},{2,0},{3,1},{4,6},{5,7},{6,4},{7,5},{8,10},{9,11},{10,... | collective-permute-start | bytes 1376264 | tf_op jit(solution)/shard_map/ppermute | solution.py:41
  61.0 11.8 %collective-permute-start.15 = (bf16[64,3584]{1,0:T(8,128)(2,1)S(1)}, bf16[64,3584]{1,0:T(8,128)(2,1)S(1)}, u32[]{:S(2)}, u32[]{:S(2)}) collective-permute-start(bf16[64,3584]{1,0:T(8,128)(2,1)S(1)} %get-tuple-element.202), channel_id=1, source_target_pairs={{0,4},{1,5},{2,6},{3,7},{4,0},{5,1},{6,2},{7,3},{8,12},{9,13},{10,... | collective-permute-start | bytes 1376264 | tf_op jit(solution)/shard_map/ppermute | solution.py:41
  73.0 6.1 %collective-permute-start.16 = (bf16[32,3584]{1,0:T(8,128)(2,1)S(1)}, bf16[32,3584]{1,0:T(8,128)(2,1)S(1)}, u32[]{:S(2)}, u32[]{:S(2)}) collective-permute-start(bf16[32,3584]{1,0:T(8,128)(2,1)S(1)} %get-tuple-element.215), channel_id=1, source_target_pairs={{0,4},{1,5},{2,6},{3,7},{4,0},{5,1},{6,2},{7,3},{8,12},{9,13},{10,... | collective-permute-start | bytes 688136 | tf_op jit(solution)/shard_map/ppermute | solution.py:41
  74.6 6.0 %collective-permute-start.17 = (bf16[32,3584]{1,0:T(8,128)(2,1)S(1)}, bf16[32,3584]{1,0:T(8,128)(2,1)S(1)}, u32[]{:S(2)}, u32[]{:S(2)}) collective-permute-start(bf16[32,3584]{1,0:T(8,128)(2,1)S(1)} %get-tuple-element.216), channel_id=1, source_target_pairs={{0,2},{1,3},{2,0},{3,1},{4,6},{5,7},{6,4},{7,5},{8,10},{9,11},{10,... | collective-permute-start | bytes 688136 | tf_op jit(solution)/shard_map/ppermute | solution.py:41
  85.5 5.1 %collective-permute-start.22 = (bf16[176,128]{1,0:T(8,128)(2,1)S(1)}, bf16[176,128]{1,0:T(8,128)(2,1)S(1)}, u32[]{:S(2)}, u32[]{:S(2)}) collective-permute-start(bf16[176,128]{1,0:T(8,128)(2,1)S(1)} %pad_maximum_fusion.9), channel_id=1, source_target_pairs={{0,6},{1,7},{2,4},{3,5},{4,2},{5,3},{6,0},{7,1},{8,14},{9,15},{10,... | collective-permute-start | bytes 135176 | tf_op jit(solution)/shard_map/ppermute | solution.py:41
  85.9 4.8 %collective-permute-start.21 = (bf16[176,128]{1,0:T(8,128)(2,1)S(1)}, bf16[176,128]{1,0:T(8,128)(2,1)S(1)}, u32[]{:S(2)}, u32[]{:S(2)}) collective-permute-start(bf16[176,128]{1,0:T(8,128)(2,1)S(1)} %pad_maximum_fusion.9), channel_id=1, source_target_pairs={{0,4},{1,5},{2,6},{3,7},{4,0},{5,1},{6,2},{7,3},{8,12},{9,13},{10,... | collective-permute-start | bytes 135176 | tf_op jit(solution)/shard_map/ppermute | solution.py:41
  87.6 4.0 %collective-permute-start.20 = (bf16[176,128]{1,0:T(8,128)(2,1)S(1)}, bf16[176,128]{1,0:T(8,128)(2,1)S(1)}, u32[]{:S(2)}, u32[]{:S(2)}) collective-permute-start(bf16[176,128]{1,0:T(8,128)(2,1)S(1)} %pad_maximum_fusion.9), channel_id=1, source_target_pairs={{0,2},{1,3},{2,0},{3,1},{4,6},{5,7},{6,4},{7,5},{8,10},{9,11},{10,... | collective-permute-start | bytes 135176 | tf_op jit(solution)/shard_map/ppermute | solution.py:41
  92.8 17.1 %collective-permute-start.23 = (bf16[16,7168]{1,0:T(8,128)(2,1)S(1)}, bf16[16,7168]{1,0:T(8,128)(2,1)S(1)}, u32[]{:S(2)}, u32[]{:S(2)}) collective-permute-start(bf16[16,7168]{1,0:T(8,128)(2,1)S(1)} %get-tuple-element.254), channel_id=1, source_target_pairs={{0,2},{1,3},{2,0},{3,1},{4,6},{5,7},{6,4},{7,5},{8,10},{9,11},{10,... | collective-permute-start | bytes 688136 | tf_op jit(solution)/shard_map/ppermute | solution.py:41
  94.4 15.6 %collective-permute-start.24 = (bf16[16,7168]{1,0:T(8,128)(2,1)S(1)}, bf16[16,7168]{1,0:T(8,128)(2,1)S(1)}, u32[]{:S(2)}, u32[]{:S(2)}) collective-permute-start(bf16[16,7168]{1,0:T(8,128)(2,1)S(1)} %get-tuple-element.255), channel_id=1, source_target_pairs={{0,4},{1,5},{2,6},{3,7},{4,0},{5,1},{6,2},{7,3},{8,12},{9,13},{10,... | collective-permute-start | bytes 688136 | tf_op jit(solution)/shard_map/ppermute | solution.py:41
  94.9 15.1 %collective-permute-start.25 = (bf16[16,7168]{1,0:T(8,128)(2,1)S(1)}, bf16[16,7168]{1,0:T(8,128)(2,1)S(1)}, u32[]{:S(2)}, u32[]{:S(2)}) collective-permute-start(bf16[16,7168]{1,0:T(8,128)(2,1)S(1)} %get-tuple-element.256), channel_id=1, source_target_pairs={{0,6},{1,7},{2,4},{3,5},{4,2},{5,3},{6,0},{7,1},{8,14},{9,15},{10,... | collective-permute-start | bytes 688136 | tf_op jit(solution)/shard_map/ppermute | solution.py:41
  111.1 12.4 %collective-permute-start.26 = (bf16[8,7168]{1,0:T(8,128)(2,1)S(1)}, bf16[8,7168]{1,0:T(8,128)(2,1)S(1)}, u32[]{:S(2)}, u32[]{:S(2)}) collective-permute-start(bf16[8,7168]{1,0:T(8,128)(2,1)S(1)} %get-tuple-element.273), channel_id=1, source_target_pairs={{0,4},{1,5},{2,6},{3,7},{4,0},{5,1},{6,2},{7,3},{8,12},{9,13},{10,... | collective-permute-start | bytes 344072 | tf_op jit(solution)/shard_map/ppermute | solution.py:41
  111.5 12.0 %collective-permute-start.27 = (bf16[8,7168]{1,0:T(8,128)(2,1)S(1)}, bf16[8,7168]{1,0:T(8,128)(2,1)S(1)}, u32[]{:S(2)}, u32[]{:S(2)}) collective-permute-start(bf16[8,7168]{1,0:T(8,128)(2,1)S(1)} %get-tuple-element.274), channel_id=1, source_target_pairs={{0,2},{1,3},{2,0},{3,1},{4,6},{5,7},{6,4},{7,5},{8,10},{9,11},{10,... | collective-permute-start | bytes 344072 | tf_op jit(solution)/shard_map/ppermute | solution.py:41
  113.1 4.4 %collective-permute-start.28 = (bf16[32,1024]{1,0:T(8,128)(2,1)S(1)}, bf16[32,1024]{1,0:T(8,128)(2,1)S(1)}, u32[]{:S(2)}, u32[]{:S(2)}) collective-permute-start(bf16[32,1024]{1,0:T(8,128)(2,1)S(1)} %get-tuple-element.275), channel_id=1, source_target_pairs={{0,8},{8,0},{16,24},{24,16},{1,9},{9,1},{17,25},{25,17},{2,10},{10... | collective-permute-start | bytes 196616 | tf_op jit(solution)/shard_map/ppermute | solution.py:41
  113.8 6.8 %collective-permute-start.29 = (bf16[32,1024]{1,0:T(8,128)(2,1)S(1)}, bf16[32,1024]{1,0:T(8,128)(2,1)S(1)}, u32[]{:S(2)}, u32[]{:S(2)}) collective-permute-start(bf16[32,1024]{1,0:T(8,128)(2,1)S(1)} %get-tuple-element.276), channel_id=1, source_target_pairs={{0,16},{8,24},{16,0},{24,8},{1,17},{9,25},{17,1},{25,9},{2,18},{10... | collective-permute-start | bytes 196616 | tf_op jit(solution)/shard_map/ppermute | solution.py:41
  117.3 6.2 %collective-permute-start.30 = (bf16[32,1024]{1,0:T(8,128)(2,1)S(1)}, bf16[32,1024]{1,0:T(8,128)(2,1)S(1)}, u32[]{:S(2)}, u32[]{:S(2)}) collective-permute-start(bf16[32,1024]{1,0:T(8,128)(2,1)S(1)} %get-tuple-element.277), channel_id=1, source_target_pairs={{0,24},{8,16},{16,8},{24,0},{1,25},{9,17},{17,9},{25,1},{2,26},{10... | collective-permute-start | bytes 196616 | tf_op jit(solution)/shard_map/ppermute | solution.py:41
  123.6 9.7 %collective-permute-start.31 = (bf16[16,7168]{1,0:T(8,128)(2,1)S(1)}, bf16[16,7168]{1,0:T(8,128)(2,1)S(1)}, u32[]{:S(2)}, u32[]{:S(2)}) collective-permute-start(bf16[16,7168]{1,0:T(8,128)(2,1)S(1)} %pad_maximum_fusion.3), channel_id=1, source_target_pairs={{0,2},{1,3},{2,0},{3,1},{4,6},{5,7},{6,4},{7,5},{8,10},{9,11},{10,... | collective-permute-start | bytes 688136 | tf_op jit(solution)/shard_map/ppermute | solution.py:41
  124.1 9.3 %collective-permute-start.32 = (bf16[16,7168]{1,0:T(8,128)(2,1)S(1)}, bf16[16,7168]{1,0:T(8,128)(2,1)S(1)}, u32[]{:S(2)}, u32[]{:S(2)}) collective-permute-start(bf16[16,7168]{1,0:T(8,128)(2,1)S(1)} %pad_maximum_fusion.4), channel_id=1, source_target_pairs={{0,4},{1,5},{2,6},{3,7},{4,0},{5,1},{6,2},{7,3},{8,12},{9,13},{10,... | collective-permute-start | bytes 688136 | tf_op jit(solution)/shard_map/ppermute | solution.py:41
  126.0 4.4 %collective-permute-start.33 = (bf16[32,1024]{1,0:T(8,128)(2,1)S(1)}, bf16[32,1024]{1,0:T(8,128)(2,1)S(1)}, u32[]{:S(2)}, u32[]{:S(2)}) collective-permute-start(bf16[32,1024]{1,0:T(8,128)(2,1)S(1)} %add_convert_fusion.5.refs_0_), channel_id=1, source_target_pairs={{0,8},{8,0},{16,24},{24,16},{1,9},{9,1},{17,25},{25,17},{2,10},{10... | collective-permute-start | bytes 196616 | tf_op jit(solution)/shard_map/ppermute | solution.py:41
  126.0 5.2 %collective-permute-start.34 = (bf16[32,1024]{1,0:T(8,128)(2,1)S(1)}, bf16[32,1024]{1,0:T(8,128)(2,1)S(1)}, u32[]{:S(2)}, u32[]{:S(2)}) collective-permute-start(bf16[32,1024]{1,0:T(8,128)(2,1)S(1)} %add_convert_fusion.5.refs_0_), channel_id=1, source_target_pairs={{0,16},{8,24},{16,0},{24,8},{1,17},{9,25},{17,1},{25,9},{2,18},{10... | collective-permute-start | bytes 196616 | tf_op jit(solution)/shard_map/ppermute | solution.py:41
  126.8 6.5 %collective-permute-start.35 = (bf16[32,1024]{1,0:T(8,128)(2,1)S(1)}, bf16[32,1024]{1,0:T(8,128)(2,1)S(1)}, u32[]{:S(2)}, u32[]{:S(2)}) collective-permute-start(bf16[32,1024]{1,0:T(8,128)(2,1)S(1)} %add_convert_fusion.5.refs_0_), channel_id=1, source_target_pairs={{0,24},{8,16},{16,8},{24,0},{1,25},{9,17},{17,9},{25,1},{2,26},{10... | collective-permute-start | bytes 196616 | tf_op jit(solution)/shard_map/ppermute | solution.py:41
  (13 other events, 112.1 us)

commit v5 on v4

--- a/solution.py
+++ b/solution.py
@@ -503,7 +503,7 @@
 
 def fold_call(n, orders, ad_keep, ad_got, g_keep, g_got, sq, stat, mag):
     _, half, width = ad_keep.shape
-    tile = tile_of(width, 1792)
+    tile = tile_of(width, 3584)
     rows = half * 4 // n
     big = pl.BlockSpec((2, half, tile), lambda f: (0, 0, f))
     line = pl.BlockSpec((2, 1, tile), lambda f: (0, 0, f))
@@ -785,7 +785,8 @@
     for c in range(1, count):
         outs = phase(turn, [lanes, halvings[c - 1]], project(c))
         halvings.append(Halving(orders, outs[0], outs[1]))
-        phase(turn, [lanes, *halvings])
+        phase(turn, halvings)
+        phase(turn, [lanes, halvings[-1]])
     hidden, results = None, []
     for c in range(count):
         while not (lanes.done() and halvings[c].done()):

time: 139 us -> 139 us (level)
  starting transfers between devices: 40.9 us -> 39 us
  waiting for transfers between devices: 38.3 us -> 39.9 us
    ppermute x37, starting transfers between devices: 40.9 us -> 39 us  [swap(): return lax.ppermute(x, axis, [(i, i ^ bit) for i in range(n)])]
    ppermute x37, waiting for transfers between devices: 38.3 us -> 39.9 us  [swap(): return lax.ppermute(x, axis, [(i, i ^ bit) for i in range(n)])]
  transfers between devices with their start and end apart: 37 -> 37, of which waited for: 15 -> 16; matrix products, arithmetic and copies ran while one was open for 1% -> 1% of each run, Pallas kernels for 35% -> 35%
where the time goes in v5:
time: 139 us; the launch traced here: 138 us
  Pallas kernels  55.7 us (40%)
  waiting for transfers between devices  39.9 us (29%)
  starting transfers between devices  39 us (28%)
  other arithmetic  1.99 us (1%)
    ppermute x37, waiting for transfers between devices, swap(): return lax.ppermute(x, axis, [(i, i ^ bit) for i in range(n)])  39.9 us
    ppermute x37, starting transfers between devices, swap(): return lax.ppermute(x, axis, [(i, i ^ bit) for i in range(n)])  39 us
    pallas_call x2, Pallas kernels, token_call(): pl.pallas_call(functools.partial(token_kernel, n, share, orders, len(xs),...  18 us
    pallas_call x1, Pallas kernels, adapter_call(): pl.pallas_call(functools.partial(adapter_kernel, n, orders, tile, width /...  13.6 us
    pallas_call x1, Pallas kernels, second_call(): pl.pallas_call(functools.partial(second_kernel, tile, size // tile, first...  13.6 us
    pallas_call x2, Pallas kernels, own_call(): pl.pallas_call(functools.partial(own_kernel, n, orders, len(parts), len(x...  4.38 us
    pallas_call x1, Pallas kernels, order_call(): pl.pallas_call(functools.partial(order_kernel, n, orders, prior is not No...  2.83 us
  transfers between devices with their start and end apart: 37, of which 16 were waited for; matrix products, arithmetic and copies ran while one was open for 1% of the time, Pallas kernels for 35%

profile of v5, /device:TPU:0, one launch (start us, length us, event | category | flops | bytes accessed | tf_op | source)
XLA Modules:
  0.0 138.4 jit_solution(246704577694450135)
XLA Ops:
  0.6 4.1 %collective-permute-start.1 = (bf16[64,1024]{1,0:T(8,128)(2,1)}, bf16[64,1024]{1,0:T(8,128)(2,1)S(1)}, u32[]{:S(2)}, u32[]{:S(2)}) collective-permute-start(bf16[64,1024]{1,0:T(8,128)(2,1)} %refs_0_.2), channel_id=1, source_target_pairs={{0,16},{8,24},{16,0},{24,8},{1,17},{9,25},{17,1},{25,9},{2,18},{10... | collective-permute-start | bytes 393224 | tf_op jit(solution)/shard_map/ppermute | solution.py:41
  4.7 1.6 %collective-permute-start = (bf16[64,1024]{1,0:T(8,128)(2,1)}, bf16[64,1024]{1,0:T(8,128)(2,1)S(1)}, u32[]{:S(2)}, u32[]{:S(2)}) collective-permute-start(bf16[64,1024]{1,0:T(8,128)(2,1)} %refs_0_.2), channel_id=1, source_target_pairs={{0,8},{8,0},{16,24},{24,16},{1,9},{9,1},{17,25},{25,17},{2,10},{10... | collective-permute-start | bytes 393224 | tf_op jit(solution)/shard_map/ppermute | solution.py:41
  6.9 13.6 %adapter_pass.1 = (bf16[2,32,7168]{2,1,0:T(8,128)(2,1)}, bf16[2,32,7168]{2,1,0:T(8,128)(2,1)}, f32[2,1,7168]{2,1,0:T(1,128)}) custom-call(s32[2]{0:T(128)} %pad_add_fusion.me_ref.token_ref, bf16[2,64,1024]{2,1,0:T(8,128)(2,1)} %a_ref.3, bf16[2,1024,7168]{2,1,0:T(8,128)(2,1)} %w_ref.3, bf16[2,64,7168]{2,1,0:T(8,128)(2,1)} %b_ref.3), custom_call_target="tpu_custom_call" | custom-call | flops 3758096384 | bytes 29360128 | tf_op jit(solution)/shard_map/adapter_pass/pallas_call | solution.py:173
  21.1 9.2 %token_pass.2 = (bf16[2,128,3584]{2,1,0:T(8,128)(2,1)S(1)}, bf16[2,128,3584]{2,1,0:T(8,128)(2,1)S(1)}, f32[128,128]{1,0:T(8,128)S(1)}, f32[128,128]{1,0:T(8,128)S(1)}) custom-call(s32[2]{0:T(128)S(1)} %copy-done.5, bf16[64,1024]{1,0:T(8,128)(2,1)S(1)} %copy-done.3, bf16[64,1024]{1,0:T(8,128)(2,1)S(1)} %collective-permute-done.refs_1_, ...), custom_call_target="tpu_custom_call" | custom-call | flops 3758096384 | bytes 14680064 | tf_op jit(solution)/shard_map/token_pass/pallas_call | solution.py:262
  30.9 3.4 %collective-permute-done.5.refs_9_ = f32[128,128]{1,0:T(8,128)S(1)} collective-permute-done((f32[128,128]{1,0:T(8,128)S(1)}, f32[128,128]{1,0:T(8,128)S(1)}, u32[]{:S(2)}, u32[]{:S(2)}) %collective-permute-start.5) | collective-permute-done | bytes 65568 | tf_op jit(solution)/shard_map/ppermute | solution.py:41
  34.5 1.8 %collective-permute-start.8 = (bf16[64,3584]{1,0:T(8,128)(2,1)S(1)}, bf16[64,3584]{1,0:T(8,128)(2,1)S(1)}, u32[]{:S(2)}, u32[]{:S(2)}) collective-permute-start(bf16[64,3584]{1,0:T(8,128)(2,1)S(1)} %get-tuple-element.183), channel_id=1, source_target_pairs={{0,2},{1,3},{2,0},{3,1},{4,6},{5,7},{6,4},{7,5},{8,10},{9,11},{10,... | collective-permute-start | bytes 1376264 | tf_op jit(solution)/shard_map/ppermute | solution.py:41
  36.3 1.5 %collective-permute-start.9 = (bf16[64,3584]{1,0:T(8,128)(2,1)S(1)}, bf16[64,3584]{1,0:T(8,128)(2,1)S(1)}, u32[]{:S(2)}, u32[]{:S(2)}) collective-permute-start(bf16[64,3584]{1,0:T(8,128)(2,1)S(1)} %get-tuple-element.184), channel_id=1, source_target_pairs={{0,4},{1,5},{2,6},{3,7},{4,0},{5,1},{6,2},{7,3},{8,12},{9,13},{10,... | collective-permute-start | bytes 1376264 | tf_op jit(solution)/shard_map/ppermute | solution.py:41
  38.4 8.8 %token_pass.3 = (bf16[2,128,3584]{2,1,0:T(8,128)(2,1)S(1)}, bf16[2,128,3584]{2,1,0:T(8,128)(2,1)S(1)}) custom-call(s32[2]{0:T(128)S(1)} %copy-done.5, bf16[64,1024]{1,0:T(8,128)(2,1)S(1)} %copy-done.3, bf16[64,1024]{1,0:T(8,128)(2,1)S(1)} %collective-permute-done.refs_1_, bf16[64,1024]{1,0:T(8,128)(2,1)S(1)} %collective-permute-done.1.refs_2_, ...), custom_call_target="tpu_custom_call" | custom-call | flops 3758096384 | bytes 14680064 | tf_op jit(solution)/shard_map/token_pass/pallas_call | solution.py:262
  47.2 1.9 %collective-permute-done.7 = f32[176,128]{1,0:T(8,128)S(1)} collective-permute-done((f32[176,128]{1,0:T(8,128)S(1)}, f32[176,128]{1,0:T(8,128)S(1)}, u32[]{:S(2)}, u32[]{:S(2)}) %collective-permute-start.7) | collective-permute-done | bytes 90144 | tf_op jit(solution)/shard_map/ppermute | solution.py:41
  49.4 1.8 %collective-permute-start.10 = (bf16[32,3584]{1,0:T(8,128)(2,1)S(1)}, bf16[32,3584]{1,0:T(8,128)(2,1)S(1)}, u32[]{:S(2)}, u32[]{:S(2)}) collective-permute-start(bf16[32,3584]{1,0:T(8,128)(2,1)S(1)} %get-tuple-element.192), channel_id=1, source_target_pairs={{0,4},{1,5},{2,6},{3,7},{4,0},{5,1},{6,2},{7,3},{8,12},{9,13},{10,... | collective-permute-start | bytes 688136 | tf_op jit(solution)/shard_map/ppermute | solution.py:41
  51.2 1.5 %collective-permute-start.11 = (bf16[32,3584]{1,0:T(8,128)(2,1)S(1)}, bf16[32,3584]{1,0:T(8,128)(2,1)S(1)}, u32[]{:S(2)}, u32[]{:S(2)}) collective-permute-start(bf16[32,3584]{1,0:T(8,128)(2,1)S(1)} %get-tuple-element.193), channel_id=1, source_target_pairs={{0,2},{1,3},{2,0},{3,1},{4,6},{5,7},{6,4},{7,5},{8,10},{9,11},{10,... | collective-permute-start | bytes 688136 | tf_op jit(solution)/shard_map/ppermute | solution.py:41
  52.7 4.7 %collective-permute-done.10.refs_6_ = bf16[32,3584]{1,0:T(8,128)(2,1)S(1)} collective-permute-done((bf16[32,3584]{1,0:T(8,128)(2,1)S(1)}, bf16[32,3584]{1,0:T(8,128)(2,1)S(1)}, u32[]{:S(2)}, u32[]{:S(2)}) %collective-permute-start.10) | collective-permute-done | bytes 229408 | tf_op jit(solution)/shard_map/ppermute | solution.py:41
  57.4 1.5 %collective-permute-done.11.refs_7_ = bf16[32,3584]{1,0:T(8,128)(2,1)S(1)} collective-permute-done((bf16[32,3584]{1,0:T(8,128)(2,1)S(1)}, bf16[32,3584]{1,0:T(8,128)(2,1)S(1)}, u32[]{:S(2)}, u32[]{:S(2)}) %collective-permute-start.11) | collective-permute-done | bytes 229408 | tf_op jit(solution)/shard_map/ppermute | solution.py:41
  59.1 1.6 %collective-permute-start.14 = (bf16[64,3584]{1,0:T(8,128)(2,1)S(1)}, bf16[64,3584]{1,0:T(8,128)(2,1)S(1)}, u32[]{:S(2)}, u32[]{:S(2)}) collective-permute-start(bf16[64,3584]{1,0:T(8,128)(2,1)S(1)} %get-tuple-element.201), channel_id=1, source_target_pairs={{0,2},{1,3},{2,0},{3,1},{4,6},{5,7},{6,4},{7,5},{8,10},{9,11},{10,... | collective-permute-start | bytes 1376264 | tf_op jit(solution)/shard_map/ppermute | solution.py:41
  61.1 1.5 %collective-permute-start.13 = (f32[144,128]{1,0:T(8,128)S(1)}, f32[144,128]{1,0:T(8,128)S(1)}, u32[]{:S(2)}, u32[]{:S(2)}) collective-permute-start(f32[144,128]{1,0:T(8,128)S(1)} %pad_maximum_fusion.6), channel_id=1, source_target_pairs={{0,4},{1,5},{2,6},{3,7},{4,0},{5,1},{6,2},{7,3},{8,12},{9,13},{10,... | collective-permute-start | bytes 221192 | tf_op jit(solution)/shard_map/ppermute | solution.py:41
  62.7 11.0 %collective-permute-done.13 = f32[144,128]{1,0:T(8,128)S(1)} collective-permute-done((f32[144,128]{1,0:T(8,128)S(1)}, f32[144,128]{1,0:T(8,128)S(1)}, u32[]{:S(2)}, u32[]{:S(2)}) %collective-permute-start.13) | collective-permute-done | bytes 73760 | tf_op jit(solution)/shard_map/ppermute | solution.py:41
  75.1 2.4 %own_tokens.2 = (bf16[32,7168]{1,0:T(8,128)(2,1)}, bf16[2,32,3584]{2,1,0:T(8,128)(2,1)S(1)}, bf16[2,32,3584]{2,1,0:T(8,128)(2,1)S(1)}, f32[2,1,3584]{2,1,0:T(1,128)S(1)}, f32[32,128]{1,0:T(8,128)S(1)}) custom-call(s32[2]{0:T(128)S(1)} %copy-done.5, bf16[2,128,3584]{2,1,0:T(8,128)(2,1)S(1)} %get-tuple-element.179.refs_0_.refs_1_, ...), custom_call_target="tpu_custom_call" | custom-call | flops 58720256 | bytes 2293760 | tf_op jit(solution)/shard_map/own_tokens/pallas_call | solution.py:362
  77.5 2.5 %collective-permute-done.16.refs_6_ = bf16[32,3584]{1,0:T(8,128)(2,1)S(1)} collective-permute-done((bf16[32,3584]{1,0:T(8,128)(2,1)S(1)}, bf16[32,3584]{1,0:T(8,128)(2,1)S(1)}, u32[]{:S(2)}, u32[]{:S(2)}) %collective-permute-start.16) | collective-permute-done | bytes 229408 | tf_op jit(solution)/shard_map/ppermute | solution.py:41
  80.6 2.0 %own_tokens.3 = (bf16[32,7168]{1,0:T(8,128)(2,1)}, bf16[2,32,3584]{2,1,0:T(8,128)(2,1)S(1)}, bf16[2,32,3584]{2,1,0:T(8,128)(2,1)S(1)}, f32[2,1,3584]{2,1,0:T(1,128)S(1)}, f32[32,128]{1,0:T(8,128)S(1)}) custom-call(s32[2]{0:T(128)S(1)} %copy-done.5, bf16[2,128,3584]{2,1,0:T(8,128)(2,1)S(1)} %get-tuple-element.197.refs_0_.refs_1_, ...), custom_call_target="tpu_custom_call", output_to_operand_aliasing={{0}: (17, {})} | custom-call | flops 58720256 | bytes 2293760 | tf_op jit(solution)/shard_map/own_tokens/pallas_call | solution.py:362
  83.4 2.1 %collective-permute-done.18 = f32[144,128]{1,0:T(8,128)S(1)} collective-permute-done((f32[144,128]{1,0:T(8,128)S(1)}, f32[144,128]{1,0:T(8,128)S(1)}, u32[]{:S(2)}, u32[]{:S(2)}) %collective-permute-start.18) | collective-permute-done | bytes 73760 | tf_op jit(solution)/shard_map/ppermute | solution.py:41
  87.5 1.5 %collective-permute-start.20 = (bf16[176,128]{1,0:T(8,128)(2,1)S(1)}, bf16[176,128]{1,0:T(8,128)(2,1)S(1)}, u32[]{:S(2)}, u32[]{:S(2)}) collective-permute-start(bf16[176,128]{1,0:T(8,128)(2,1)S(1)} %pad_maximum_fusion.9), channel_id=1, source_target_pairs={{0,2},{1,3},{2,0},{3,1},{4,6},{5,7},{6,4},{7,5},{8,10},{9,11},{10,... | collective-permute-start | bytes 135176 | tf_op jit(solution)/shard_map/ppermute | solution.py:41
  89.0 1.5 %collective-permute-done.22 = bf16[176,128]{1,0:T(8,128)(2,1)S(1)} collective-permute-done((bf16[176,128]{1,0:T(8,128)(2,1)S(1)}, bf16[176,128]{1,0:T(8,128)(2,1)S(1)}, u32[]{:S(2)}, u32[]{:S(2)}) %collective-permute-start.22) | collective-permute-done | bytes 45088 | tf_op jit(solution)/shard_map/ppermute | solution.py:41
  92.7 1.6 %collective-permute-start.23 = (bf16[16,7168]{1,0:T(8,128)(2,1)S(1)}, bf16[16,7168]{1,0:T(8,128)(2,1)S(1)}, u32[]{:S(2)}, u32[]{:S(2)}) collective-permute-start(bf16[16,7168]{1,0:T(8,128)(2,1)S(1)} %get-tuple-element.254), channel_id=1, source_target_pairs={{0,2},{1,3},{2,0},{3,1},{4,6},{5,7},{6,4},{7,5},{8,10},{9,11},{10,... | collective-permute-start | bytes 688136 | tf_op jit(solution)/shard_map/ppermute | solution.py:41
  96.3 13.6 %second_pass.1.refs_4_ = f32[2,64,1024]{2,1,0:T(8,128)S(1)} custom-call(s32[2]{0:T(128)S(1)} %copy-done.5, bf16[2,1024,7168]{2,1,0:T(8,128)(2,1)} %w_ref.3, bf16[2,64,7168]{2,1,0:T(8,128)(2,1)S(1)} %copy-done, bf16[2,64,1024]{2,1,0:T(8,128)(2,1)S(1)} %copy-done.1, f32[2,1,7168]{2,1,0:T(1,128)S(1)} %get-tuple-element.257.cd_ref), custom_call_target="tpu_custom_call" | custom-call | flops 1879048192 | bytes 29360128 | tf_op jit(solution)/shard_map/second_pass/pallas_call | solution.py:412
  110.9 1.5 %collective-permute-start.26 = (bf16[8,7168]{1,0:T(8,128)(2,1)S(1)}, bf16[8,7168]{1,0:T(8,128)(2,1)S(1)}, u32[]{:S(2)}, u32[]{:S(2)}) collective-permute-start(bf16[8,7168]{1,0:T(8,128)(2,1)S(1)} %get-tuple-element.273), channel_id=1, source_target_pairs={{0,4},{1,5},{2,6},{3,7},{4,0},{5,1},{6,2},{7,3},{8,12},{9,13},{10,... | collective-permute-start | bytes 344072 | tf_op jit(solution)/shard_map/ppermute | solution.py:41
  112.4 1.5 %collective-permute-start.27 = (bf16[8,7168]{1,0:T(8,128)(2,1)S(1)}, bf16[8,7168]{1,0:T(8,128)(2,1)S(1)}, u32[]{:S(2)}, u32[]{:S(2)}) collective-permute-start(bf16[8,7168]{1,0:T(8,128)(2,1)S(1)} %get-tuple-element.274), channel_id=1, source_target_pairs={{0,2},{1,3},{2,0},{3,1},{4,6},{5,7},{6,4},{7,5},{8,10},{9,11},{10,... | collective-permute-start | bytes 344072 | tf_op jit(solution)/shard_map/ppermute | solution.py:41
  114.6 3.5 %collective-permute-start.29 = (bf16[32,1024]{1,0:T(8,128)(2,1)S(1)}, bf16[32,1024]{1,0:T(8,128)(2,1)S(1)}, u32[]{:S(2)}, u32[]{:S(2)}) collective-permute-start(bf16[32,1024]{1,0:T(8,128)(2,1)S(1)} %get-tuple-element.276), channel_id=1, source_target_pairs={{0,16},{8,24},{16,0},{24,8},{1,17},{9,25},{17,1},{25,9},{2,18},{10... | collective-permute-start | bytes 196616 | tf_op jit(solution)/shard_map/ppermute | solution.py:41
  118.3 3.2 %collective-permute-done.29 = bf16[32,1024]{1,0:T(8,128)(2,1)S(1)} collective-permute-done((bf16[32,1024]{1,0:T(8,128)(2,1)S(1)}, bf16[32,1024]{1,0:T(8,128)(2,1)S(1)}, u32[]{:S(2)}, u32[]{:S(2)}) %collective-permute-start.29) | collective-permute-done | bytes 65568 | tf_op jit(solution)/shard_map/ppermute | solution.py:41
  121.5 3.2 %collective-permute-done.30 = bf16[32,1024]{1,0:T(8,128)(2,1)S(1)} collective-permute-done((bf16[32,1024]{1,0:T(8,128)(2,1)S(1)}, bf16[32,1024]{1,0:T(8,128)(2,1)S(1)}, u32[]{:S(2)}, u32[]{:S(2)}) %collective-permute-start.30) | collective-permute-done | bytes 65568 | tf_op jit(solution)/shard_map/ppermute | solution.py:41
  126.8 3.0 %collective-permute-start.35 = (bf16[32,1024]{1,0:T(8,128)(2,1)S(1)}, bf16[32,1024]{1,0:T(8,128)(2,1)S(1)}, u32[]{:S(2)}, u32[]{:S(2)}) collective-permute-start(bf16[32,1024]{1,0:T(8,128)(2,1)S(1)} %add_convert_fusion.5.refs_0_), channel_id=1, source_target_pairs={{0,24},{8,16},{16,8},{24,0},{1,25},{9,17},{17,9},{25,1},{2,26},{10... | collective-permute-start | bytes 196616 | tf_op jit(solution)/shard_map/ppermute | solution.py:41
  130.6 2.2 %collective-permute-done.35.refs_3_ = bf16[32,1024]{1,0:T(8,128)(2,1)S(1)} collective-permute-done((bf16[32,1024]{1,0:T(8,128)(2,1)S(1)}, bf16[32,1024]{1,0:T(8,128)(2,1)S(1)}, u32[]{:S(2)}, u32[]{:S(2)}) %collective-permute-start.35) | collective-permute-done | bytes 65568 | tf_op jit(solution)/shard_map/ppermute | solution.py:41
  135.5 2.8 %order_rows.1 = f32[2,64,7168]{2,1,0:T(8,128)} custom-call(s32[2]{0:T(128)S(1)} %copy-done.5, bf16[2,32,7168]{2,1,0:T(8,128)(2,1)S(1)} %pad_maximum_fusion.2.low_ref, bf16[2,32,7168]{2,1,0:T(8,128)(2,1)S(1)} %collective-permute-done.36.high_ref), custom_call_target="tpu_custom_call" | custom-call | tf_op jit(solution)/shard_map/order_rows/pallas_call | solution.py:546
  (105 shorter events, 20.1 us)
Async XLA Ops:
  0.6 19.8 %collective-permute-start.1 = (bf16[64,1024]{1,0:T(8,128)(2,1)}, bf16[64,1024]{1,0:T(8,128)(2,1)S(1)}, u32[]{:S(2)}, u32[]{:S(2)}) collective-permute-start(bf16[64,1024]{1,0:T(8,128)(2,1)} %refs_0_.2), channel_id=1, source_target_pairs={{0,16},{8,24},{16,0},{24,8},{1,17},{9,25},{17,1},{25,9},{2,18},{10... | collective-permute-start | bytes 393224 | tf_op jit(solution)/shard_map/ppermute | solution.py:41
  4.7 15.7 %collective-permute-start = (bf16[64,1024]{1,0:T(8,128)(2,1)}, bf16[64,1024]{1,0:T(8,128)(2,1)S(1)}, u32[]{:S(2)}, u32[]{:S(2)}) collective-permute-start(bf16[64,1024]{1,0:T(8,128)(2,1)} %refs_0_.2), channel_id=1, source_target_pairs={{0,8},{8,0},{16,24},{24,16},{1,9},{9,1},{17,25},{25,17},{2,10},{10... | collective-permute-start | bytes 393224 | tf_op jit(solution)/shard_map/ppermute | solution.py:41
  6.3 14.2 %collective-permute-start.2 = (bf16[64,1024]{1,0:T(8,128)(2,1)}, bf16[64,1024]{1,0:T(8,128)(2,1)S(1)}, u32[]{:S(2)}, u32[]{:S(2)}) collective-permute-start(bf16[64,1024]{1,0:T(8,128)(2,1)} %refs_0_.2), channel_id=1, source_target_pairs={{0,24},{8,16},{16,8},{24,0},{1,25},{9,17},{17,9},{25,1},{2,26},{10... | collective-permute-start | bytes 393224 | tf_op jit(solution)/shard_map/ppermute | solution.py:41
  20.5 9.8 %collective-permute-start.4 = (bf16[2,32,7168]{2,1,0:T(8,128)(2,1)}, bf16[2,32,7168]{2,1,0:T(8,128)(2,1)S(1)}, u32[]{:S(2)}, u32[]{:S(2)}) collective-permute-start(bf16[2,32,7168]{2,1,0:T(8,128)(2,1)} %get-tuple-element.160), channel_id=1, source_target_pairs={{0,1},{1,0},{2,3},{3,2},{4,5},{5,4},{6,7},{7,6},{8,9},{9,8},{10,11... | collective-permute-start | bytes 2752520 | tf_op jit(solution)/shard_map/ppermute | solution.py:41
  20.6 9.7 %collective-permute-start.3 = (f32[112,128]{1,0:T(8,128)}, f32[112,128]{1,0:T(8,128)S(1)}, u32[]{:S(2)}, u32[]{:S(2)}) collective-permute-start(f32[112,128]{1,0:T(8,128)} %bitcast.43), channel_id=1, source_target_pairs={{0,1},{1,0},{2,3},{3,2},{4,5},{5,4},{6,7},{7,6},{8,9},{9,8},{10,11... | collective-permute-start | bytes 172040 | tf_op jit(solution)/shard_map/ppermute | solution.py:41
  34.5 14.6 %collective-permute-start.8 = (bf16[64,3584]{1,0:T(8,128)(2,1)S(1)}, bf16[64,3584]{1,0:T(8,128)(2,1)S(1)}, u32[]{:S(2)}, u32[]{:S(2)}) collective-permute-start(bf16[64,3584]{1,0:T(8,128)(2,1)S(1)} %get-tuple-element.183), channel_id=1, source_target_pairs={{0,2},{1,3},{2,0},{3,1},{4,6},{5,7},{6,4},{7,5},{8,10},{9,11},{10,... | collective-permute-start | bytes 1376264 | tf_op jit(solution)/shard_map/ppermute | solution.py:41
  36.3 12.8 %collective-permute-start.9 = (bf16[64,3584]{1,0:T(8,128)(2,1)S(1)}, bf16[64,3584]{1,0:T(8,128)(2,1)S(1)}, u32[]{:S(2)}, u32[]{:S(2)}) collective-permute-start(bf16[64,3584]{1,0:T(8,128)(2,1)S(1)} %get-tuple-element.184), channel_id=1, source_target_pairs={{0,4},{1,5},{2,6},{3,7},{4,0},{5,1},{6,2},{7,3},{8,12},{9,13},{10,... | collective-permute-start | bytes 1376264 | tf_op jit(solution)/shard_map/ppermute | solution.py:41
  37.8 11.3 %collective-permute-start.7 = (f32[176,128]{1,0:T(8,128)S(1)}, f32[176,128]{1,0:T(8,128)S(1)}, u32[]{:S(2)}, u32[]{:S(2)}) collective-permute-start(f32[176,128]{1,0:T(8,128)S(1)} %pad_maximum_fusion.5), channel_id=1, source_target_pairs={{0,2},{1,3},{2,0},{3,1},{4,6},{5,7},{6,4},{7,5},{8,10},{9,11},{10,... | collective-permute-start | bytes 270344 | tf_op jit(solution)/shard_map/ppermute | solution.py:41
  49.3 9.6 %collective-permute-start.12 = (bf16[2,128,3584]{2,1,0:T(8,128)(2,1)S(1)}, bf16[2,128,3584]{2,1,0:T(8,128)(2,1)S(1)}, u32[]{:S(2)}, u32[]{:S(2)}) collective-permute-start(bf16[2,128,3584]{2,1,0:T(8,128)(2,1)S(1)} %get-tuple-element.194), channel_id=1, source_target_pairs={{0,1},{1,0},{2,3},{3,2},{4,5},{5,4},{6,7},{7,6},{8,9},{9,8},{10,11... | collective-permute-start | bytes 5505032 | tf_op jit(solution)/shard_map/ppermute | solution.py:41
  49.4 8.0 %collective-permute-start.10 = (bf16[32,3584]{1,0:T(8,128)(2,1)S(1)}, bf16[32,3584]{1,0:T(8,128)(2,1)S(1)}, u32[]{:S(2)}, u32[]{:S(2)}) collective-permute-start(bf16[32,3584]{1,0:T(8,128)(2,1)S(1)} %get-tuple-element.192), channel_id=1, source_target_pairs={{0,4},{1,5},{2,6},{3,7},{4,0},{5,1},{6,2},{7,3},{8,12},{9,13},{10,... | collective-permute-start | bytes 688136 | tf_op jit(solution)/shard_map/ppermute | solution.py:41
  51.2 7.7 %collective-permute-start.11 = (bf16[32,3584]{1,0:T(8,128)(2,1)S(1)}, bf16[32,3584]{1,0:T(8,128)(2,1)S(1)}, u32[]{:S(2)}, u32[]{:S(2)}) collective-permute-start(bf16[32,3584]{1,0:T(8,128)(2,1)S(1)} %get-tuple-element.193), channel_id=1, source_target_pairs={{0,2},{1,3},{2,0},{3,1},{4,6},{5,7},{6,4},{7,5},{8,10},{9,11},{10,... | collective-permute-start | bytes 688136 | tf_op jit(solution)/shard_map/ppermute | solution.py:41
  59.1 14.6 %collective-permute-start.14 = (bf16[64,3584]{1,0:T(8,128)(2,1)S(1)}, bf16[64,3584]{1,0:T(8,128)(2,1)S(1)}, u32[]{:S(2)}, u32[]{:S(2)}) collective-permute-start(bf16[64,3584]{1,0:T(8,128)(2,1)S(1)} %get-tuple-element.201), channel_id=1, source_target_pairs={{0,2},{1,3},{2,0},{3,1},{4,6},{5,7},{6,4},{7,5},{8,10},{9,11},{10,... | collective-permute-start | bytes 1376264 | tf_op jit(solution)/shard_map/ppermute | solution.py:41
  60.6 13.1 %collective-permute-start.15 = (bf16[64,3584]{1,0:T(8,128)(2,1)S(1)}, bf16[64,3584]{1,0:T(8,128)(2,1)S(1)}, u32[]{:S(2)}, u32[]{:S(2)}) collective-permute-start(bf16[64,3584]{1,0:T(8,128)(2,1)S(1)} %get-tuple-element.202), channel_id=1, source_target_pairs={{0,4},{1,5},{2,6},{3,7},{4,0},{5,1},{6,2},{7,3},{8,12},{9,13},{10,... | collective-permute-start | bytes 1376264 | tf_op jit(solution)/shard_map/ppermute | solution.py:41
  61.1 12.5 %collective-permute-start.13 = (f32[144,128]{1,0:T(8,128)S(1)}, f32[144,128]{1,0:T(8,128)S(1)}, u32[]{:S(2)}, u32[]{:S(2)}) collective-permute-start(f32[144,128]{1,0:T(8,128)S(1)} %pad_maximum_fusion.6), channel_id=1, source_target_pairs={{0,4},{1,5},{2,6},{3,7},{4,0},{5,1},{6,2},{7,3},{8,12},{9,13},{10,... | collective-permute-start | bytes 221192 | tf_op jit(solution)/shard_map/ppermute | solution.py:41
  73.9 6.1 %collective-permute-start.16 = (bf16[32,3584]{1,0:T(8,128)(2,1)S(1)}, bf16[32,3584]{1,0:T(8,128)(2,1)S(1)}, u32[]{:S(2)}, u32[]{:S(2)}) collective-permute-start(bf16[32,3584]{1,0:T(8,128)(2,1)S(1)} %get-tuple-element.207), channel_id=1, source_target_pairs={{0,4},{1,5},{2,6},{3,7},{4,0},{5,1},{6,2},{7,3},{8,12},{9,13},{10,... | collective-permute-start | bytes 688136 | tf_op jit(solution)/shard_map/ppermute | solution.py:41
  74.5 6.0 %collective-permute-start.17 = (bf16[32,3584]{1,0:T(8,128)(2,1)S(1)}, bf16[32,3584]{1,0:T(8,128)(2,1)S(1)}, u32[]{:S(2)}, u32[]{:S(2)}) collective-permute-start(bf16[32,3584]{1,0:T(8,128)(2,1)S(1)} %get-tuple-element.208), channel_id=1, source_target_pairs={{0,2},{1,3},{2,0},{3,1},{4,6},{5,7},{6,4},{7,5},{8,10},{9,11},{10,... | collective-permute-start | bytes 688136 | tf_op jit(solution)/shard_map/ppermute | solution.py:41
  85.5 5.1 %collective-permute-start.22 = (bf16[176,128]{1,0:T(8,128)(2,1)S(1)}, bf16[176,128]{1,0:T(8,128)(2,1)S(1)}, u32[]{:S(2)}, u32[]{:S(2)}) collective-permute-start(bf16[176,128]{1,0:T(8,128)(2,1)S(1)} %pad_maximum_fusion.9), channel_id=1, source_target_pairs={{0,6},{1,7},{2,4},{3,5},{4,2},{5,3},{6,0},{7,1},{8,14},{9,15},{10,... | collective-permute-start | bytes 135176 | tf_op jit(solution)/shard_map/ppermute | solution.py:41
  86.9 4.2 %collective-permute-start.21 = (bf16[176,128]{1,0:T(8,128)(2,1)S(1)}, bf16[176,128]{1,0:T(8,128)(2,1)S(1)}, u32[]{:S(2)}, u32[]{:S(2)}) collective-permute-start(bf16[176,128]{1,0:T(8,128)(2,1)S(1)} %pad_maximum_fusion.9), channel_id=1, source_target_pairs={{0,4},{1,5},{2,6},{3,7},{4,0},{5,1},{6,2},{7,3},{8,12},{9,13},{10,... | collective-permute-start | bytes 135176 | tf_op jit(solution)/shard_map/ppermute | solution.py:41
  87.5 4.0 %collective-permute-start.20 = (bf16[176,128]{1,0:T(8,128)(2,1)S(1)}, bf16[176,128]{1,0:T(8,128)(2,1)S(1)}, u32[]{:S(2)}, u32[]{:S(2)}) collective-permute-start(bf16[176,128]{1,0:T(8,128)(2,1)S(1)} %pad_maximum_fusion.9), channel_id=1, source_target_pairs={{0,2},{1,3},{2,0},{3,1},{4,6},{5,7},{6,4},{7,5},{8,10},{9,11},{10,... | collective-permute-start | bytes 135176 | tf_op jit(solution)/shard_map/ppermute | solution.py:41
  92.7 17.1 %collective-permute-start.23 = (bf16[16,7168]{1,0:T(8,128)(2,1)S(1)}, bf16[16,7168]{1,0:T(8,128)(2,1)S(1)}, u32[]{:S(2)}, u32[]{:S(2)}) collective-permute-start(bf16[16,7168]{1,0:T(8,128)(2,1)S(1)} %get-tuple-element.254), channel_id=1, source_target_pairs={{0,2},{1,3},{2,0},{3,1},{4,6},{5,7},{6,4},{7,5},{8,10},{9,11},{10,... | collective-permute-start | bytes 688136 | tf_op jit(solution)/shard_map/ppermute | solution.py:41
  94.3 15.6 %collective-permute-start.24 = (bf16[16,7168]{1,0:T(8,128)(2,1)S(1)}, bf16[16,7168]{1,0:T(8,128)(2,1)S(1)}, u32[]{:S(2)}, u32[]{:S(2)}) collective-permute-start(bf16[16,7168]{1,0:T(8,128)(2,1)S(1)} %get-tuple-element.255), channel_id=1, source_target_pairs={{0,4},{1,5},{2,6},{3,7},{4,0},{5,1},{6,2},{7,3},{8,12},{9,13},{10,... | collective-permute-start | bytes 688136 | tf_op jit(solution)/shard_map/ppermute | solution.py:41
  95.7 14.2 %collective-permute-start.25 = (bf16[16,7168]{1,0:T(8,128)(2,1)S(1)}, bf16[16,7168]{1,0:T(8,128)(2,1)S(1)}, u32[]{:S(2)}, u32[]{:S(2)}) collective-permute-start(bf16[16,7168]{1,0:T(8,128)(2,1)S(1)} %get-tuple-element.256), channel_id=1, source_target_pairs={{0,6},{1,7},{2,4},{3,5},{4,2},{5,3},{6,0},{7,1},{8,14},{9,15},{10,... | collective-permute-start | bytes 688136 | tf_op jit(solution)/shard_map/ppermute | solution.py:41
  110.9 13.8 %collective-permute-start.26 = (bf16[8,7168]{1,0:T(8,128)(2,1)S(1)}, bf16[8,7168]{1,0:T(8,128)(2,1)S(1)}, u32[]{:S(2)}, u32[]{:S(2)}) collective-permute-start(bf16[8,7168]{1,0:T(8,128)(2,1)S(1)} %get-tuple-element.273), channel_id=1, source_target_pairs={{0,4},{1,5},{2,6},{3,7},{4,0},{5,1},{6,2},{7,3},{8,12},{9,13},{10,... | collective-permute-start | bytes 344072 | tf_op jit(solution)/shard_map/ppermute | solution.py:41
  112.4 12.3 %collective-permute-start.27 = (bf16[8,7168]{1,0:T(8,128)(2,1)S(1)}, bf16[8,7168]{1,0:T(8,128)(2,1)S(1)}, u32[]{:S(2)}, u32[]{:S(2)}) collective-permute-start(bf16[8,7168]{1,0:T(8,128)(2,1)S(1)} %get-tuple-element.274), channel_id=1, source_target_pairs={{0,2},{1,3},{2,0},{3,1},{4,6},{5,7},{6,4},{7,5},{8,10},{9,11},{10,... | collective-permute-start | bytes 344072 | tf_op jit(solution)/shard_map/ppermute | solution.py:41
  113.9 4.4 %collective-permute-start.28 = (bf16[32,1024]{1,0:T(8,128)(2,1)S(1)}, bf16[32,1024]{1,0:T(8,128)(2,1)S(1)}, u32[]{:S(2)}, u32[]{:S(2)}) collective-permute-start(bf16[32,1024]{1,0:T(8,128)(2,1)S(1)} %get-tuple-element.275), channel_id=1, source_target_pairs={{0,8},{8,0},{16,24},{24,16},{1,9},{9,1},{17,25},{25,17},{2,10},{10... | collective-permute-start | bytes 196616 | tf_op jit(solution)/shard_map/ppermute | solution.py:41
  114.6 6.9 %collective-permute-start.29 = (bf16[32,1024]{1,0:T(8,128)(2,1)S(1)}, bf16[32,1024]{1,0:T(8,128)(2,1)S(1)}, u32[]{:S(2)}, u32[]{:S(2)}) collective-permute-start(bf16[32,1024]{1,0:T(8,128)(2,1)S(1)} %get-tuple-element.276), channel_id=1, source_target_pairs={{0,16},{8,24},{16,0},{24,8},{1,17},{9,25},{17,1},{25,9},{2,18},{10... | collective-permute-start | bytes 196616 | tf_op jit(solution)/shard_map/ppermute | solution.py:41
  118.1 6.6 %collective-permute-start.30 = (bf16[32,1024]{1,0:T(8,128)(2,1)S(1)}, bf16[32,1024]{1,0:T(8,128)(2,1)S(1)}, u32[]{:S(2)}, u32[]{:S(2)}) collective-permute-start(bf16[32,1024]{1,0:T(8,128)(2,1)S(1)} %get-tuple-element.277), channel_id=1, source_target_pairs={{0,24},{8,16},{16,8},{24,0},{1,25},{9,17},{17,9},{25,1},{2,26},{10... | collective-permute-start | bytes 196616 | tf_op jit(solution)/shard_map/ppermute | solution.py:41
  124.8 8.1 %collective-permute-start.31 = (bf16[16,7168]{1,0:T(8,128)(2,1)S(1)}, bf16[16,7168]{1,0:T(8,128)(2,1)S(1)}, u32[]{:S(2)}, u32[]{:S(2)}) collective-permute-start(bf16[16,7168]{1,0:T(8,128)(2,1)S(1)} %pad_maximum_fusion.3), channel_id=1, source_target_pairs={{0,2},{1,3},{2,0},{3,1},{4,6},{5,7},{6,4},{7,5},{8,10},{9,11},{10,... | collective-permute-start | bytes 688136 | tf_op jit(solution)/shard_map/ppermute | solution.py:41
  125.2 7.6 %collective-permute-start.32 = (bf16[16,7168]{1,0:T(8,128)(2,1)S(1)}, bf16[16,7168]{1,0:T(8,128)(2,1)S(1)}, u32[]{:S(2)}, u32[]{:S(2)}) collective-permute-start(bf16[16,7168]{1,0:T(8,128)(2,1)S(1)} %pad_maximum_fusion.4), channel_id=1, source_target_pairs={{0,4},{1,5},{2,6},{3,7},{4,0},{5,1},{6,2},{7,3},{8,12},{9,13},{10,... | collective-permute-start | bytes 688136 | tf_op jit(solution)/shard_map/ppermute | solution.py:41
  125.4 4.4 %collective-permute-start.33 = (bf16[32,1024]{1,0:T(8,128)(2,1)S(1)}, bf16[32,1024]{1,0:T(8,128)(2,1)S(1)}, u32[]{:S(2)}, u32[]{:S(2)}) collective-permute-start(bf16[32,1024]{1,0:T(8,128)(2,1)S(1)} %add_convert_fusion.5.refs_0_), channel_id=1, source_target_pairs={{0,8},{8,0},{16,24},{24,16},{1,9},{9,1},{17,25},{25,17},{2,10},{10... | collective-permute-start | bytes 196616 | tf_op jit(solution)/shard_map/ppermute | solution.py:41
  125.4 5.2 %collective-permute-start.34 = (bf16[32,1024]{1,0:T(8,128)(2,1)S(1)}, bf16[32,1024]{1,0:T(8,128)(2,1)S(1)}, u32[]{:S(2)}, u32[]{:S(2)}) collective-permute-start(bf16[32,1024]{1,0:T(8,128)(2,1)S(1)} %add_convert_fusion.5.refs_0_), channel_id=1, source_target_pairs={{0,16},{8,24},{16,0},{24,8},{1,17},{9,25},{17,1},{25,9},{2,18},{10... | collective-permute-start | bytes 196616 | tf_op jit(solution)/shard_map/ppermute | solution.py:41
  126.8 6.1 %collective-permute-start.35 = (bf16[32,1024]{1,0:T(8,128)(2,1)S(1)}, bf16[32,1024]{1,0:T(8,128)(2,1)S(1)}, u32[]{:S(2)}, u32[]{:S(2)}) collective-permute-start(bf16[32,1024]{1,0:T(8,128)(2,1)S(1)} %add_convert_fusion.5.refs_0_), channel_id=1, source_target_pairs={{0,24},{8,16},{16,8},{24,0},{1,25},{9,17},{17,9},{25,1},{2,26},{10... | collective-permute-start | bytes 196616 | tf_op jit(solution)/shard_map/ppermute | solution.py:41
  (13 other events, 121.3 us)
